TPU v7x, 256 devices: a whole 4x4x8 slice. The times are simulated.
256 devices in a mesh: band: 4 (over z_lo), col: 64 (over z_hi, y, x, core).
Axes of the slice: x: 4, y: 4, z: 8 (z_hi: 2, z_lo: 4; z = z_hi * 4 + z_lo), core: 2. Of those that a mesh axis runs over, the one named last changes fastest.
Arguments:
- fields: bfloat16 [4, 80, 32, 8192], P(None, None, 'band', 'col'), may hold values from -6 to 6
- inverse: bfloat16 [4, 80, 80], replicated, may hold values from -1 to 2
- block_costs: int32 [64, 32], P('col', 'band'), may hold values from 1 to 8, as said below
- row_length: int32 [32], P('band'), may hold values from 4097 to 8192
Outputs:
- spectra: float32 [320, 32, 2, 2048], P('col', None, None, 'band')
Inputs may be any that keep to these rules, and one draw needn't show every extreme that they name: `block_costs`: at least one block takes 8 substeps and at least one takes 1.
All inputs are finite; a program needn't handle non-finite values.
Results may differ from a plain program's by a relative error of at most 0.0042.
Values may be sent and summed in bfloat16 or wider, within the bound.
No kernel may reach another device: no remote copies, remote signals or barrier semaphores. Data moves between devices by JAX's collectives and lax.ppermute only.
A program may use at most 64 MiB of HBM per device.

v0:
```python
import math

import jax
import jax.numpy as jnp
from jax import lax
from jax.sharding import PartitionSpec as P

group_width = 4


def relax(blocks, counts, inverse):
    group_total = blocks.shape[2] // group_width

    def one_group(group_index, result):
        offset_start = group_index * group_width
        block_set = lax.dynamic_slice_in_dim(blocks, offset_start, group_width, 2)
        steps_here = lax.dynamic_slice_in_dim(counts, offset_start, group_width, 0)

        def sweep(sweep_index, block_state):
            applied = jnp.einsum(
                "fkl,flgb->fkgb", inverse, block_state, preferred_element_type=jnp.float32
            ).astype(jnp.bfloat16)
            return jnp.where((sweep_index < steps_here)[None, None, :, None], applied, block_state)

        block_set = lax.fori_loop(jnp.int32(0), jnp.max(steps_here), sweep, block_set)
        return lax.dynamic_update_slice_in_dim(result, block_set, offset_start, 2)

    return lax.fori_loop(0, group_total, one_group, blocks)


def tendency_of(relaxed, initial):
    return (relaxed.astype(jnp.float32) - initial.astype(jnp.float32)).astype(jnp.bfloat16)


def apply_tendency(initial, tendency):
    tendency = lax.optimization_barrier(tendency)
    return (initial.astype(jnp.float32) + tendency.astype(jnp.float32)).astype(jnp.bfloat16)


def mask_rows(values_in, lengths, first_longitude):
    block_width = values_in.shape[3]
    longitude = first_longitude + jnp.arange(block_width, dtype=jnp.int32)
    keep_mask = longitude[None, :] < lengths[:, None]
    return jnp.where(keep_mask[None, None], values_in, jnp.zeros_like(values_in))


def transform(row_piece, wave_first, wave_total):
    group_count = lax.axis_size("col")
    length_all = row_piece.shape[-1]
    block_width = length_all // group_count
    level_count = row_piece.shape[0]
    piece_rows = row_piece.shape[1]
    values_f32 = row_piece.astype(jnp.float32).reshape(
        level_count, piece_rows, group_count, block_width
    )
    group_ids = jnp.arange(group_count, dtype=jnp.int32)
    angle_one = (group_ids[:, None] * group_ids[None, :] % group_count).astype(jnp.float32) * (
        2.0 * math.pi / group_count
    )
    table_one = jnp.stack([jnp.cos(angle_one), -jnp.sin(angle_one)], axis=0)
    section_one = jnp.einsum(
        "icm,prcb->iprmb", table_one, values_f32, precision=lax.Precision.HIGHEST
    )
    lane_ids = jnp.arange(block_width, dtype=jnp.int32)
    angle_twist = (group_ids[:, None] * lane_ids[None, :] % length_all).astype(jnp.float32) * (
        2.0 * math.pi / length_all
    )
    cos_twist = jnp.cos(angle_twist)
    sin_twist = jnp.sin(angle_twist)
    real_part = section_one[0] * cos_twist + section_one[1] * sin_twist
    imaginary = section_one[1] * cos_twist - section_one[0] * sin_twist
    twisted = jnp.stack([real_part, imaginary], axis=0)
    wave_ids = wave_first + jnp.arange(wave_total, dtype=jnp.int32)
    angle_two = (lane_ids[:, None] * wave_ids[None, :] % block_width).astype(jnp.float32) * (
        2.0 * math.pi / block_width
    )
    cos_two = jnp.cos(angle_two)
    sin_two = jnp.sin(angle_two)
    table_two = jnp.stack(
        [jnp.stack([cos_two, -sin_two], axis=1), jnp.stack([sin_two, cos_two], axis=1)], axis=0
    )
    section_two = jnp.einsum(
        "iprmb,iboq->proqm", twisted, table_two, precision=lax.Precision.HIGHEST
    )
    return section_two.reshape(level_count, piece_rows, 2, wave_total * group_count) / math.sqrt(
        length_all
    )


def shards(fields, inverse, block_costs, row_length):
    field_levels = fields.shape[0] * fields.shape[1]
    row_count = fields.shape[2]
    block_width = fields.shape[3]
    own_cost = block_costs[0]
    first_longitude = lax.axis_index("col") * block_width
    relaxed = relax(fields, own_cost, inverse)
    updated = apply_tendency(fields, tendency_of(relaxed, fields))
    masked = mask_rows(updated, row_length, first_longitude)
    flat_blocks = masked.reshape(field_levels, row_count, block_width)
    whole_rows = lax.all_to_all(flat_blocks, "col", split_axis=0, concat_axis=2, tiled=True)
    share = block_width // 4 // lax.axis_size("band")
    wave_first = lax.axis_index("band") * share
    return transform(lax.all_gather(whole_rows, "band", axis=1, tiled=True), wave_first, share)


def solution(mesh):
    return jax.shard_map(
        shards,
        mesh=mesh,
        in_specs=(P(None, None, "band", "col"), P(), P("col", "band"), P("band")),
        out_specs=P("col", None, None, "band"),
        check_vma=False,
    )
```

profile of v0, /device:TPU:1, one launch (start us, length us, event | category | flops | bytes accessed | tf_op | source)
XLA Modules:
  0.0 172.3 jit_solution(11574804040881151017)
XLA Ops:
  6.5 0.0 all-gather.2.cloned.1.call-start
  6.5 1.1 copy.46
  7.6 0.0 copy-start
  7.6 10.9 %while.36 = (s32[]{:T(128)}, bf16[4,80,8,128]{3,2,1,0:T(8,128)(2,1)S(1)}, bf16[4,80,8,128]{3,2,1,0:T(8,128)(2,1)}, s32[8]{0:T(128)}, bf16[4,80,80]{2,1,0:T(8,128...) while((s32[]{:T(128)}, bf16[4,80,8,128]{3,2,1,0:T(8,128)(2,1)S(1)}, ...), condition=%wide.region_4.5_spmd, body=%wide.region_0.4_spmd.sunk | while | flops 26542092 | bytes 3328364 | solution.py:28
  7.6 1.3 constant_dynamic-slice_fusion.2
  9.0 1.4 fusion.48
  10.4 2.4 %while.37 = (s32[]{:T(128)}, bf16[4,80,4,128]{3,1,2,0:T(8,128)(2,1)S(1)}, s32[]{:T(128)}, s32[4]{0:T(128)S(1)}, bf16[4,80,80]{2,1,0:T(8,128)(2,1)}, /*index=5*/s32[]{:T(128)}) while((s32[]{:T(128)}, bf16[4,80,4,128]{3,1,2,0:T(8,128)(2,1)S(1)}, s32[]{:T(128)}, s32[4]{0:T(128)S(1)}, bf16[4,80,80]{2,1,0:T(8,128)(2,1)}, /*index=5*/s32[]{:T(128)}) %tuple.56), condition=%wide.region_3.3_spmd, body=%wide.region_2.2_spmd.sunk | while | flops 26542084 | bytes 1362025 | solution.py:25
  11.1 1.1 fusion.51
  12.8 0.2 copy_dynamic-update-slice_fusion.2
  13.1 1.3 constant_dynamic-slice_fusion.2
  14.4 1.4 fusion.48
  15.8 2.4 %while.37 = (s32[]{:T(128)}, bf16[4,80,4,128]{3,1,2,0:T(8,128)(2,1)S(1)}, s32[]{:T(128)}, s32[4]{0:T(128)S(1)}, bf16[4,80,80]{2,1,0:T(8,128)(2,1)}, /*index=5*/s32[]{:T(128)}) while((s32[]{:T(128)}, bf16[4,80,4,128]{3,1,2,0:T(8,128)(2,1)S(1)}, s32[]{:T(128)}, s32[4]{0:T(128)S(1)}, bf16[4,80,80]{2,1,0:T(8,128)(2,1)}, /*index=5*/s32[]{:T(128)}) %tuple.56), condition=%wide.region_3.3_spmd, body=%wide.region_2.2_spmd.sunk | while | flops 26542084 | bytes 1362025 | solution.py:25
  16.5 1.1 fusion.51
  18.2 0.2 copy_dynamic-update-slice_fusion.2
  18.5 1.3 fusion.9
  19.8 0.0 copy-done
  19.8 0.1 broadcast_compare_fusion.1
  19.9 1.3 fusion.11
  21.2 58.2 %all_to_all.18 = bf16[320,8,128]{2,1,0:T(8,128)(2,1)S(1)} all-to-all(bf16[320,8,128]{2,1,0:T(8,128)(2,1)S(1)} %bitcast.68), channel_id=1, replica_groups=mesh['band'=4,'col'=64] {'col'}, dimensions={0} | all-to-all | bytes 1310720 | tf_op jit(solution)/shard_map/all_to_all | solution.py:100
  79.4 0.9 copy.33
  80.3 0.0 all-gather.2.cloned.1.call-update
  80.4 0.1 fusion.39
  80.5 0.1 sine_negate_fusion
  80.7 0.1 fusion.28
  80.8 55.8 %all-gather.2.cloned.1.call-done = bf16[5,32,8192]{2,1,0:T(8,128)(2,1)} async-done(((bf16[5,8,8192]{2,1,0:T(8,128)(2,1)}), bf16[5,32,8192]{2,1,0:T(8,128)(2,1)}) %all-gather.2.cloned.1.call-update) | async-done | bytes 2621456 | tf_op jit(solution)/shard_map/all_gather | solution.py:103
  136.6 2.5 %copy.30 = bf16[20,8,64,128]{3,2,1,0:T(8,128)(2,1)S(1)} copy(bf16[20,8,64,128]{3,1,2,0:T(8,128)(2,1)} %bitcast.69) | data formatting | bytes 5242880
  139.0 4.2 %convolution_bitcast_fusion = f32[2,5,32,64,128]{4,3,0,2,1:T(8,128)S(1)} fusion(bf16[5,32,64,128,1]{3,2,1,0,4:T(8,128)(2,1)S(1)} %bitcast.67, f32[1,64,64]{1,2,0:T(8,128)S(1)} %get-tuple-element.172, f32[1,64,64]{1,2,0:T(8,128)S(1)} %get-tuple-element.173), kind=kOutput, calls=%fused_computation.12 | convolution fusion | flops 2013274112 | bytes 13139968 | tf_op jit(solution)/shard_map/icm,prcb->iprmb/dot_general | solution.py:61
  143.3 5.5 %multiply_add_fusion = (f32[1,5,32,64,128]{4,3,0,2,1:T(8,128)}, f32[1,5,32,64,128]{4,3,0,2,1:T(8,128)}) fusion(f32[2,5,32,64,128]{4,3,0,2,1:T(8,128)S(1)} %convolution_bitcast_fusion, f32[64,128]{1,0:T(8,128)S(1)} %get-tuple-element.174, f32[64,128]{1,0:T(8,128)S(1)} %get-tuple-element.175), kind=kLoop, calls=%fused_computation.11 | loop fusion | flops 7864320 | bytes 21037056 | tf_op jit(solution)/shard_map/add | solution.py:70
  148.8 15.0 %fusion.8 = f32[5,32,2,8,64]{4,3,1,0,2:T(8,128)S(1)} fusion(f32[1,5,32,64,128]{4,3,0,2,1:T(8,128)} %get-tuple-element.166, f32[1,5,32,64,128]{4,3,0,2,1:T(8,128)} %get-tuple-element.165, f32[1,128,2,8]{1,3,0,2:T(8,128)S(1)} %get-tuple-element.168, f32[1,128,2,8]{1,3,0,2:T(8,128)S(1)} %get-tuple-element.167), kind=kOutput, calls=%fused_computation.18 | convolution fusion | flops 506105856 | bytes 11157504 | tf_op jit(solution)/shard_map/iprmb,iboq->proqm/dot_general | solution.py:82
  163.8 0.3 div.13
  164.1 1.3 copy.20
  (9 shorter events, 0.2 us)
Async XLA Ops:
  6.5 130.0 %all-gather.2.cloned.1.call-start = ((), (), s32[]{:S(2)}) async-start(), calls=%async_computation.1 | async-start | bytes 3276800 | tf_op jit(solution)/shard_map/all_gather | solution.py:103
  7.6 12.2 %copy-start = (s32[8]{0:T(128)S(1)}, s32[8]{0:T(128)}, u32[]{:S(2)}) copy-start(s32[8]{0:T(128)} %param.11) | copy-start | bytes 100
Sparse Core Ops, SparseCore 0:
  80.5 56.0 all-gather.1
where the time goes:
time: 173 us; the launch traced here: 172 us
  blocking collectives  58.2 us (34%)
  waiting for transfers between devices  55.8 us (32%)
  matrix products  21.4 us (12%)
  between operations  13.5 us (8%)
  other arithmetic  11.4 us (7%)
  local copies, waits for them, and re-layouts  9.32 us (5%)
  loops' own time  2.65 us (2%)
    all_to_all x1, blocking collectives, shards(): lax.all_to_all(flat_blocks, 'col', split_axis=0, concat_axis=2, tiled=True)  58.2 us
    all_gather x1, waiting for transfers between devices, shards(): lax.all_gather(whole_rows, 'band', axis=1, tiled=True)  55.8 us
    dot_general x1, matrix products, transform(): jnp.einsum('iprmb,iboq->proqm', twisted, table_two, precision=lax.Precisi...  15 us
    add x1, other arithmetic, transform(): real_part = section_one[0] * cos_twist + section_one[1] * sin_twist  5.51 us
    dot_general x1, matrix products, transform(): jnp.einsum('icm,prcb->iprmb', table_one, values_f32, precision=lax.Precis...  4.21 us
    unnamed x4, local copies, waits for them, and re-layouts  3.55 us
  transfers between devices with their start and end apart: 1, of which 1 were waited for; matrix products, arithmetic and copies ran while one was open for 0% of the time, Pallas kernels for 0%

commit v1 on v0

v1 whole, which is shorter than its diff:
```python
import math

import jax
import jax.numpy as jnp
import numpy as np
from jax import lax
from jax.experimental import pallas as pl
from jax.experimental.pallas import tpu as pltpu
from jax.sharding import PartitionSpec as P

f32 = jnp.float32
bf16 = jnp.bfloat16
VMEM_BYTES = 40 * 1024 * 1024

FIELDS = 4
LEV = 80
ROWS = 8
BLOCK = 128
N_COL = 64
N_BAND = 4
NLON = N_COL * BLOCK
WAVES = 2048
TILES = WAVES // BLOCK
LEVELS = FIELDS * LEV // N_COL


def split_bf16(table):
    high = table.astype(np.float32).astype(jnp.bfloat16)
    low = (table - high.astype(np.float64)).astype(np.float32).astype(jnp.bfloat16)
    return high, low


def tables():
    q = np.arange(N_COL)
    angle = 2.0 * np.pi / N_COL * ((q[:, None] * q[None, :]) % N_COL)
    inner = np.concatenate([np.cos(angle), -np.sin(angle)], axis=0)
    inner = np.concatenate(split_bf16(inner), axis=1)
    u = np.arange(BLOCK)
    angle = 2.0 * np.pi / NLON * (u[:, None] * u[None, :])
    twiddle = np.stack([np.cos(angle), np.sin(angle)]).astype(np.float32)
    t = np.arange(TILES)
    angle = 2.0 * np.pi / (NLON // BLOCK) * ((t[:, None] * u[None, :]) % (NLON // BLOCK))
    cosine, sine = np.cos(angle), np.sin(angle)
    real_row = np.concatenate([cosine, sine], axis=1)
    imag_row = np.concatenate([-sine, cosine], axis=1)
    outer = np.stack([real_row, imag_row], axis=1).reshape(2 * TILES, 2 * BLOCK) / math.sqrt(NLON)
    outer = np.concatenate(split_bf16(outer), axis=0)
    return inner, twiddle, outer


def relax_kernel(cost_ref, length_ref, fields_ref, inverse_ref, out_ref, flat, state):
    first = lax.axis_index("col") * BLOCK
    flat[...] = fields_ref[...].astype(f32).reshape(FIELDS * LEV * ROWS, BLOCK)
    for f in range(FIELDS):
        for r in range(ROWS):
            piece = flat[pl.ds(f * LEV * ROWS + r, LEV, stride=ROWS), :]
            state[f, :, r * BLOCK:(r + 1) * BLOCK] = piece.astype(bf16)
    costs = [cost_ref[0, r] for r in range(ROWS)]
    most = costs[0]
    for r in range(1, ROWS):
        most = jnp.maximum(most, costs[r])
    cost_lanes = jnp.concatenate([jnp.full((1, BLOCK), costs[r], jnp.int32) for r in range(ROWS)], axis=1)

    @pl.loop(0, most)
    def _(s):
        active = s < cost_lanes
        for f in range(FIELDS):
            now = state[f]
            new = jnp.dot(inverse_ref[f], now, preferred_element_type=f32)
            state[f] = jnp.where(active, new, now.astype(f32)).astype(bf16)

    lane = first + lax.broadcasted_iota(jnp.int32, (1, BLOCK), 1)
    for r in range(ROWS):
        keep = lane < length_ref[r]
        for f in range(FIELDS):
            rows = pl.ds(f * LEV * ROWS + r, LEV, stride=ROWS)
            initial = flat[rows, :]
            relaxed = state[f, :, r * BLOCK:(r + 1) * BLOCK].astype(f32)
            tendency = (relaxed - initial).astype(bf16).astype(f32)
            updated = (initial + tendency).astype(bf16).astype(f32)
            flat[rows, :] = jnp.where(keep, updated, 0.0)
    out_ref[...] = flat[...].reshape(FIELDS * LEV, ROWS, BLOCK).astype(bf16)


def relax(fields, inverse, costs, lengths):
    vmem = pl.BlockSpec(memory_space=pltpu.VMEM)
    smem = pl.BlockSpec(memory_space=pltpu.SMEM)
    return pl.pallas_call(
        relax_kernel,
        out_shape=jax.ShapeDtypeStruct((FIELDS * LEV, ROWS, BLOCK), bf16),
        in_specs=[smem, smem, vmem, vmem],
        out_specs=vmem,
        scratch_shapes=[
            pltpu.VMEM((FIELDS * LEV * ROWS, BLOCK), f32),
            pltpu.VMEM((FIELDS, LEV, ROWS * BLOCK), bf16),
        ],
        compiler_params=pltpu.CompilerParams(vmem_limit_bytes=VMEM_BYTES),
        name="relax",
    )(costs, lengths, fields, inverse)


def fourier_kernel(x_ref, inner_ref, twiddle_ref, outer_ref, out_ref, flat):
    flat[...] = x_ref[...].astype(f32).reshape(N_COL * LEVELS * ROWS, BLOCK)
    inner = inner_ref[...]
    outer = outer_ref[...]

    @pl.loop(0, LEVELS)
    def _(i):
        for r in range(0, ROWS, 2):
            pair = [flat[pl.ds(i * ROWS + r + d, N_COL, stride=LEVELS * ROWS), :] for d in range(2)]
            x = jnp.concatenate(pair, axis=1).astype(bf16)
            y = jnp.dot(inner, jnp.concatenate([x, x], axis=0), preferred_element_type=f32)
            for d in range(2):
                lanes = slice(d * BLOCK, (d + 1) * BLOCK)
                real, imag = y[:N_COL, lanes], y[N_COL:, lanes]
                halves = []
                for h in range(2):
                    cosine = twiddle_ref[0, h * N_COL:(h + 1) * N_COL, :]
                    sine = twiddle_ref[1, h * N_COL:(h + 1) * N_COL, :]
                    halves.append(jnp.concatenate(
                        [(real * cosine + imag * sine).astype(bf16), (imag * cosine - real * sine).astype(bf16)], axis=1))
                z = jnp.concatenate(halves, axis=0)
                w = lax.dot_general(outer, z, (((1,), (1,)), ((), ())), preferred_element_type=f32)
                w = w[:2 * TILES] + w[2 * TILES:]
                for band in range(N_BAND):
                    out_ref[band, i, r + d] = w[band * 8:(band + 1) * 8].astype(bf16)


def fourier(pieces):
    inner, twiddle, outer = tables()
    vmem = pl.BlockSpec(memory_space=pltpu.VMEM)
    return pl.pallas_call(
        fourier_kernel,
        out_shape=jax.ShapeDtypeStruct((N_BAND, LEVELS, ROWS, 8, BLOCK), bf16),
        in_specs=[vmem] * 4,
        out_specs=vmem,
        scratch_shapes=[pltpu.VMEM((N_COL * LEVELS * ROWS, BLOCK), f32)],
        compiler_params=pltpu.CompilerParams(vmem_limit_bytes=VMEM_BYTES),
        name="fourier",
    )(pieces, jnp.asarray(inner), jnp.asarray(twiddle), jnp.asarray(outer))


def finish_kernel(x_ref, out_ref):
    for i in range(LEVELS):
        for band in range(N_BAND):
            for r in range(ROWS):
                piece = x_ref[band, i, r].astype(f32)
                for t in range(4):
                    out_ref[i, band * ROWS + r, :, t * BLOCK:(t + 1) * BLOCK] = piece[2 * t:2 * t + 2]


def finish(pieces):
    vmem = pl.BlockSpec(memory_space=pltpu.VMEM)
    return pl.pallas_call(
        finish_kernel,
        out_shape=jax.ShapeDtypeStruct((LEVELS, N_BAND * ROWS, 2, WAVES // N_BAND), f32),
        in_specs=[vmem],
        out_specs=vmem,
        compiler_params=pltpu.CompilerParams(vmem_limit_bytes=VMEM_BYTES),
        name="finish",
    )(pieces)


def shards(fields, inverse, block_costs, row_length):
    updated = relax(fields, inverse, block_costs, row_length)
    whole_rows = lax.all_to_all(updated, "col", split_axis=0, concat_axis=0, tiled=True)
    spectra = fourier(whole_rows)
    spectra = lax.all_to_all(spectra, "band", split_axis=0, concat_axis=0, tiled=True)
    return finish(spectra)


def solution(mesh):
    return jax.shard_map(
        shards,
        mesh=mesh,
        in_specs=(P(None, None, "band", "col"), P(), P("col", "band"), P("band")),
        out_specs=P("col", None, None, "band"),
        check_vma=False,
    )
```

time: 173 us -> 65.3 us (0.38)
  waiting for transfers between devices: 55.8 us -> 0 us
  matrix products: 21.4 us -> 0 us
  between operations: 13.5 us -> 0.04 us
  other arithmetic: 11.4 us -> 0 us
  Pallas kernels: 0 us -> 7.54 us
  local copies, waits for them, and re-layouts: 9.32 us -> 3.3 us
  blocking collectives: 58.2 us -> 54.2 us
  loops' own time: 2.65 us -> 0 us
    all_gather x1 -> x0, waiting for transfers between devices: 55.8 us -> none  [shards(): lax.all_gather(whole_rows, 'band', axis=1, tiled=True)]
    dot_general x4 -> x0, matrix products: 21.4 us -> none  [the longest x1 15 us: transform(): jnp.einsum('iprmb,iboq->proqm', twisted, table_two, precision=lax.Precisi...]
    pallas_call x0 -> x3, Pallas kernels: none -> 7.54 us  [the longest x1 4.74 us: fourier(): pl.pallas_call(fourier_kernel, out_shape=jax.ShapeDtypeStruct((N_BAND, LE...]
    add x3 -> x0, other arithmetic: 5.52 us -> none  [the longest x1 5.51 us: transform(): real_part = section_one[0] * cos_twist + section_one[1] * sin_twist]
    all_to_all x1 -> x2, blocking collectives: 58.2 us -> 54.2 us  [the longest x1 36 us: shards(): lax.all_to_all(updated, 'col', split_axis=0, concat_axis=0, tiled=True)]
    reduce_max x2 -> x0, other arithmetic: 2.84 us -> none  [one_group(): jnp.max(steps_here)]
    another operation x3 -> x0, loops' own time: 2.65 us -> none  [the longest x2 2.57 us: one_group(): lax.fori_loop(jnp.int32(0), jnp.max(steps_here), sweep, block_set)]
    dynamic_slice x4 -> x0, local copies, waits for them, and re-layouts: 2.63 us -> none  [one_group(): block_set = lax.dynamic_slice_in_dim(blocks, offset_start, group_width, 2)]
  transfers between devices with their start and end apart: 1 -> 0, of which waited for: 1 -> 0; matrix products, arithmetic and copies ran while one was open for 0% -> 0% of each run, Pallas kernels for 0% -> 0%
where the time goes in v1:
time: 65.3 us; the launch traced here: 65.1 us
  blocking collectives  54.2 us (83%)
  Pallas kernels  7.54 us (12%)
  local copies, waits for them, and re-layouts  3.3 us (5%)
    all_to_all x1, blocking collectives, shards(): lax.all_to_all(updated, 'col', split_axis=0, concat_axis=0, tiled=True)  36 us
    all_to_all x1, blocking collectives, shards(): lax.all_to_all(spectra, 'band', split_axis=0, concat_axis=0, tiled=True)  18.2 us
    pallas_call x1, Pallas kernels, fourier(): pl.pallas_call(fourier_kernel, out_shape=jax.ShapeDtypeStruct((N_BAND, LE...  4.74 us
    unnamed x14, local copies, waits for them, and re-layouts  3.3 us
    pallas_call x1, Pallas kernels, relax(): pl.pallas_call(relax_kernel, out_shape=jax.ShapeDtypeStruct((FIELDS * LEV...  1.79 us

profile of v1, /device:TPU:1, one launch (start us, length us, event | category | flops | bytes accessed | tf_op | source)
XLA Modules:
  0.0 65.1 jit_solution(7129482216822982978)
XLA Ops:
  0.0 0.0 copy-start
  0.0 1.1 %copy-done = bf16[4,80,8,128]{3,2,1,0:T(8,128)(2,1)S(1)} copy-done((bf16[4,80,8,128]{3,2,1,0:T(8,128)(2,1)S(1)}, bf16[4,80,8,128]{3,2,1,0:T(8,128)(2,1)}, u32[]{:S(2)}) %copy-start) | copy-done | bytes 655384
  1.1 0.0 copy-start.2
  1.1 0.9 %copy-done.2 = bf16[4,80,80]{2,1,0:T(8,128)(2,1)S(1)} copy-done((bf16[4,80,80]{2,1,0:T(8,128)(2,1)S(1)}, bf16[4,80,80]{2,1,0:T(8,128)(2,1)}, u32[]{:S(2)}) %copy-start.2) | copy-done | bytes 51224
  2.0 0.0 copy-start.5
  2.0 0.7 %copy-done.5 = s32[1,8]{1,0:T(1,128)S(1)} copy-done((s32[1,8]{1,0:T(1,128)S(1)}, s32[1,8]{1,0:T(1,128)}, u32[]{:S(2)}) %copy-start.5) | copy-done | bytes 56
  2.6 0.0 copy-start.6
  2.6 0.7 %copy-done.6 = s32[8]{0:T(128)S(1)} copy-done((s32[8]{0:T(128)S(1)}, s32[8]{0:T(128)}, u32[]{:S(2)}) %copy-start.6) | copy-done | bytes 56
  3.3 1.8 %relax.1 = bf16[320,8,128]{2,1,0:T(8,128)(2,1)S(1)} custom-call(s32[1,8]{1,0:T(1,128)S(1)} %copy-done.5, s32[8]{0:T(128)S(1)} %copy-done.6, bf16[4,80,8,128]{3,2,1,0:T(8,128)(2,1)S(1)} %copy-done, bf16[4,80,80]{2,1,0:T(8,128)(2,1)S(1)} %copy-done.2), custom_call_target="tpu_custom_call" | custom-call | tf_op jit(solution)/shard_map/relax/pallas_call | solution.py:88
  5.1 0.0 copy-start.1
  5.1 0.0 copy-start.3
  5.1 0.0 copy-start.4
  5.1 36.0 %all_to_all.10.x_ref = bf16[320,8,128]{2,1,0:T(8,128)(2,1)S(1)} all-to-all(bf16[320,8,128]{2,1,0:T(8,128)(2,1)S(1)} %relax.1), channel_id=1, replica_groups=mesh['band'=4,'col'=64] {'col'}, dimensions={0} | all-to-all | bytes 1310720 | tf_op jit(solution)/shard_map/all_to_all | solution.py:166
  41.1 0.0 copy-done.1
  41.1 0.0 copy-done.3
  41.1 0.0 copy-done.4
  41.1 4.7 %fourier.1 = bf16[4,5,8,8,128]{4,3,2,1,0:T(8,128)(2,1)S(1)} custom-call(bf16[320,8,128]{2,1,0:T(8,128)(2,1)S(1)} %all_to_all.10.x_ref, bf16[128,128]{1,0:T(8,128)(2,1)S(1)} %copy-done.4, f32[2,128,128]{2,1,0:T(8,128)S(1)} %copy-done.1, bf16[64,256]{1,0:T(8,128)(2,1)S(1)} %copy-done.3), custom_call_target="tpu_custom_call" | custom-call | tf_op jit(solution)/shard_map/fourier/pallas_call | solution.py:132
  45.9 18.2 %all_to_all.11.x_ref = bf16[4,5,8,8,128]{4,3,2,1,0:T(8,128)(2,1)S(1)} all-to-all(bf16[4,5,8,8,128]{4,3,2,1,0:T(8,128)(2,1)S(1)} %fourier.1), channel_id=1, replica_groups=mesh['band'=4,'col'=64] {'band'}, dimensions={0} | all-to-all | bytes 655360 | tf_op jit(solution)/shard_map/all_to_all | solution.py:168
  64.1 1.0 %finish.1 = f32[5,32,2,512]{3,2,1,0:T(2,128)} custom-call(bf16[4,5,8,8,128]{4,3,2,1,0:T(8,128)(2,1)S(1)} %all_to_all.11.x_ref), custom_call_target="tpu_custom_call" | custom-call | tf_op jit(solution)/shard_map/finish/pallas_call | solution.py:154
Async XLA Ops:
  0.0 1.1 %copy-start = (bf16[4,80,8,128]{3,2,1,0:T(8,128)(2,1)S(1)}, bf16[4,80,8,128]{3,2,1,0:T(8,128)(2,1)}, u32[]{:S(2)}) copy-start(bf16[4,80,8,128]{3,2,1,0:T(8,128)(2,1)} %fields_ref.1) | copy-start | bytes 1966084
  1.1 0.9 %copy-start.2 = (bf16[4,80,80]{2,1,0:T(8,128)(2,1)S(1)}, bf16[4,80,80]{2,1,0:T(8,128)(2,1)}, u32[]{:S(2)}) copy-start(bf16[4,80,80]{2,1,0:T(8,128)(2,1)} %inverse_ref.1) | copy-start | bytes 153604
  2.0 0.7 %copy-start.5 = (s32[1,8]{1,0:T(1,128)S(1)}, s32[1,8]{1,0:T(1,128)}, u32[]{:S(2)}) copy-start(s32[1,8]{1,0:T(1,128)} %cost_ref.1) | copy-start | bytes 100
  2.6 0.7 %copy-start.6 = (s32[8]{0:T(128)S(1)}, s32[8]{0:T(128)}, u32[]{:S(2)}) copy-start(s32[8]{0:T(128)} %length_ref.1) | copy-start | bytes 100
  5.1 36.0 %copy-start.1 = (f32[2,128,128]{2,1,0:T(8,128)S(1)}, f32[2,128,128]{2,1,0:T(8,128)}, u32[]{:S(2)}) copy-start(f32[2,128,128]{2,1,0:T(8,128)} %constant.7.clone.twiddle_ref) | copy-start | bytes 393220
  5.1 36.0 %copy-start.3 = (bf16[64,256]{1,0:T(8,128)(2,1)S(1)}, bf16[64,256]{1,0:T(8,128)(2,1)}, u32[]{:S(2)}) copy-start(bf16[64,256]{1,0:T(8,128)(2,1)} %constant.8.clone.outer_ref) | copy-start | bytes 98308
  5.1 36.0 %copy-start.4 = (bf16[128,128]{1,0:T(8,128)(2,1)S(1)}, bf16[128,128]{1,0:T(8,128)(2,1)}, u32[]{:S(2)}) copy-start(bf16[128,128]{1,0:T(8,128)(2,1)} %constant.6.clone.inner_ref) | copy-start | bytes 98308

commit v2 on v1

--- a/solution.py
+++ b/solution.py
@@ -6,7 +6,7 @@
 from jax import lax
 from jax.experimental import pallas as pl
 from jax.experimental.pallas import tpu as pltpu
-from jax.sharding import PartitionSpec as P
+from jax.sharding import Mesh, PartitionSpec as P
 
 f32 = jnp.float32
 bf16 = jnp.bfloat16
@@ -22,6 +22,12 @@
 WAVES = 2048
 TILES = WAVES // BLOCK
 LEVELS = FIELDS * LEV // N_COL
+COL_AXES = ("zhi", "y", "x", "core")
+BAND_AXES = ("b1", "b0")
+SEND_ORDER = ("y", "zhi", "x", "core")
+SECTION = LEV // 2
+SECTIONS = [y + 4 * zhi for y in range(4) for zhi in range(2)]
+BANDS = [b0 + 2 * b1 for b0 in range(2) for b1 in range(2)]
 
 
 def split_bf16(table):
@@ -32,7 +38,8 @@
 
 def tables():
     q = np.arange(N_COL)
-    angle = 2.0 * np.pi / N_COL * ((q[:, None] * q[None, :]) % N_COL)
+    source = np.concatenate([np.arange(8) + 8 * section for section in SECTIONS])
+    angle = 2.0 * np.pi / N_COL * ((q[:, None] * source[None, :]) % N_COL)
     inner = np.concatenate([np.cos(angle), -np.sin(angle)], axis=0)
     inner = np.concatenate(split_bf16(inner), axis=1)
     u = np.arange(BLOCK)
@@ -45,11 +52,12 @@
     imag_row = np.concatenate([-sine, cosine], axis=1)
     outer = np.stack([real_row, imag_row], axis=1).reshape(2 * TILES, 2 * BLOCK) / math.sqrt(NLON)
     outer = np.concatenate(split_bf16(outer), axis=0)
+    outer = np.stack([outer[:, :BLOCK], outer[:, BLOCK:]])
     return inner, twiddle, outer
 
 
 def relax_kernel(cost_ref, length_ref, fields_ref, inverse_ref, out_ref, flat, state):
-    first = lax.axis_index("col") * BLOCK
+    first = lax.axis_index(COL_AXES) * BLOCK
     flat[...] = fields_ref[...].astype(f32).reshape(FIELDS * LEV * ROWS, BLOCK)
     for f in range(FIELDS):
         for r in range(ROWS):
@@ -79,7 +87,9 @@
             tendency = (relaxed - initial).astype(bf16).astype(f32)
             updated = (initial + tendency).astype(bf16).astype(f32)
             flat[rows, :] = jnp.where(keep, updated, 0.0)
-    out_ref[...] = flat[...].reshape(FIELDS * LEV, ROWS, BLOCK).astype(bf16)
+    for place, section in enumerate(SECTIONS):
+        piece = flat[section * SECTION * ROWS:(section + 1) * SECTION * ROWS, :].reshape(SECTION, ROWS, BLOCK)
+        out_ref[place * SECTION:(place + 1) * SECTION] = piece.astype(bf16)
 
 
 def relax(fields, inverse, costs, lengths):
@@ -102,7 +112,7 @@
 def fourier_kernel(x_ref, inner_ref, twiddle_ref, outer_ref, out_ref, flat):
     flat[...] = x_ref[...].astype(f32).reshape(N_COL * LEVELS * ROWS, BLOCK)
     inner = inner_ref[...]
-    outer = outer_ref[...]
+    outer = jnp.concatenate([outer_ref[0], outer_ref[1]], axis=1)
 
     @pl.loop(0, LEVELS)
     def _(i):
@@ -122,8 +132,8 @@
                 z = jnp.concatenate(halves, axis=0)
                 w = lax.dot_general(outer, z, (((1,), (1,)), ((), ())), preferred_element_type=f32)
                 w = w[:2 * TILES] + w[2 * TILES:]
-                for band in range(N_BAND):
-                    out_ref[band, i, r + d] = w[band * 8:(band + 1) * 8].astype(bf16)
+                for place, band in enumerate(BANDS):
+                    out_ref[place, i, r + d] = w[band * 8:(band + 1) * 8].astype(bf16)
 
 
 def fourier(pieces):
@@ -142,9 +152,9 @@
 
 def finish_kernel(x_ref, out_ref):
     for i in range(LEVELS):
-        for band in range(N_BAND):
+        for place, band in enumerate(BANDS):
             for r in range(ROWS):
-                piece = x_ref[band, i, r].astype(f32)
+                piece = x_ref[place, i, r].astype(f32)
                 for t in range(4):
                     out_ref[i, band * ROWS + r, :, t * BLOCK:(t + 1) * BLOCK] = piece[2 * t:2 * t + 2]
 
@@ -163,17 +173,18 @@
 
 def shards(fields, inverse, block_costs, row_length):
     updated = relax(fields, inverse, block_costs, row_length)
-    whole_rows = lax.all_to_all(updated, "col", split_axis=0, concat_axis=0, tiled=True)
+    whole_rows = lax.all_to_all(updated, SEND_ORDER, split_axis=0, concat_axis=0, tiled=True)
     spectra = fourier(whole_rows)
-    spectra = lax.all_to_all(spectra, "band", split_axis=0, concat_axis=0, tiled=True)
+    spectra = lax.all_to_all(spectra, ("b0", "b1"), split_axis=0, concat_axis=0, tiled=True)
     return finish(spectra)
 
 
 def solution(mesh):
+    fine = Mesh(mesh.devices.reshape(2, 2, 2, 4, 4, 2), BAND_AXES + COL_AXES)
     return jax.shard_map(
         shards,
-        mesh=mesh,
-        in_specs=(P(None, None, "band", "col"), P(), P("col", "band"), P("band")),
-        out_specs=P("col", None, None, "band"),
+        mesh=fine,
+        in_specs=(P(None, None, BAND_AXES, COL_AXES), P(), P(COL_AXES, BAND_AXES), P(BAND_AXES)),
+        out_specs=P(COL_AXES, None, None, BAND_AXES),
         check_vma=False,
     )

time: 65.3 us -> 64.1 us (0.982); the launches traced: 65.1 us -> 63.1 us
  blocking collectives: 54.2 us -> 52.2 us
    all_to_all x2, blocking collectives: 54.2 us -> 52.2 us  [the longest x1 34.8 us: shards(): lax.all_to_all(updated, SEND_ORDER, split_axis=0, concat_axis=0, tiled=True)]
where the time goes in v2:
time: 64.1 us; the launch traced here: 63.1 us
  blocking collectives  52.2 us (81%)
  Pallas kernels  7.55 us (12%)
  local copies, waits for them, and re-layouts  3.3 us (5%)
    all_to_all x1, blocking collectives, shards(): lax.all_to_all(updated, SEND_ORDER, split_axis=0, concat_axis=0, tiled=True)  34.8 us
    all_to_all x1, blocking collectives, shards(): lax.all_to_all(spectra, ('b0', 'b1'), split_axis=0, concat_axis=0, tiled=...  17.4 us
    pallas_call x1, Pallas kernels, fourier(): pl.pallas_call(fourier_kernel, out_shape=jax.ShapeDtypeStruct((N_BAND, LE...  4.75 us
    unnamed x14, local copies, waits for them, and re-layouts  3.3 us
    pallas_call x1, Pallas kernels, relax(): pl.pallas_call(relax_kernel, out_shape=jax.ShapeDtypeStruct((FIELDS * LEV...  1.79 us

profile of v2, /device:TPU:1, one launch (start us, length us, event | category | flops | bytes accessed | tf_op | source)
XLA Modules:
  0.0 63.1 jit_solution(10229572473878054881)
XLA Ops:
  0.0 0.0 copy-start
  0.0 1.1 %copy-done = bf16[4,80,8,128]{3,2,1,0:T(8,128)(2,1)S(1)} copy-done((bf16[4,80,8,128]{3,2,1,0:T(8,128)(2,1)S(1)}, bf16[4,80,8,128]{3,2,1,0:T(8,128)(2,1)}, u32[]{:S(2)}) %copy-start) | copy-done | bytes 655384
  1.1 0.0 copy-start.2
  1.1 0.9 %copy-done.2 = bf16[4,80,80]{2,1,0:T(8,128)(2,1)S(1)} copy-done((bf16[4,80,80]{2,1,0:T(8,128)(2,1)S(1)}, bf16[4,80,80]{2,1,0:T(8,128)(2,1)}, u32[]{:S(2)}) %copy-start.2) | copy-done | bytes 51224
  2.0 0.0 copy-start.5
  2.0 0.7 %copy-done.5 = s32[1,8]{1,0:T(1,128)S(1)} copy-done((s32[1,8]{1,0:T(1,128)S(1)}, s32[1,8]{1,0:T(1,128)}, u32[]{:S(2)}) %copy-start.5) | copy-done | bytes 56
  2.6 0.0 copy-start.6
  2.6 0.7 %copy-done.6 = s32[8]{0:T(128)S(1)} copy-done((s32[8]{0:T(128)S(1)}, s32[8]{0:T(128)}, u32[]{:S(2)}) %copy-start.6) | copy-done | bytes 56
  3.3 1.8 %relax.1 = bf16[320,8,128]{2,1,0:T(8,128)(2,1)S(1)} custom-call(s32[1,8]{1,0:T(1,128)S(1)} %copy-done.5, s32[8]{0:T(128)S(1)} %copy-done.6, bf16[4,80,8,128]{3,2,1,0:T(8,128)(2,1)S(1)} %copy-done, bf16[4,80,80]{2,1,0:T(8,128)(2,1)S(1)} %copy-done.2), custom_call_target="tpu_custom_call" | custom-call | tf_op jit(solution)/shard_map/relax/pallas_call | solution.py:98
  5.1 0.0 copy-start.1
  5.1 0.0 copy-start.3
  5.1 0.0 copy-start.4
  5.1 34.8 %all_to_all.10.x_ref = bf16[320,8,128]{2,1,0:T(8,128)(2,1)S(1)} all-to-all(bf16[320,8,128]{2,1,0:T(8,128)(2,1)S(1)} %relax.1), channel_id=1, replica_groups=mesh['b1'=2,'b0'=2,'zhi'=2,'y'=4,'x'=4,'core'=2] {'y','zhi','x','core'}, dimensions={0} | all-to-all | bytes 1310720 | tf_op jit(solution)/shard_map/all_to_all | solution.py:176
  39.9 0.0 copy-done.1
  39.9 0.0 copy-done.3
  39.9 0.0 copy-done.4
  39.9 4.7 %fourier.1 = bf16[4,5,8,8,128]{4,3,2,1,0:T(8,128)(2,1)S(1)} custom-call(bf16[320,8,128]{2,1,0:T(8,128)(2,1)S(1)} %all_to_all.10.x_ref, bf16[128,128]{1,0:T(8,128)(2,1)S(1)} %copy-done.4, f32[2,128,128]{2,1,0:T(8,128)S(1)} %copy-done.1, bf16[2,64,128]{2,1,0:T(8,128)(2,1)S(1)} %copy-done.3), custom_call_target="tpu_custom_call" | custom-call | tf_op jit(solution)/shard_map/fourier/pallas_call | solution.py:142
  44.7 17.4 %all_to_all.11.x_ref = bf16[4,5,8,8,128]{4,3,2,1,0:T(8,128)(2,1)S(1)} all-to-all(bf16[4,5,8,8,128]{4,3,2,1,0:T(8,128)(2,1)S(1)} %fourier.1), channel_id=1, replica_groups=mesh['b1'=2,'b0'=2,'zhi'=2,'y'=4,'x'=4,'core'=2] {'b0','b1'}, dimensions={0} | all-to-all | bytes 655360 | tf_op jit(solution)/shard_map/all_to_all | solution.py:178
  62.1 1.0 %finish.1 = f32[5,32,2,512]{3,2,1,0:T(2,128)} custom-call(bf16[4,5,8,8,128]{4,3,2,1,0:T(8,128)(2,1)S(1)} %all_to_all.11.x_ref), custom_call_target="tpu_custom_call" | custom-call | tf_op jit(solution)/shard_map/finish/pallas_call | solution.py:164
Async XLA Ops:
  0.0 1.1 %copy-start = (bf16[4,80,8,128]{3,2,1,0:T(8,128)(2,1)S(1)}, bf16[4,80,8,128]{3,2,1,0:T(8,128)(2,1)}, u32[]{:S(2)}) copy-start(bf16[4,80,8,128]{3,2,1,0:T(8,128)(2,1)} %fields_ref.1) | copy-start | bytes 1966084
  1.1 0.9 %copy-start.2 = (bf16[4,80,80]{2,1,0:T(8,128)(2,1)S(1)}, bf16[4,80,80]{2,1,0:T(8,128)(2,1)}, u32[]{:S(2)}) copy-start(bf16[4,80,80]{2,1,0:T(8,128)(2,1)} %inverse_ref.1) | copy-start | bytes 153604
  2.0 0.7 %copy-start.5 = (s32[1,8]{1,0:T(1,128)S(1)}, s32[1,8]{1,0:T(1,128)}, u32[]{:S(2)}) copy-start(s32[1,8]{1,0:T(1,128)} %cost_ref.1) | copy-start | bytes 100
  2.6 0.7 %copy-start.6 = (s32[8]{0:T(128)S(1)}, s32[8]{0:T(128)}, u32[]{:S(2)}) copy-start(s32[8]{0:T(128)} %length_ref.1) | copy-start | bytes 100
  5.1 34.8 %copy-start.1 = (f32[2,128,128]{2,1,0:T(8,128)S(1)}, f32[2,128,128]{2,1,0:T(8,128)}, u32[]{:S(2)}) copy-start(f32[2,128,128]{2,1,0:T(8,128)} %constant.7.clone.twiddle_ref) | copy-start | bytes 393220
  5.1 34.8 %copy-start.3 = (bf16[2,64,128]{2,1,0:T(8,128)(2,1)S(1)}, bf16[2,64,128]{2,1,0:T(8,128)(2,1)}, u32[]{:S(2)}) copy-start(bf16[2,64,128]{2,1,0:T(8,128)(2,1)} %constant.8.clone.outer_ref) | copy-start | bytes 98308
  5.1 34.8 %copy-start.4 = (bf16[128,128]{1,0:T(8,128)(2,1)S(1)}, bf16[128,128]{1,0:T(8,128)(2,1)}, u32[]{:S(2)}) copy-start(bf16[128,128]{1,0:T(8,128)(2,1)} %constant.6.clone.inner_ref) | copy-start | bytes 98308

commit v3 on v2

v3 whole, which is shorter than its diff:
```python
import functools
import math

import jax
import jax.numpy as jnp
import numpy as np
from jax import lax
from jax.experimental import pallas as pl
from jax.experimental.pallas import tpu as pltpu
from jax.sharding import Mesh, PartitionSpec as P

f32 = jnp.float32
bf16 = jnp.bfloat16
VMEM_BYTES = 40 * 1024 * 1024

FIELDS = 4
LEV = 80
ROWS = 8
BLOCK = 128
N_COL = 64
N_BAND = 4
NLON = N_COL * BLOCK
WAVES = 2048
LEVELS = FIELDS * LEV // N_COL
COL_AXES = ("zhi", "y", "x", "core")
HALF = N_COL // 2


def split_bf16(table):
    high = table.astype(np.float32).astype(jnp.bfloat16)
    low = (table - high.astype(np.float64)).astype(np.float32).astype(jnp.bfloat16)
    return high, low


def tables():
    q = np.arange(N_COL)
    s = np.arange(HALF)
    angle = 2.0 * np.pi / N_COL * ((q[:, None] * s[None, :]) % N_COL)
    inner = np.concatenate([np.cos(angle), -np.sin(angle)], axis=0)
    sign = np.where(np.arange(2 * N_COL) % 2 == 0, 1.0, -1.0)
    inner = np.stack([inner, inner * sign[:, None]])
    inner = np.concatenate(split_bf16(inner), axis=2)
    b = np.arange(BLOCK)
    angle = 2.0 * np.pi / NLON * (q[:, None] * b[None, :])
    twiddle = np.stack([np.cos(angle), np.sin(angle)]).astype(np.float32)
    p = np.arange(WAVES // N_COL).reshape(-1, 2).T.reshape(-1)
    angle = 2.0 * np.pi / BLOCK * ((p[:, None] * b[None, :]) % BLOCK)
    cosine, sine = np.cos(angle), np.sin(angle)
    real_row = np.concatenate([cosine, sine], axis=1)
    imag_row = np.concatenate([-sine, cosine], axis=1)
    outer = np.stack([real_row, imag_row], axis=1).reshape(2 * WAVES // N_COL, 2 * BLOCK) / math.sqrt(NLON)
    outer = np.concatenate(split_bf16(outer), axis=0)
    outer = np.stack([outer[:, :BLOCK], outer[:, BLOCK:]])
    return inner, twiddle, outer


def relax_kernel(cost_ref, length_ref, fields_ref, inverse_ref, out_ref, flat, state):
    first = lax.axis_index(COL_AXES) * BLOCK
    flat[...] = fields_ref[...].astype(f32).reshape(FIELDS * LEV * ROWS, BLOCK)
    for f in range(FIELDS):
        for r in range(ROWS):
            piece = flat[pl.ds(f * LEV * ROWS + r, LEV, stride=ROWS), :]
            state[f, :, r * BLOCK:(r + 1) * BLOCK] = piece.astype(bf16)
    costs = [cost_ref[0, r] for r in range(ROWS)]
    most = costs[0]
    for r in range(1, ROWS):
        most = jnp.maximum(most, costs[r])
    cost_lanes = jnp.concatenate([jnp.full((1, BLOCK), costs[r], jnp.int32) for r in range(ROWS)], axis=1)

    @pl.loop(0, most)
    def _(s):
        active = s < cost_lanes
        for f in range(FIELDS):
            now = state[f]
            new = jnp.dot(inverse_ref[f], now, preferred_element_type=f32)
            state[f] = jnp.where(active, new, now.astype(f32)).astype(bf16)

    lane = first + lax.broadcasted_iota(jnp.int32, (1, BLOCK), 1)
    for r in range(ROWS):
        keep = lane < length_ref[r]
        for f in range(FIELDS):
            rows = pl.ds(f * LEV * ROWS + r, LEV, stride=ROWS)
            initial = flat[rows, :]
            relaxed = state[f, :, r * BLOCK:(r + 1) * BLOCK].astype(f32)
            tendency = (relaxed - initial).astype(bf16).astype(f32)
            updated = (initial + tendency).astype(bf16).astype(f32)
            flat[rows, :] = jnp.where(keep, updated, 0.0)
    span = HALF * LEVELS
    for h in range(2):
        piece = flat[h * span * ROWS:(h + 1) * span * ROWS, :].reshape(HALF, LEVELS, ROWS, BLOCK)
        out_ref[:, h] = piece.astype(bf16)


def relax(fields, inverse, costs, lengths):
    vmem = pl.BlockSpec(memory_space=pltpu.VMEM)
    smem = pl.BlockSpec(memory_space=pltpu.SMEM)
    return pl.pallas_call(
        relax_kernel,
        out_shape=jax.ShapeDtypeStruct((HALF, 2, LEVELS, ROWS, BLOCK), bf16),
        in_specs=[smem, smem, vmem, vmem],
        out_specs=vmem,
        scratch_shapes=[
            pltpu.VMEM((FIELDS * LEV * ROWS, BLOCK), f32),
            pltpu.VMEM((FIELDS, LEV, ROWS * BLOCK), bf16),
        ],
        compiler_params=pltpu.CompilerParams(vmem_limit_bytes=VMEM_BYTES),
        name="relax",
    )(costs, lengths, fields, inverse)


def fourier_kernel(own, x_ref, inner_ref, twiddle_ref, outer_ref, out_ref, flat):
    half = lax.axis_index("zhi")
    band = lax.axis_index("band")
    part = half if own else 1 - half
    flat[...] = x_ref[:, part].astype(f32).reshape(HALF * LEVELS * ROWS, BLOCK)
    inner = inner_ref[half]
    outer = jnp.concatenate([outer_ref[0], outer_ref[1]], axis=1)
    cosine, sine = twiddle_ref[0], twiddle_ref[1]
    left = lax.broadcasted_iota(jnp.int32, (1, BLOCK), 1) < N_COL
    place = [lax.rem(to + N_BAND - band, N_BAND) for to in range(N_BAND)]
    waves = WAVES // N_COL

    @pl.loop(0, LEVELS)
    def _(i):
        for r in range(0, ROWS, 4):
            twisted = []
            for e in range(r, r + 4, 2):
                pair = [flat[pl.ds(i * ROWS + e + d, HALF, stride=LEVELS * ROWS), :] for d in range(2)]
                x = jnp.concatenate(pair, axis=1).astype(bf16)
                y = jnp.dot(inner, jnp.concatenate([x, x], axis=0), preferred_element_type=f32)
                for d in range(2):
                    lanes = slice(d * BLOCK, (d + 1) * BLOCK)
                    real, imag = y[:N_COL, lanes], y[N_COL:, lanes]
                    twisted.append(jnp.concatenate(
                        [(real * cosine + imag * sine).astype(bf16), (imag * cosine - real * sine).astype(bf16)], axis=1))
            z = jnp.concatenate(twisted, axis=0)
            w = lax.dot_general(outer, z, (((1,), (1,)), ((), ())), preferred_element_type=f32)
            w = w[:2 * waves] + w[2 * waves:]
            for k in range(2):
                even = w[:waves, k * BLOCK:(k + 1) * BLOCK]
                odd = w[waves:, k * BLOCK:(k + 1) * BLOCK]
                rows = (jnp.where(left, even, pltpu.roll(odd, N_COL, 1)), jnp.where(left, pltpu.roll(even, N_COL, 1), odd))
                for d in range(2):
                    for to in range(N_BAND):
                        out_ref[place[to], i, r + 2 * k + d] = rows[d][to * 8:(to + 1) * 8].astype(bf16)


def fourier(pieces, own):
    inner, twiddle, outer = tables()
    vmem = pl.BlockSpec(memory_space=pltpu.VMEM)
    return pl.pallas_call(
        functools.partial(fourier_kernel, own),
        out_shape=jax.ShapeDtypeStruct((N_BAND, LEVELS, ROWS, 8, BLOCK), bf16),
        in_specs=[vmem] * 4,
        out_specs=vmem,
        scratch_shapes=[pltpu.VMEM((HALF * LEVELS * ROWS, BLOCK), f32)],
        compiler_params=pltpu.CompilerParams(vmem_limit_bytes=VMEM_BYTES),
        cost_estimate=pl.CostEstimate(flops=3_000_000_000, bytes_accessed=1_000_000, transcendentals=0),
        name="fourier_own" if own else "fourier_other",
    )(pieces, jnp.asarray(inner), jnp.asarray(twiddle), jnp.asarray(outer))


def finish_kernel(own_ref, *refs):
    ours, theirs, out_ref = refs[:N_BAND - 1], refs[N_BAND - 1:-1], refs[-1]
    band = lax.axis_index("band")
    for shift in range(N_BAND):
        first = lax.rem(band + N_BAND - shift, N_BAND) * ROWS
        for i in range(LEVELS):
            for r in range(ROWS):
                near = own_ref[0, i, r] if shift == 0 else ours[shift - 1][i, r]
                piece = near.astype(f32) + theirs[shift][i, r].astype(f32)
                for t in range(4):
                    out_ref[i, first + r, :, t * BLOCK:(t + 1) * BLOCK] = piece[2 * t:2 * t + 2]


def finish(own, ours, theirs):
    vmem = pl.BlockSpec(memory_space=pltpu.VMEM)
    return pl.pallas_call(
        finish_kernel,
        out_shape=jax.ShapeDtypeStruct((LEVELS, N_BAND * ROWS, 2, WAVES // N_BAND), f32),
        in_specs=[vmem] * (2 * N_BAND),
        out_specs=vmem,
        compiler_params=pltpu.CompilerParams(vmem_limit_bytes=VMEM_BYTES),
        name="finish",
    )(own, *ours, *theirs)


def along_z(piece, flip, shift):
    pairs = []
    for band in range(N_BAND):
        for half in range(2):
            pairs.append((band * 2 + half, (band + shift) % N_BAND * 2 + (half ^ flip)))
    return lax.ppermute(piece, ("band", "zhi"), pairs)


def shards(fields, inverse, block_costs, row_length):
    updated = relax(fields, inverse, block_costs, row_length)
    half_rows = lax.all_to_all(updated, ("y", "x", "core"), split_axis=0, concat_axis=0, tiled=True)
    other = fourier(half_rows, False)
    theirs = [along_z(other[shift], 1, shift) for shift in range(N_BAND)]
    own = fourier(half_rows, True)
    ours = [along_z(own[shift], 0, shift) for shift in range(1, N_BAND)]
    return finish(own, ours, theirs)


def solution(mesh):
    fine = Mesh(mesh.devices.reshape(N_BAND, 2, 4, 4, 2), ("band",) + COL_AXES)
    return jax.shard_map(
        shards,
        mesh=fine,
        in_specs=(P(None, None, "band", COL_AXES), P(), P(COL_AXES, "band"), P("band")),
        out_specs=P(COL_AXES, None, None, "band"),
        check_vma=False,
    )
```

time: 64.1 us -> 59.2 us (0.924); the launches traced: 63.1 us -> 59 us
  blocking collectives: 52.2 us -> 23.3 us
  starting transfers between devices: 0 us -> 14.4 us
  waiting for transfers between devices: 0 us -> 9.76 us
    all_to_all x2 -> x1, blocking collectives: 52.2 us -> 23.3 us  [shards(): lax.all_to_all(updated, ('y', 'x', 'core'), split_axis=0, concat_axis=0,...]
    ppermute x0 -> x7, starting transfers between devices: none -> 14.4 us  [along_z(): return lax.ppermute(piece, ('band', 'zhi'), pairs)]
    ppermute x0 -> x7, waiting for transfers between devices: none -> 9.76 us  [along_z(): return lax.ppermute(piece, ('band', 'zhi'), pairs)]
    pallas_call x2 -> x3, Pallas kernels: 6.54 us -> 7.01 us  [the longest x2 5.21 us: fourier(): pl.pallas_call(functools.partial(fourier_kernel, own), out_shape=jax.Shap...]
  transfers between devices with their start and end apart: 0 -> 7, of which waited for: 0 -> 4; matrix products, arithmetic and copies ran while one was open for 0% -> 0% of each run, Pallas kernels for 0% -> 4%
where the time goes in v3:
time: 59.2 us; the launch traced here: 59 us
  blocking collectives  23.3 us (39%)
  starting transfers between devices  14.4 us (24%)
  waiting for transfers between devices  9.76 us (16%)
  Pallas kernels  8.04 us (14%)
  local copies, waits for them, and re-layouts  3.35 us (6%)
    all_to_all x1, blocking collectives, shards(): lax.all_to_all(updated, ('y', 'x', 'core'), split_axis=0, concat_axis=0,...  23.3 us
    ppermute x7, starting transfers between devices, along_z(): return lax.ppermute(piece, ('band', 'zhi'), pairs)  14.4 us
    ppermute x7, waiting for transfers between devices, along_z(): return lax.ppermute(piece, ('band', 'zhi'), pairs)  9.76 us
    pallas_call x2, Pallas kernels, fourier(): pl.pallas_call(functools.partial(fourier_kernel, own), out_shape=jax.Shap...  5.21 us
    unnamed x14, local copies, waits for them, and re-layouts  3.3 us
    pallas_call x1, Pallas kernels, relax(): pl.pallas_call(relax_kernel, out_shape=jax.ShapeDtypeStruct((HALF, 2, LEV...  1.8 us
  transfers between devices with their start and end apart: 7, of which 4 were waited for; matrix products, arithmetic and copies ran while one was open for 0% of the time, Pallas kernels for 4%

profile of v3, /device:TPU:1, one launch (start us, length us, event | category | flops | bytes accessed | tf_op | source)
XLA Modules:
  0.0 59.0 jit_solution(2823175069921188331)
XLA Ops:
  0.0 0.0 copy-start
  0.0 1.1 %copy-done = bf16[4,80,8,128]{3,2,1,0:T(8,128)(2,1)S(1)} copy-done((bf16[4,80,8,128]{3,2,1,0:T(8,128)(2,1)S(1)}, bf16[4,80,8,128]{3,2,1,0:T(8,128)(2,1)}, u32[]{:S(2)}) %copy-start) | copy-done | bytes 655384
  1.1 0.0 copy-start.1
  1.1 0.9 %copy-done.1 = bf16[4,80,80]{2,1,0:T(8,128)(2,1)S(1)} copy-done((bf16[4,80,80]{2,1,0:T(8,128)(2,1)S(1)}, bf16[4,80,80]{2,1,0:T(8,128)(2,1)}, u32[]{:S(2)}) %copy-start.1) | copy-done | bytes 51224
  2.0 0.0 copy-start.2
  2.0 0.7 %copy-done.2 = s32[1,8]{1,0:T(1,128)S(1)} copy-done((s32[1,8]{1,0:T(1,128)S(1)}, s32[1,8]{1,0:T(1,128)}, u32[]{:S(2)}) %copy-start.2) | copy-done | bytes 56
  2.6 0.0 copy-start.3
  2.6 0.7 %copy-done.3 = s32[8]{0:T(128)S(1)} copy-done((s32[8]{0:T(128)S(1)}, s32[8]{0:T(128)}, u32[]{:S(2)}) %copy-start.3) | copy-done | bytes 56
  3.3 1.8 %relax.1 = bf16[32,2,5,8,128]{4,3,2,1,0:T(8,128)(2,1)S(1)} custom-call(s32[1,8]{1,0:T(1,128)S(1)} %copy-done.2, s32[8]{0:T(128)S(1)} %copy-done.3, bf16[4,80,8,128]{3,2,1,0:T(8,128)(2,1)S(1)} %copy-done, bf16[4,80,80]{2,1,0:T(8,128)(2,1)S(1)} %copy-done.1), custom_call_target="tpu_custom_call" | custom-call | tf_op jit(solution)/shard_map/relax/pallas_call | solution.py:97
  5.1 0.0 copy-start.4
  5.1 0.0 copy-start.5
  5.1 0.0 copy-start.6
  5.1 23.3 %all_to_all.5.x_ref = bf16[32,2,5,8,128]{4,3,2,1,0:T(8,128)(2,1)S(1)} all-to-all(bf16[32,2,5,8,128]{4,3,2,1,0:T(8,128)(2,1)S(1)} %relax.1), channel_id=1, replica_groups=mesh['band'=4,'zhi'=2,'y'=4,'x'=4,'core'=2] {'y','x','core'}, dimensions={0} | all-to-all | bytes 1310720 | tf_op jit(solution)/shard_map/all_to_all | solution.py:198
  28.5 0.0 copy-done.4
  28.5 0.0 copy-done.5
  28.5 0.0 copy-done.6
  28.5 2.6 %fourier_other.1 = bf16[4,5,8,8,128]{4,3,2,1,0:T(8,128)(2,1)S(1)} custom-call(bf16[32,2,5,8,128]{4,3,2,1,0:T(8,128)(2,1)S(1)} %all_to_all.5.x_ref, bf16[2,128,64]{2,1,0:T(8,128)(2,1)S(1)} %copy-done.6, f32[2,64,128]{2,1,0:T(8,128)S(1)} %copy-done.5, bf16[2,128,128]{2,1,0:T(8,128)(2,1)S(1)} %copy-done.4), custom_call_target="tpu_custom_call" | custom-call | flops 3000000000 | bytes 1000000 | tf_op jit(solution)/shard_map/fourier_other/pallas_call | solution.py:151
  31.1 5.9 %collective-permute-start.6 = (bf16[5,8,8,128]{3,2,1,0:T(8,128)(2,1)S(1)}, bf16[5,8,8,128]{3,2,1,0:T(8,128)(2,1)S(1)}, u32[]{:S(2)}, u32[]{:S(2)}) collective-permute-start(bf16[5,8,8,128]{3,2,1,0:T(8,128)(2,1)S(1)} %get-tuple-element.5), channel_id=1, source_target_pairs={{0,224},{32,192},{64,32},{96,0},{128,96},{160,64},{192,160},{224,1... | collective-permute-start | bytes 245768 | tf_op jit(solution)/shard_map/ppermute | solution.py:193
  37.1 0.1 collective-permute-start.5
  37.2 4.4 %collective-permute-start.4 = (bf16[5,8,8,128]{3,2,1,0:T(8,128)(2,1)S(1)}, bf16[5,8,8,128]{3,2,1,0:T(8,128)(2,1)S(1)}, u32[]{:S(2)}, u32[]{:S(2)}) collective-permute-start(bf16[5,8,8,128]{3,2,1,0:T(8,128)(2,1)S(1)} %get-tuple-element.7), channel_id=1, source_target_pairs={{0,96},{32,64},{64,160},{96,128},{128,224},{160,192},{192,32},{224... | collective-permute-start | bytes 245768 | tf_op jit(solution)/shard_map/ppermute | solution.py:193
  41.5 1.0 %collective-permute-start.3 = (bf16[5,8,8,128]{3,2,1,0:T(8,128)(2,1)S(1)}, bf16[5,8,8,128]{3,2,1,0:T(8,128)(2,1)S(1)}, u32[]{:S(2)}, u32[]{:S(2)}) collective-permute-start(bf16[5,8,8,128]{3,2,1,0:T(8,128)(2,1)S(1)} %get-tuple-element.8), channel_id=1, source_target_pairs={{0,32},{32,0},{64,96},{96,64},{128,160},{160,128},{192,224},{224,1... | collective-permute-start | bytes 245768 | tf_op jit(solution)/shard_map/ppermute | solution.py:193
  42.6 2.6 %fourier_own.1.own_ref = bf16[4,5,8,8,128]{4,3,2,1,0:T(8,128)(2,1)S(1)} custom-call(bf16[32,2,5,8,128]{4,3,2,1,0:T(8,128)(2,1)S(1)} %all_to_all.5.x_ref, bf16[2,128,64]{2,1,0:T(8,128)(2,1)S(1)} %copy-done.6, f32[2,64,128]{2,1,0:T(8,128)S(1)} %copy-done.5, bf16[2,128,128]{2,1,0:T(8,128)(2,1)S(1)} %copy-done.4), custom_call_target="tpu_custom_call" | custom-call | flops 3000000000 | bytes 1000000 | tf_op jit(solution)/shard_map/fourier_own/pallas_call | solution.py:151
  45.2 1.3 %collective-permute-start.2 = (bf16[5,8,8,128]{3,2,1,0:T(8,128)(2,1)S(1)}, bf16[5,8,8,128]{3,2,1,0:T(8,128)(2,1)S(1)}, u32[]{:S(2)}, u32[]{:S(2)}) collective-permute-start(bf16[5,8,8,128]{3,2,1,0:T(8,128)(2,1)S(1)} %get-tuple-element.9), channel_id=1, source_target_pairs={{0,192},{32,224},{64,0},{96,32},{128,64},{160,96},{192,128},{224,1... | collective-permute-start | bytes 245768 | tf_op jit(solution)/shard_map/ppermute | solution.py:193
  46.5 0.0 collective-permute-done.6.refs_6_
  46.5 0.9 %collective-permute-start.1 = (bf16[5,8,8,128]{3,2,1,0:T(8,128)(2,1)S(1)}, bf16[5,8,8,128]{3,2,1,0:T(8,128)(2,1)S(1)}, u32[]{:S(2)}, u32[]{:S(2)}) collective-permute-start(bf16[5,8,8,128]{3,2,1,0:T(8,128)(2,1)S(1)} %get-tuple-element.10), channel_id=1, source_target_pairs={{0,128},{32,160},{64,192},{96,224},{128,0},{160,32},{192,64},{224,... | collective-permute-start | bytes 245768 | tf_op jit(solution)/shard_map/ppermute | solution.py:193
  47.3 0.0 collective-permute-done.5.refs_5_
  47.3 0.9 %collective-permute-start = (bf16[5,8,8,128]{3,2,1,0:T(8,128)(2,1)S(1)}, bf16[5,8,8,128]{3,2,1,0:T(8,128)(2,1)S(1)}, u32[]{:S(2)}, u32[]{:S(2)}) collective-permute-start(bf16[5,8,8,128]{3,2,1,0:T(8,128)(2,1)S(1)} %get-tuple-element.11), channel_id=1, source_target_pairs={{0,64},{32,96},{64,128},{96,160},{128,192},{160,224},{192,0},{224,... | collective-permute-start | bytes 245768 | tf_op jit(solution)/shard_map/ppermute | solution.py:193
  48.2 2.8 %collective-permute-done.4.refs_4_ = bf16[5,8,8,128]{3,2,1,0:T(8,128)(2,1)S(1)} collective-permute-done((bf16[5,8,8,128]{3,2,1,0:T(8,128)(2,1)S(1)}, bf16[5,8,8,128]{3,2,1,0:T(8,128)(2,1)S(1)}, u32[]{:S(2)}, u32[]{:S(2)}) %collective-permute-start.4) | collective-permute-done | bytes 81952 | tf_op jit(solution)/shard_map/ppermute | solution.py:193
  51.0 2.4 %collective-permute-done.3.refs_3_ = bf16[5,8,8,128]{3,2,1,0:T(8,128)(2,1)S(1)} collective-permute-done((bf16[5,8,8,128]{3,2,1,0:T(8,128)(2,1)S(1)}, bf16[5,8,8,128]{3,2,1,0:T(8,128)(2,1)S(1)}, u32[]{:S(2)}, u32[]{:S(2)}) %collective-permute-start.3) | collective-permute-done | bytes 81952 | tf_op jit(solution)/shard_map/ppermute | solution.py:193
  53.4 0.0 collective-permute-done.2.refs_2_
  53.4 0.1 collective-permute-done.1.refs_1_
  53.5 4.5 %collective-permute-done.refs_0_ = bf16[5,8,8,128]{3,2,1,0:T(8,128)(2,1)S(1)} collective-permute-done((bf16[5,8,8,128]{3,2,1,0:T(8,128)(2,1)S(1)}, bf16[5,8,8,128]{3,2,1,0:T(8,128)(2,1)S(1)}, u32[]{:S(2)}, u32[]{:S(2)}) %collective-permute-start) | collective-permute-done | bytes 81952 | tf_op jit(solution)/shard_map/ppermute | solution.py:193
  58.0 1.0 %finish.1 = f32[5,32,2,512]{3,2,1,0:T(2,128)} custom-call(bf16[4,5,8,8,128]{4,3,2,1,0:T(8,128)(2,1)S(1)} %fourier_own.1.own_ref, bf16[5,8,8,128]{3,2,1,0:T(8,128)(2,1)S(1)} %collective-permute-done.refs_0_, bf16[5,8,8,128]{3,2,1,0:T(8,128)(2,1)S(1)} %collective-permute-done.1.refs_1_, bf16[5,8,8,128]{3,2,1,0:T(8,128)(2,1)S(1)} %collective-permute-done.2.refs_2_, ...), custom_call_target="tpu_custom_call" | custom-call | tf_op jit(solution)/shard_map/finish/pallas_call | solution.py:178
  (2 shorter events, 0.0 us)
Async XLA Ops:
  0.0 1.1 %copy-start = (bf16[4,80,8,128]{3,2,1,0:T(8,128)(2,1)S(1)}, bf16[4,80,8,128]{3,2,1,0:T(8,128)(2,1)}, u32[]{:S(2)}) copy-start(bf16[4,80,8,128]{3,2,1,0:T(8,128)(2,1)} %fields_ref.1) | copy-start | bytes 1966084
  1.1 0.9 %copy-start.1 = (bf16[4,80,80]{2,1,0:T(8,128)(2,1)S(1)}, bf16[4,80,80]{2,1,0:T(8,128)(2,1)}, u32[]{:S(2)}) copy-start(bf16[4,80,80]{2,1,0:T(8,128)(2,1)} %inverse_ref.1) | copy-start | bytes 153604
  2.0 0.7 %copy-start.2 = (s32[1,8]{1,0:T(1,128)S(1)}, s32[1,8]{1,0:T(1,128)}, u32[]{:S(2)}) copy-start(s32[1,8]{1,0:T(1,128)} %cost_ref.1) | copy-start | bytes 100
  2.6 0.7 %copy-start.3 = (s32[8]{0:T(128)S(1)}, s32[8]{0:T(128)}, u32[]{:S(2)}) copy-start(s32[8]{0:T(128)} %length_ref.1) | copy-start | bytes 100
  5.1 23.4 %copy-start.4 = (bf16[2,128,128]{2,1,0:T(8,128)(2,1)S(1)}, bf16[2,128,128]{2,1,0:T(8,128)(2,1)}, u32[]{:S(2)}) copy-start(bf16[2,128,128]{2,1,0:T(8,128)(2,1)} %constant.8.clone.outer_ref) | copy-start | bytes 196612
  5.1 23.4 %copy-start.5 = (f32[2,64,128]{2,1,0:T(8,128)S(1)}, f32[2,64,128]{2,1,0:T(8,128)}, u32[]{:S(2)}) copy-start(f32[2,64,128]{2,1,0:T(8,128)} %constant.7.clone.twiddle_ref) | copy-start | bytes 196612
  5.1 23.4 %copy-start.6 = (bf16[2,128,64]{2,1,0:T(8,128)(2,1)S(1)}, bf16[2,128,64]{2,1,0:T(8,128)(2,1)}, u32[]{:S(2)}) copy-start(bf16[2,128,64]{2,1,0:T(8,128)(2,1)} %constant.6.clone.inner_ref) | copy-start | bytes 98308
  31.1 15.3 %collective-permute-start.6 = (bf16[5,8,8,128]{3,2,1,0:T(8,128)(2,1)S(1)}, bf16[5,8,8,128]{3,2,1,0:T(8,128)(2,1)S(1)}, u32[]{:S(2)}, u32[]{:S(2)}) collective-permute-start(bf16[5,8,8,128]{3,2,1,0:T(8,128)(2,1)S(1)} %get-tuple-element.5), channel_id=1, source_target_pairs={{0,224},{32,192},{64,32},{96,0},{128,96},{160,64},{192,160},{224,1... | collective-permute-start | bytes 245768 | tf_op jit(solution)/shard_map/ppermute | solution.py:193
  37.1 10.3 %collective-permute-start.5 = (bf16[5,8,8,128]{3,2,1,0:T(8,128)(2,1)S(1)}, bf16[5,8,8,128]{3,2,1,0:T(8,128)(2,1)S(1)}, u32[]{:S(2)}, u32[]{:S(2)}) collective-permute-start(bf16[5,8,8,128]{3,2,1,0:T(8,128)(2,1)S(1)} %get-tuple-element.6), channel_id=1, source_target_pairs={{0,160},{32,128},{64,224},{96,192},{128,32},{160,0},{192,96},{224,... | collective-permute-start | bytes 245768 | tf_op jit(solution)/shard_map/ppermute | solution.py:193
  37.2 13.9 %collective-permute-start.4 = (bf16[5,8,8,128]{3,2,1,0:T(8,128)(2,1)S(1)}, bf16[5,8,8,128]{3,2,1,0:T(8,128)(2,1)S(1)}, u32[]{:S(2)}, u32[]{:S(2)}) collective-permute-start(bf16[5,8,8,128]{3,2,1,0:T(8,128)(2,1)S(1)} %get-tuple-element.7), channel_id=1, source_target_pairs={{0,96},{32,64},{64,160},{96,128},{128,224},{160,192},{192,32},{224... | collective-permute-start | bytes 245768 | tf_op jit(solution)/shard_map/ppermute | solution.py:193
  41.5 11.9 %collective-permute-start.3 = (bf16[5,8,8,128]{3,2,1,0:T(8,128)(2,1)S(1)}, bf16[5,8,8,128]{3,2,1,0:T(8,128)(2,1)S(1)}, u32[]{:S(2)}, u32[]{:S(2)}) collective-permute-start(bf16[5,8,8,128]{3,2,1,0:T(8,128)(2,1)S(1)} %get-tuple-element.8), channel_id=1, source_target_pairs={{0,32},{32,0},{64,96},{96,64},{128,160},{160,128},{192,224},{224,1... | collective-permute-start | bytes 245768 | tf_op jit(solution)/shard_map/ppermute | solution.py:193
  45.2 8.2 %collective-permute-start.2 = (bf16[5,8,8,128]{3,2,1,0:T(8,128)(2,1)S(1)}, bf16[5,8,8,128]{3,2,1,0:T(8,128)(2,1)S(1)}, u32[]{:S(2)}, u32[]{:S(2)}) collective-permute-start(bf16[5,8,8,128]{3,2,1,0:T(8,128)(2,1)S(1)} %get-tuple-element.9), channel_id=1, source_target_pairs={{0,192},{32,224},{64,0},{96,32},{128,64},{160,96},{192,128},{224,1... | collective-permute-start | bytes 245768 | tf_op jit(solution)/shard_map/ppermute | solution.py:193
  46.5 7.0 %collective-permute-start.1 = (bf16[5,8,8,128]{3,2,1,0:T(8,128)(2,1)S(1)}, bf16[5,8,8,128]{3,2,1,0:T(8,128)(2,1)S(1)}, u32[]{:S(2)}, u32[]{:S(2)}) collective-permute-start(bf16[5,8,8,128]{3,2,1,0:T(8,128)(2,1)S(1)} %get-tuple-element.10), channel_id=1, source_target_pairs={{0,128},{32,160},{64,192},{96,224},{128,0},{160,32},{192,64},{224,... | collective-permute-start | bytes 245768 | tf_op jit(solution)/shard_map/ppermute | solution.py:193
  47.3 10.6 %collective-permute-start = (bf16[5,8,8,128]{3,2,1,0:T(8,128)(2,1)S(1)}, bf16[5,8,8,128]{3,2,1,0:T(8,128)(2,1)S(1)}, u32[]{:S(2)}, u32[]{:S(2)}) collective-permute-start(bf16[5,8,8,128]{3,2,1,0:T(8,128)(2,1)S(1)} %get-tuple-element.11), channel_id=1, source_target_pairs={{0,64},{32,96},{64,128},{96,160},{128,192},{160,224},{192,0},{224,... | collective-permute-start | bytes 245768 | tf_op jit(solution)/shard_map/ppermute | solution.py:193

commit v4 on v3

--- a/solution.py
+++ b/solution.py
@@ -12,6 +12,7 @@
 f32 = jnp.float32
 bf16 = jnp.bfloat16
 VMEM_BYTES = 40 * 1024 * 1024
+RELAX_BYTES = 61 * 1024 * 1024
 
 FIELDS = 4
 LEV = 80
@@ -54,13 +55,28 @@
     return inner, twiddle, outer
 
 
-def relax_kernel(cost_ref, length_ref, fields_ref, inverse_ref, out_ref, flat, state):
+def relax_kernel(
+    cost_hbm, length_hbm, fields_hbm, inverse_hbm, out_hbm,
+    cost_ref, length_ref, fields_ref, inverse_ref, flat, state, start, out_ref, sems, out_sems,
+):
+    copies = [pltpu.make_async_copy(fields_hbm.at[f], fields_ref.at[f], sems.at[f]) for f in range(FIELDS)]
+    small = [
+        pltpu.make_async_copy(inverse_hbm, inverse_ref, sems.at[FIELDS]),
+        pltpu.make_async_copy(cost_hbm, cost_ref, sems.at[FIELDS + 1]),
+        pltpu.make_async_copy(length_hbm, length_ref, sems.at[FIELDS + 2]),
+    ]
+    for copy in copies + small:
+        copy.start()
     first = lax.axis_index(COL_AXES) * BLOCK
-    flat[...] = fields_ref[...].astype(f32).reshape(FIELDS * LEV * ROWS, BLOCK)
     for f in range(FIELDS):
+        copies[f].wait()
+        flat[f * LEV * ROWS:(f + 1) * LEV * ROWS, :] = fields_ref[f].astype(f32).reshape(LEV * ROWS, BLOCK)
         for r in range(ROWS):
-            piece = flat[pl.ds(f * LEV * ROWS + r, LEV, stride=ROWS), :]
-            state[f, :, r * BLOCK:(r + 1) * BLOCK] = piece.astype(bf16)
+            piece = flat[pl.ds(f * LEV * ROWS + r, LEV, stride=ROWS), :].astype(bf16)
+            state[f, :, r * BLOCK:(r + 1) * BLOCK] = piece
+            start[f, :, r * BLOCK:(r + 1) * BLOCK] = piece
+    for copy in small:
+        copy.wait()
     costs = [cost_ref[0, r] for r in range(ROWS)]
     most = costs[0]
     for r in range(1, ROWS):
@@ -76,34 +92,44 @@
             state[f] = jnp.where(active, new, now.astype(f32)).astype(bf16)
 
     lane = first + lax.broadcasted_iota(jnp.int32, (1, BLOCK), 1)
-    for r in range(ROWS):
-        keep = lane < length_ref[r]
-        for f in range(FIELDS):
-            rows = pl.ds(f * LEV * ROWS + r, LEV, stride=ROWS)
-            initial = flat[rows, :]
-            relaxed = state[f, :, r * BLOCK:(r + 1) * BLOCK].astype(f32)
+    keep = [lane < length_ref[r] for r in range(ROWS)]
+    sends = []
+    for f in range(FIELDS):
+        for r in range(ROWS):
+            lanes = slice(r * BLOCK, (r + 1) * BLOCK)
+            initial = start[f, :, lanes].astype(f32)
+            relaxed = state[f, :, lanes].astype(f32)
             tendency = (relaxed - initial).astype(bf16).astype(f32)
             updated = (initial + tendency).astype(bf16).astype(f32)
-            flat[rows, :] = jnp.where(keep, updated, 0.0)
-    span = HALF * LEVELS
-    for h in range(2):
-        piece = flat[h * span * ROWS:(h + 1) * span * ROWS, :].reshape(HALF, LEVELS, ROWS, BLOCK)
-        out_ref[:, h] = piece.astype(bf16)
+            flat[pl.ds(f * LEV * ROWS + r, LEV, stride=ROWS), :] = jnp.where(keep[r], updated, 0.0)
+        piece = flat[f * LEV * ROWS:(f + 1) * LEV * ROWS, :].reshape(LEV // LEVELS, LEVELS, ROWS, BLOCK)
+        out_ref[f] = piece.astype(bf16)
+        first = f % 2 * (LEV // LEVELS)
+        sends.append(pltpu.make_async_copy(out_ref.at[f], out_hbm.at[pl.ds(first, LEV // LEVELS), f // 2], out_sems.at[f]))
+        sends[-1].start()
+    for send in sends:
+        send.wait()
 
 
 def relax(fields, inverse, costs, lengths):
-    vmem = pl.BlockSpec(memory_space=pltpu.VMEM)
-    smem = pl.BlockSpec(memory_space=pltpu.SMEM)
     return pl.pallas_call(
         relax_kernel,
         out_shape=jax.ShapeDtypeStruct((HALF, 2, LEVELS, ROWS, BLOCK), bf16),
-        in_specs=[smem, smem, vmem, vmem],
-        out_specs=vmem,
+        in_specs=[pl.BlockSpec(memory_space=pltpu.HBM)] * 4,
+        out_specs=pl.BlockSpec(memory_space=pltpu.HBM),
         scratch_shapes=[
+            pltpu.SMEM((1, ROWS), jnp.int32),
+            pltpu.SMEM((ROWS,), jnp.int32),
+            pltpu.VMEM((FIELDS, LEV, ROWS, BLOCK), bf16),
+            pltpu.VMEM((FIELDS, LEV, LEV), bf16),
             pltpu.VMEM((FIELDS * LEV * ROWS, BLOCK), f32),
             pltpu.VMEM((FIELDS, LEV, ROWS * BLOCK), bf16),
+            pltpu.VMEM((FIELDS, LEV, ROWS * BLOCK), bf16),
+            pltpu.VMEM((FIELDS, LEV // LEVELS, LEVELS, ROWS, BLOCK), bf16),
+            pltpu.SemaphoreType.DMA((FIELDS + 3,)),
+            pltpu.SemaphoreType.DMA((FIELDS,)),
         ],
-        compiler_params=pltpu.CompilerParams(vmem_limit_bytes=VMEM_BYTES),
+        compiler_params=pltpu.CompilerParams(vmem_limit_bytes=RELAX_BYTES),
         name="relax",
     )(costs, lengths, fields, inverse)
 
@@ -161,8 +187,10 @@
 
 
 def finish_kernel(own_ref, *refs):
-    ours, theirs, out_ref = refs[:N_BAND - 1], refs[N_BAND - 1:-1], refs[-1]
+    ours, theirs = refs[:N_BAND - 1], refs[N_BAND - 1:2 * N_BAND - 1]
+    out_hbm, buffer, sems = refs[2 * N_BAND - 1:]
     band = lax.axis_index("band")
+    copies = []
     for shift in range(N_BAND):
         first = lax.rem(band + N_BAND - shift, N_BAND) * ROWS
         for i in range(LEVELS):
@@ -170,7 +198,11 @@
                 near = own_ref[0, i, r] if shift == 0 else ours[shift - 1][i, r]
                 piece = near.astype(f32) + theirs[shift][i, r].astype(f32)
                 for t in range(4):
-                    out_ref[i, first + r, :, t * BLOCK:(t + 1) * BLOCK] = piece[2 * t:2 * t + 2]
+                    buffer[shift, i, r, :, t * BLOCK:(t + 1) * BLOCK] = piece[2 * t:2 * t + 2]
+        copies.append(pltpu.make_async_copy(buffer.at[shift], out_hbm.at[:, pl.ds(first, ROWS)], sems.at[shift]))
+        copies[-1].start()
+    for copy in copies:
+        copy.wait()
 
 
 def finish(own, ours, theirs):
@@ -179,7 +211,11 @@
         finish_kernel,
         out_shape=jax.ShapeDtypeStruct((LEVELS, N_BAND * ROWS, 2, WAVES // N_BAND), f32),
         in_specs=[vmem] * (2 * N_BAND),
-        out_specs=vmem,
+        out_specs=pl.BlockSpec(memory_space=pltpu.HBM),
+        scratch_shapes=[
+            pltpu.VMEM((N_BAND, LEVELS, ROWS, 2, WAVES // N_BAND), f32),
+            pltpu.SemaphoreType.DMA((N_BAND,)),
+        ],
         compiler_params=pltpu.CompilerParams(vmem_limit_bytes=VMEM_BYTES),
         name="finish",
     )(own, *ours, *theirs)

time: 59.2 us -> 57.3 us (0.968)
  local copies, waits for them, and re-layouts: 3.35 us -> 0.06 us
  Pallas kernels: 8.04 us -> 9.14 us
  starting transfers between devices: 14.4 us -> 15.4 us
    unnamed x14 -> x6, local copies, waits for them, and re-layouts: 3.3 us -> 0.02 us
    pallas_call x1, Pallas kernels: 1.8 us -> 3.01 us  [relax(): pl.pallas_call(relax_kernel, out_shape=jax.ShapeDtypeStruct((HALF, 2, LEV...]
    ppermute x7, starting transfers between devices: 14.4 us -> 15.4 us  [along_z(): return lax.ppermute(piece, ('band', 'zhi'), pairs)]
  transfers between devices with their start and end apart: 7 -> 7, of which waited for: 4 -> 4; matrix products, arithmetic and copies ran while one was open for 0% -> 0% of each run, Pallas kernels for 4% -> 5%
where the time goes in v4:
time: 57.3 us; the launch traced here: 57.1 us
  blocking collectives  22.8 us (40%)
  starting transfers between devices  15.4 us (27%)
  waiting for transfers between devices  9.67 us (17%)
  Pallas kernels  9.14 us (16%)
    all_to_all x1, blocking collectives, shards(): lax.all_to_all(updated, ('y', 'x', 'core'), split_axis=0, concat_axis=0,...  22.8 us
    ppermute x7, starting transfers between devices, along_z(): return lax.ppermute(piece, ('band', 'zhi'), pairs)  15.4 us
    ppermute x7, waiting for transfers between devices, along_z(): return lax.ppermute(piece, ('band', 'zhi'), pairs)  9.67 us
    pallas_call x2, Pallas kernels, fourier(): pl.pallas_call(functools.partial(fourier_kernel, own), out_shape=jax.Shap...  5.22 us
    pallas_call x1, Pallas kernels, relax(): pl.pallas_call(relax_kernel, out_shape=jax.ShapeDtypeStruct((HALF, 2, LEV...  3.01 us
  transfers between devices with their start and end apart: 7, of which 4 were waited for; matrix products, arithmetic and copies ran while one was open for 0% of the time, Pallas kernels for 5%

profile of v4, /device:TPU:1, one launch (start us, length us, event | category | flops | bytes accessed | tf_op | source)
XLA Modules:
  0.0 57.1 jit_solution(1149036402006412729)
XLA Ops:
  0.0 3.0 %relax.1 = bf16[32,2,5,8,128]{4,3,2,1,0:T(8,128)(2,1)} custom-call(s32[1,8]{1,0:T(1,128)} %cost_hbm.1, s32[8]{0:T(128)} %length_hbm.1, bf16[4,80,8,128]{3,2,1,0:T(8,128)(2,1)} %fields_hbm.1, bf16[4,80,80]{2,1,0:T(8,128)(2,1)} %inverse_hbm.1), custom_call_target="tpu_custom_call" | custom-call | tf_op jit(solution)/shard_map/relax/pallas_call | solution.py:115
  3.0 0.0 copy-start
  3.0 0.0 copy-start.1
  3.0 0.0 copy-start.2
  3.1 22.8 %all_to_all.5.x_ref = bf16[32,2,5,8,128]{4,3,2,1,0:T(8,128)(2,1)S(1)} all-to-all(bf16[32,2,5,8,128]{4,3,2,1,0:T(8,128)(2,1)} %relax.1), channel_id=1, replica_groups=mesh['band'=4,'zhi'=2,'y'=4,'x'=4,'core'=2] {'y','x','core'}, dimensions={0} | all-to-all | bytes 1310720 | tf_op jit(solution)/shard_map/all_to_all | solution.py:234
  25.8 0.0 copy-done
  25.8 0.0 copy-done.1
  25.8 0.0 copy-done.2
  25.8 2.6 %fourier_other.1 = bf16[4,5,8,8,128]{4,3,2,1,0:T(8,128)(2,1)S(1)} custom-call(bf16[32,2,5,8,128]{4,3,2,1,0:T(8,128)(2,1)S(1)} %all_to_all.5.x_ref, bf16[2,128,64]{2,1,0:T(8,128)(2,1)S(1)} %copy-done.2, f32[2,64,128]{2,1,0:T(8,128)S(1)} %copy-done.1, bf16[2,128,128]{2,1,0:T(8,128)(2,1)S(1)} %copy-done), custom_call_target="tpu_custom_call" | custom-call | flops 3000000000 | bytes 1000000 | tf_op jit(solution)/shard_map/fourier_other/pallas_call | solution.py:177
  28.5 6.2 %collective-permute-start.6 = (bf16[5,8,8,128]{3,2,1,0:T(8,128)(2,1)S(1)}, bf16[5,8,8,128]{3,2,1,0:T(8,128)(2,1)S(1)}, u32[]{:S(2)}, u32[]{:S(2)}) collective-permute-start(bf16[5,8,8,128]{3,2,1,0:T(8,128)(2,1)S(1)} %get-tuple-element.5), channel_id=1, source_target_pairs={{0,224},{32,192},{64,32},{96,0},{128,96},{160,64},{192,160},{224,1... | collective-permute-start | bytes 245768 | tf_op jit(solution)/shard_map/ppermute | solution.py:229
  34.7 0.9 %collective-permute-start.5 = (bf16[5,8,8,128]{3,2,1,0:T(8,128)(2,1)S(1)}, bf16[5,8,8,128]{3,2,1,0:T(8,128)(2,1)S(1)}, u32[]{:S(2)}, u32[]{:S(2)}) collective-permute-start(bf16[5,8,8,128]{3,2,1,0:T(8,128)(2,1)S(1)} %get-tuple-element.6), channel_id=1, source_target_pairs={{0,160},{32,128},{64,224},{96,192},{128,32},{160,0},{192,96},{224,... | collective-permute-start | bytes 245768 | tf_op jit(solution)/shard_map/ppermute | solution.py:229
  35.6 4.4 %collective-permute-start.4 = (bf16[5,8,8,128]{3,2,1,0:T(8,128)(2,1)S(1)}, bf16[5,8,8,128]{3,2,1,0:T(8,128)(2,1)S(1)}, u32[]{:S(2)}, u32[]{:S(2)}) collective-permute-start(bf16[5,8,8,128]{3,2,1,0:T(8,128)(2,1)S(1)} %get-tuple-element.7), channel_id=1, source_target_pairs={{0,96},{32,64},{64,160},{96,128},{128,224},{160,192},{192,32},{224... | collective-permute-start | bytes 245768 | tf_op jit(solution)/shard_map/ppermute | solution.py:229
  39.9 0.9 %collective-permute-start.3 = (bf16[5,8,8,128]{3,2,1,0:T(8,128)(2,1)S(1)}, bf16[5,8,8,128]{3,2,1,0:T(8,128)(2,1)S(1)}, u32[]{:S(2)}, u32[]{:S(2)}) collective-permute-start(bf16[5,8,8,128]{3,2,1,0:T(8,128)(2,1)S(1)} %get-tuple-element.8), channel_id=1, source_target_pairs={{0,32},{32,0},{64,96},{96,64},{128,160},{160,128},{192,224},{224,1... | collective-permute-start | bytes 245768 | tf_op jit(solution)/shard_map/ppermute | solution.py:229
  40.8 2.6 %fourier_own.1.own_ref = bf16[4,5,8,8,128]{4,3,2,1,0:T(8,128)(2,1)S(1)} custom-call(bf16[32,2,5,8,128]{4,3,2,1,0:T(8,128)(2,1)S(1)} %all_to_all.5.x_ref, bf16[2,128,64]{2,1,0:T(8,128)(2,1)S(1)} %copy-done.2, f32[2,64,128]{2,1,0:T(8,128)S(1)} %copy-done.1, bf16[2,128,128]{2,1,0:T(8,128)(2,1)S(1)} %copy-done), custom_call_target="tpu_custom_call" | custom-call | flops 3000000000 | bytes 1000000 | tf_op jit(solution)/shard_map/fourier_own/pallas_call | solution.py:177
  43.5 1.3 %collective-permute-start.2 = (bf16[5,8,8,128]{3,2,1,0:T(8,128)(2,1)S(1)}, bf16[5,8,8,128]{3,2,1,0:T(8,128)(2,1)S(1)}, u32[]{:S(2)}, u32[]{:S(2)}) collective-permute-start(bf16[5,8,8,128]{3,2,1,0:T(8,128)(2,1)S(1)} %get-tuple-element.9), channel_id=1, source_target_pairs={{0,192},{32,224},{64,0},{96,32},{128,64},{160,96},{192,128},{224,1... | collective-permute-start | bytes 245768 | tf_op jit(solution)/shard_map/ppermute | solution.py:229
  44.7 0.0 collective-permute-done.6.refs_6_
  44.7 0.7 %collective-permute-start.1 = (bf16[5,8,8,128]{3,2,1,0:T(8,128)(2,1)S(1)}, bf16[5,8,8,128]{3,2,1,0:T(8,128)(2,1)S(1)}, u32[]{:S(2)}, u32[]{:S(2)}) collective-permute-start(bf16[5,8,8,128]{3,2,1,0:T(8,128)(2,1)S(1)} %get-tuple-element.10), channel_id=1, source_target_pairs={{0,128},{32,160},{64,192},{96,224},{128,0},{160,32},{192,64},{224,... | collective-permute-start | bytes 245768 | tf_op jit(solution)/shard_map/ppermute | solution.py:229
  45.5 0.0 collective-permute-done.5.refs_5_
  45.5 1.0 %collective-permute-start = (bf16[5,8,8,128]{3,2,1,0:T(8,128)(2,1)S(1)}, bf16[5,8,8,128]{3,2,1,0:T(8,128)(2,1)S(1)}, u32[]{:S(2)}, u32[]{:S(2)}) collective-permute-start(bf16[5,8,8,128]{3,2,1,0:T(8,128)(2,1)S(1)} %get-tuple-element.11), channel_id=1, source_target_pairs={{0,64},{32,96},{64,128},{96,160},{128,192},{160,224},{192,0},{224,... | collective-permute-start | bytes 245768 | tf_op jit(solution)/shard_map/ppermute | solution.py:229
  46.5 1.8 %collective-permute-done.4.refs_4_ = bf16[5,8,8,128]{3,2,1,0:T(8,128)(2,1)S(1)} collective-permute-done((bf16[5,8,8,128]{3,2,1,0:T(8,128)(2,1)S(1)}, bf16[5,8,8,128]{3,2,1,0:T(8,128)(2,1)S(1)}, u32[]{:S(2)}, u32[]{:S(2)}) %collective-permute-start.4) | collective-permute-done | bytes 81952 | tf_op jit(solution)/shard_map/ppermute | solution.py:229
  48.3 3.3 %collective-permute-done.3.refs_3_ = bf16[5,8,8,128]{3,2,1,0:T(8,128)(2,1)S(1)} collective-permute-done((bf16[5,8,8,128]{3,2,1,0:T(8,128)(2,1)S(1)}, bf16[5,8,8,128]{3,2,1,0:T(8,128)(2,1)S(1)}, u32[]{:S(2)}, u32[]{:S(2)}) %collective-permute-start.3) | collective-permute-done | bytes 81952 | tf_op jit(solution)/shard_map/ppermute | solution.py:229
  51.6 0.0 collective-permute-done.2.refs_2_
  51.6 0.2 collective-permute-done.1.refs_1_
  51.8 4.4 %collective-permute-done.refs_0_ = bf16[5,8,8,128]{3,2,1,0:T(8,128)(2,1)S(1)} collective-permute-done((bf16[5,8,8,128]{3,2,1,0:T(8,128)(2,1)S(1)}, bf16[5,8,8,128]{3,2,1,0:T(8,128)(2,1)S(1)}, u32[]{:S(2)}, u32[]{:S(2)}) %collective-permute-start) | collective-permute-done | bytes 81952 | tf_op jit(solution)/shard_map/ppermute | solution.py:229
  56.2 0.9 %finish.1 = f32[5,32,2,512]{3,2,1,0:T(2,128)} custom-call(bf16[4,5,8,8,128]{4,3,2,1,0:T(8,128)(2,1)S(1)} %fourier_own.1.own_ref, bf16[5,8,8,128]{3,2,1,0:T(8,128)(2,1)S(1)} %collective-permute-done.refs_0_, bf16[5,8,8,128]{3,2,1,0:T(8,128)(2,1)S(1)} %collective-permute-done.1.refs_1_, bf16[5,8,8,128]{3,2,1,0:T(8,128)(2,1)S(1)} %collective-permute-done.2.refs_2_, ...), custom_call_target="tpu_custom_call" | custom-call | tf_op jit(solution)/shard_map/finish/pallas_call | solution.py:210
  (2 shorter events, 0.0 us)
Async XLA Ops:
  3.0 22.8 %copy-start = (bf16[2,128,128]{2,1,0:T(8,128)(2,1)S(1)}, bf16[2,128,128]{2,1,0:T(8,128)(2,1)}, u32[]{:S(2)}) copy-start(bf16[2,128,128]{2,1,0:T(8,128)(2,1)} %constant.8.clone.outer_ref) | copy-start | bytes 196612
  3.0 22.8 %copy-start.1 = (f32[2,64,128]{2,1,0:T(8,128)S(1)}, f32[2,64,128]{2,1,0:T(8,128)}, u32[]{:S(2)}) copy-start(f32[2,64,128]{2,1,0:T(8,128)} %constant.7.clone.twiddle_ref) | copy-start | bytes 196612
  3.0 22.8 %copy-start.2 = (bf16[2,128,64]{2,1,0:T(8,128)(2,1)S(1)}, bf16[2,128,64]{2,1,0:T(8,128)(2,1)}, u32[]{:S(2)}) copy-start(bf16[2,128,64]{2,1,0:T(8,128)(2,1)} %constant.6.clone.inner_ref) | copy-start | bytes 98308
  28.5 16.2 %collective-permute-start.6 = (bf16[5,8,8,128]{3,2,1,0:T(8,128)(2,1)S(1)}, bf16[5,8,8,128]{3,2,1,0:T(8,128)(2,1)S(1)}, u32[]{:S(2)}, u32[]{:S(2)}) collective-permute-start(bf16[5,8,8,128]{3,2,1,0:T(8,128)(2,1)S(1)} %get-tuple-element.5), channel_id=1, source_target_pairs={{0,224},{32,192},{64,32},{96,0},{128,96},{160,64},{192,160},{224,1... | collective-permute-start | bytes 245768 | tf_op jit(solution)/shard_map/ppermute | solution.py:229
  34.7 10.8 %collective-permute-start.5 = (bf16[5,8,8,128]{3,2,1,0:T(8,128)(2,1)S(1)}, bf16[5,8,8,128]{3,2,1,0:T(8,128)(2,1)S(1)}, u32[]{:S(2)}, u32[]{:S(2)}) collective-permute-start(bf16[5,8,8,128]{3,2,1,0:T(8,128)(2,1)S(1)} %get-tuple-element.6), channel_id=1, source_target_pairs={{0,160},{32,128},{64,224},{96,192},{128,32},{160,0},{192,96},{224,... | collective-permute-start | bytes 245768 | tf_op jit(solution)/shard_map/ppermute | solution.py:229
  35.6 12.7 %collective-permute-start.4 = (bf16[5,8,8,128]{3,2,1,0:T(8,128)(2,1)S(1)}, bf16[5,8,8,128]{3,2,1,0:T(8,128)(2,1)S(1)}, u32[]{:S(2)}, u32[]{:S(2)}) collective-permute-start(bf16[5,8,8,128]{3,2,1,0:T(8,128)(2,1)S(1)} %get-tuple-element.7), channel_id=1, source_target_pairs={{0,96},{32,64},{64,160},{96,128},{128,224},{160,192},{192,32},{224... | collective-permute-start | bytes 245768 | tf_op jit(solution)/shard_map/ppermute | solution.py:229
  39.9 11.7 %collective-permute-start.3 = (bf16[5,8,8,128]{3,2,1,0:T(8,128)(2,1)S(1)}, bf16[5,8,8,128]{3,2,1,0:T(8,128)(2,1)S(1)}, u32[]{:S(2)}, u32[]{:S(2)}) collective-permute-start(bf16[5,8,8,128]{3,2,1,0:T(8,128)(2,1)S(1)} %get-tuple-element.8), channel_id=1, source_target_pairs={{0,32},{32,0},{64,96},{96,64},{128,160},{160,128},{192,224},{224,1... | collective-permute-start | bytes 245768 | tf_op jit(solution)/shard_map/ppermute | solution.py:229
  43.5 8.1 %collective-permute-start.2 = (bf16[5,8,8,128]{3,2,1,0:T(8,128)(2,1)S(1)}, bf16[5,8,8,128]{3,2,1,0:T(8,128)(2,1)S(1)}, u32[]{:S(2)}, u32[]{:S(2)}) collective-permute-start(bf16[5,8,8,128]{3,2,1,0:T(8,128)(2,1)S(1)} %get-tuple-element.9), channel_id=1, source_target_pairs={{0,192},{32,224},{64,0},{96,32},{128,64},{160,96},{192,128},{224,1... | collective-permute-start | bytes 245768 | tf_op jit(solution)/shard_map/ppermute | solution.py:229
  44.7 7.0 %collective-permute-start.1 = (bf16[5,8,8,128]{3,2,1,0:T(8,128)(2,1)S(1)}, bf16[5,8,8,128]{3,2,1,0:T(8,128)(2,1)S(1)}, u32[]{:S(2)}, u32[]{:S(2)}) collective-permute-start(bf16[5,8,8,128]{3,2,1,0:T(8,128)(2,1)S(1)} %get-tuple-element.10), channel_id=1, source_target_pairs={{0,128},{32,160},{64,192},{96,224},{128,0},{160,32},{192,64},{224,... | collective-permute-start | bytes 245768 | tf_op jit(solution)/shard_map/ppermute | solution.py:229
  45.5 10.7 %collective-permute-start = (bf16[5,8,8,128]{3,2,1,0:T(8,128)(2,1)S(1)}, bf16[5,8,8,128]{3,2,1,0:T(8,128)(2,1)S(1)}, u32[]{:S(2)}, u32[]{:S(2)}) collective-permute-start(bf16[5,8,8,128]{3,2,1,0:T(8,128)(2,1)S(1)} %get-tuple-element.11), channel_id=1, source_target_pairs={{0,64},{32,96},{64,128},{96,160},{128,192},{160,224},{192,0},{224,... | collective-permute-start | bytes 245768 | tf_op jit(solution)/shard_map/ppermute | solution.py:229

commit v5 on v4

--- a/solution.py
+++ b/solution.py
@@ -1,4 +1,3 @@
-import functools
 import math
 
 import jax
@@ -25,6 +24,8 @@
 LEVELS = FIELDS * LEV // N_COL
 COL_AXES = ("zhi", "y", "x", "core")
 HALF = N_COL // 2
+PAIRS = N_COL // 4
+PAIR = 2 * LEVELS
 
 
 def split_bf16(table):
@@ -81,15 +82,16 @@
     most = costs[0]
     for r in range(1, ROWS):
         most = jnp.maximum(most, costs[r])
-    cost_lanes = jnp.concatenate([jnp.full((1, BLOCK), costs[r], jnp.int32) for r in range(ROWS)], axis=1)
+    cost_lanes = jnp.concatenate([jnp.full((16, BLOCK), costs[r], jnp.int32) for r in range(ROWS)], axis=1).astype(f32).astype(bf16)
 
     @pl.loop(0, most)
     def _(s):
-        active = s < cost_lanes
+        step = jnp.full((16, ROWS * BLOCK), s, jnp.int32).astype(f32).astype(bf16)
+        active = jnp.concatenate([cost_lanes > step] * (LEV // 16), axis=0)
         for f in range(FIELDS):
             now = state[f]
             new = jnp.dot(inverse_ref[f], now, preferred_element_type=f32)
-            state[f] = jnp.where(active, new, now.astype(f32)).astype(bf16)
+            state[f] = jnp.where(active, new.astype(bf16), now)
 
     lane = first + lax.broadcasted_iota(jnp.int32, (1, BLOCK), 1)
     keep = [lane < length_ref[r] for r in range(ROWS)]
@@ -102,10 +104,10 @@
             tendency = (relaxed - initial).astype(bf16).astype(f32)
             updated = (initial + tendency).astype(bf16).astype(f32)
             flat[pl.ds(f * LEV * ROWS + r, LEV, stride=ROWS), :] = jnp.where(keep[r], updated, 0.0)
-        piece = flat[f * LEV * ROWS:(f + 1) * LEV * ROWS, :].reshape(LEV // LEVELS, LEVELS, ROWS, BLOCK)
+        piece = flat[f * LEV * ROWS:(f + 1) * LEV * ROWS, :].reshape(LEV // PAIR, PAIR, ROWS, BLOCK)
         out_ref[f] = piece.astype(bf16)
-        first = f % 2 * (LEV // LEVELS)
-        sends.append(pltpu.make_async_copy(out_ref.at[f], out_hbm.at[pl.ds(first, LEV // LEVELS), f // 2], out_sems.at[f]))
+        first = f % 2 * (LEV // PAIR)
+        sends.append(pltpu.make_async_copy(out_ref.at[f], out_hbm.at[pl.ds(first, LEV // PAIR), f // 2], out_sems.at[f]))
         sends[-1].start()
     for send in sends:
         send.wait()
@@ -114,7 +116,7 @@
 def relax(fields, inverse, costs, lengths):
     return pl.pallas_call(
         relax_kernel,
-        out_shape=jax.ShapeDtypeStruct((HALF, 2, LEVELS, ROWS, BLOCK), bf16),
+        out_shape=jax.ShapeDtypeStruct((PAIRS, 2, PAIR, ROWS, BLOCK), bf16),
         in_specs=[pl.BlockSpec(memory_space=pltpu.HBM)] * 4,
         out_specs=pl.BlockSpec(memory_space=pltpu.HBM),
         scratch_shapes=[
@@ -125,7 +127,7 @@
             pltpu.VMEM((FIELDS * LEV * ROWS, BLOCK), f32),
             pltpu.VMEM((FIELDS, LEV, ROWS * BLOCK), bf16),
             pltpu.VMEM((FIELDS, LEV, ROWS * BLOCK), bf16),
-            pltpu.VMEM((FIELDS, LEV // LEVELS, LEVELS, ROWS, BLOCK), bf16),
+            pltpu.VMEM((FIELDS, LEV // PAIR, PAIR, ROWS, BLOCK), bf16),
             pltpu.SemaphoreType.DMA((FIELDS + 3,)),
             pltpu.SemaphoreType.DMA((FIELDS,)),
         ],
@@ -134,11 +136,9 @@
     )(costs, lengths, fields, inverse)
 
 
-def fourier_kernel(own, x_ref, inner_ref, twiddle_ref, outer_ref, out_ref, flat):
+def fourier_kernel(x_ref, inner_ref, twiddle_ref, outer_ref, out_ref, flat):
     half = lax.axis_index("zhi")
     band = lax.axis_index("band")
-    part = half if own else 1 - half
-    flat[...] = x_ref[:, part].astype(f32).reshape(HALF * LEVELS * ROWS, BLOCK)
     inner = inner_ref[half]
     outer = jnp.concatenate([outer_ref[0], outer_ref[1]], axis=1)
     cosine, sine = twiddle_ref[0], twiddle_ref[1]
@@ -146,12 +146,17 @@
     place = [lax.rem(to + N_BAND - band, N_BAND) for to in range(N_BAND)]
     waves = WAVES // N_COL
 
-    @pl.loop(0, LEVELS)
-    def _(i):
+    def load(i, slot):
+        flat[slot] = x_ref[:, i].astype(f32).reshape(HALF * ROWS, BLOCK)
+
+    def transform(i, buffer):
+        core = lax.div(i, LEVELS)
+        level = i - core * LEVELS
+        slot = lax.rem(core + half, 2)
         for r in range(0, ROWS, 4):
             twisted = []
             for e in range(r, r + 4, 2):
-                pair = [flat[pl.ds(i * ROWS + e + d, HALF, stride=LEVELS * ROWS), :] for d in range(2)]
+                pair = [flat[buffer, pl.ds(e + d, HALF, stride=ROWS), :] for d in range(2)]
                 x = jnp.concatenate(pair, axis=1).astype(bf16)
                 y = jnp.dot(inner, jnp.concatenate([x, x], axis=0), preferred_element_type=f32)
                 for d in range(2):
@@ -162,41 +167,48 @@
             z = jnp.concatenate(twisted, axis=0)
             w = lax.dot_general(outer, z, (((1,), (1,)), ((), ())), preferred_element_type=f32)
             w = w[:2 * waves] + w[2 * waves:]
-            for k in range(2):
+            for k in range(4 // 2):
                 even = w[:waves, k * BLOCK:(k + 1) * BLOCK]
                 odd = w[waves:, k * BLOCK:(k + 1) * BLOCK]
                 rows = (jnp.where(left, even, pltpu.roll(odd, N_COL, 1)), jnp.where(left, pltpu.roll(even, N_COL, 1), odd))
                 for d in range(2):
                     for to in range(N_BAND):
-                        out_ref[place[to], i, r + 2 * k + d] = rows[d][to * 8:(to + 1) * 8].astype(bf16)
-
-
-def fourier(pieces, own):
+                        out_ref[place[to], slot, level, r + 2 * k + d] = rows[d][to * 8:(to + 1) * 8].astype(bf16)
+
+    load(0, 0)
+
+    @pl.loop(0, PAIR // 2)
+    def _(j):
+        load(2 * j + 1, 1)
+        transform(2 * j, 0)
+        load(jnp.minimum(2 * j + 2, PAIR - 1), 0)
+        transform(2 * j + 1, 1)
+
+
+def fourier(pieces):
     inner, twiddle, outer = tables()
     vmem = pl.BlockSpec(memory_space=pltpu.VMEM)
     return pl.pallas_call(
-        functools.partial(fourier_kernel, own),
-        out_shape=jax.ShapeDtypeStruct((N_BAND, LEVELS, ROWS, 8, BLOCK), bf16),
+        fourier_kernel,
+        out_shape=jax.ShapeDtypeStruct((N_BAND, 2, LEVELS, ROWS, 8, BLOCK), bf16),
         in_specs=[vmem] * 4,
         out_specs=vmem,
-        scratch_shapes=[pltpu.VMEM((HALF * LEVELS * ROWS, BLOCK), f32)],
+        scratch_shapes=[pltpu.VMEM((2, HALF * ROWS, BLOCK), f32)],
         compiler_params=pltpu.CompilerParams(vmem_limit_bytes=VMEM_BYTES),
-        cost_estimate=pl.CostEstimate(flops=3_000_000_000, bytes_accessed=1_000_000, transcendentals=0),
-        name="fourier_own" if own else "fourier_other",
+        name="fourier",
     )(pieces, jnp.asarray(inner), jnp.asarray(twiddle), jnp.asarray(outer))
 
 
-def finish_kernel(own_ref, *refs):
-    ours, theirs = refs[:N_BAND - 1], refs[N_BAND - 1:2 * N_BAND - 1]
-    out_hbm, buffer, sems = refs[2 * N_BAND - 1:]
+def finish_kernel(*refs):
+    ours, theirs = refs[:N_BAND], refs[N_BAND:2 * N_BAND]
+    out_hbm, buffer, sems = refs[2 * N_BAND:]
     band = lax.axis_index("band")
     copies = []
     for shift in range(N_BAND):
         first = lax.rem(band + N_BAND - shift, N_BAND) * ROWS
         for i in range(LEVELS):
             for r in range(ROWS):
-                near = own_ref[0, i, r] if shift == 0 else ours[shift - 1][i, r]
-                piece = near.astype(f32) + theirs[shift][i, r].astype(f32)
+                piece = ours[shift][0, i, r].astype(f32) + theirs[shift][i, r].astype(f32)
                 for t in range(4):
                     buffer[shift, i, r, :, t * BLOCK:(t + 1) * BLOCK] = piece[2 * t:2 * t + 2]
         copies.append(pltpu.make_async_copy(buffer.at[shift], out_hbm.at[:, pl.ds(first, ROWS)], sems.at[shift]))
@@ -205,7 +217,7 @@
         copy.wait()
 
 
-def finish(own, ours, theirs):
+def finish(ours, theirs):
     vmem = pl.BlockSpec(memory_space=pltpu.VMEM)
     return pl.pallas_call(
         finish_kernel,
@@ -218,25 +230,28 @@
         ],
         compiler_params=pltpu.CompilerParams(vmem_limit_bytes=VMEM_BYTES),
         name="finish",
-    )(own, *ours, *theirs)
-
-
-def along_z(piece, flip, shift):
+    )(*ours, *theirs)
+
+
+def along_z(piece, shift):
     pairs = []
     for band in range(N_BAND):
         for half in range(2):
-            pairs.append((band * 2 + half, (band + shift) % N_BAND * 2 + (half ^ flip)))
-    return lax.ppermute(piece, ("band", "zhi"), pairs)
+            for core in range(2):
+                to = ((band + shift) % N_BAND * 2 + core) * 2 + half
+                pairs.append(((band * 2 + half) * 2 + core, to))
+    return lax.ppermute(piece, ("band", "zhi", "core"), pairs)
 
 
 def shards(fields, inverse, block_costs, row_length):
     updated = relax(fields, inverse, block_costs, row_length)
-    half_rows = lax.all_to_all(updated, ("y", "x", "core"), split_axis=0, concat_axis=0, tiled=True)
-    other = fourier(half_rows, False)
-    theirs = [along_z(other[shift], 1, shift) for shift in range(N_BAND)]
-    own = fourier(half_rows, True)
-    ours = [along_z(own[shift], 0, shift) for shift in range(1, N_BAND)]
-    return finish(own, ours, theirs)
+    half_rows = lax.all_to_all(
+        updated.reshape(HALF, PAIR, ROWS, BLOCK), ("y", "x", "core"), split_axis=0, concat_axis=0, tiled=True
+    )
+    spectra = fourier(half_rows)
+    ours = [along_z(spectra[shift], shift) for shift in range(N_BAND)]
+    theirs = [lax.ppermute(piece[1], "core", [(0, 1), (1, 0)]) for piece in ours]
+    return finish(ours, theirs)
 
 
 def solution(mesh):

time: 57.3 us -> 55.8 us (0.974)
  Pallas kernels: 9.14 us -> 7.24 us
  starting transfers between devices: 15.4 us -> 14.7 us
    pallas_call x3 -> x2, Pallas kernels: 8.23 us -> 6.33 us  [the longest x1 3.31 us: fourier(): pl.pallas_call(fourier_kernel, out_shape=jax.ShapeDtypeStruct((N_BAND, 2,...]
    ppermute x7 -> x8, starting transfers between devices: 15.4 us -> 14.7 us  [the longest x4 14.6 us: along_z(): return lax.ppermute(piece, ('band', 'zhi', 'core'), pairs)]
    ppermute x7 -> x8, waiting for transfers between devices: 9.67 us -> 9.85 us  [the longest x4 8.6 us: along_z(): return lax.ppermute(piece, ('band', 'zhi', 'core'), pairs)]
  transfers between devices with their start and end apart: 7 -> 8, of which waited for: 4 -> 5; matrix products, arithmetic and copies ran while one was open for 0% -> 0% of each run, Pallas kernels for 5% -> 0%
where the time goes in v5:
time: 55.8 us; the launch traced here: 55.1 us
  blocking collectives  23.1 us (41%)
  starting transfers between devices  14.7 us (26%)
  waiting for transfers between devices  9.85 us (18%)
  Pallas kernels  7.24 us (13%)
    all_to_all x1, blocking collectives, shards(): lax.all_to_all(updated.reshape(HALF, PAIR, ROWS, BLOCK), ('y', 'x', 'core...  23.1 us
    ppermute x4, starting transfers between devices, along_z(): return lax.ppermute(piece, ('band', 'zhi', 'core'), pairs)  14.6 us
    ppermute x4, waiting for transfers between devices, along_z(): return lax.ppermute(piece, ('band', 'zhi', 'core'), pairs)  8.6 us
    pallas_call x1, Pallas kernels, fourier(): pl.pallas_call(fourier_kernel, out_shape=jax.ShapeDtypeStruct((N_BAND, 2,...  3.31 us
    pallas_call x1, Pallas kernels, relax(): pl.pallas_call(relax_kernel, out_shape=jax.ShapeDtypeStruct((PAIRS, 2, PA...  3.02 us
    ppermute x4, waiting for transfers between devices, shards(): lax.ppermute(piece[1], 'core', [(0, 1), (1, 0)])  1.24 us
  transfers between devices with their start and end apart: 8, of which 5 were waited for; matrix products, arithmetic and copies ran while one was open for 0% of the time, Pallas kernels for 0%

profile of v5, /device:TPU:1, one launch (start us, length us, event | category | flops | bytes accessed | tf_op | source)
XLA Modules:
  0.0 55.1 jit_solution(14819043305147108859)
XLA Ops:
  0.0 3.0 %relax.1 = bf16[16,2,10,8,128]{4,3,2,1,0:T(8,128)(2,1)} custom-call(s32[1,8]{1,0:T(1,128)} %cost_hbm.1, s32[8]{0:T(128)} %length_hbm.1, bf16[4,80,8,128]{3,2,1,0:T(8,128)(2,1)} %fields_hbm.1, bf16[4,80,80]{2,1,0:T(8,128)(2,1)} %inverse_hbm.1), custom_call_target="tpu_custom_call" | custom-call | tf_op jit(solution)/shard_map/relax/pallas_call | solution.py:117
  3.0 0.0 copy-start
  3.0 0.0 copy-start.1
  3.0 0.0 copy-start.2
  3.1 23.1 %all_to_all.5.x_ref = bf16[32,10,8,128]{3,2,1,0:T(8,128)(2,1)S(1)} all-to-all(bf16[32,10,8,128]{3,2,1,0:T(8,128)(2,1)} %bitcast.17), channel_id=1, replica_groups=mesh['band'=4,'zhi'=2,'y'=4,'x'=4,'core'=2] {'y','x','core'}, dimensions={0} | all-to-all | bytes 1310720 | tf_op jit(solution)/shard_map/all_to_all | solution.py:248
  26.2 0.0 copy-done
  26.2 0.0 copy-done.1
  26.2 0.0 copy-done.2
  26.2 3.3 %fourier.1 = bf16[4,2,5,8,8,128]{5,4,3,2,1,0:T(8,128)(2,1)S(1)} custom-call(bf16[32,10,8,128]{3,2,1,0:T(8,128)(2,1)S(1)} %all_to_all.5.x_ref, bf16[2,128,64]{2,1,0:T(8,128)(2,1)S(1)} %copy-done.2, f32[2,64,128]{2,1,0:T(8,128)S(1)} %copy-done.1, bf16[2,128,128]{2,1,0:T(8,128)(2,1)S(1)} %copy-done), custom_call_target="tpu_custom_call" | custom-call | tf_op jit(solution)/shard_map/fourier/pallas_call | solution.py:191
  29.5 0.1 slice_bitcast_fusion
  29.6 6.6 %collective-permute-start.3 = (bf16[2,5,8,8,128]{4,3,2,1,0:T(8,128)(2,1)S(1)}, bf16[2,5,8,8,128]{4,3,2,1,0:T(8,128)(2,1)S(1)}, u32[]{:S(2)}, u32[]{:S(2)}) collective-permute-start(bf16[2,5,8,8,128]{4,3,2,1,0:T(8,128)(2,1)S(1)} %get-tuple-element.5), channel_id=1, source_target_pairs={{0,192},{1,224},{32,193},{33,225},{64,0},{65,32},{96,1},{97,33},{1... | collective-permute-start | bytes 491528 | tf_op jit(solution)/shard_map/ppermute | solution.py:243
  36.2 0.2 collective-permute-start.2
  36.4 4.7 %collective-permute-start.1 = (bf16[2,5,8,8,128]{4,3,2,1,0:T(8,128)(2,1)S(1)}, bf16[2,5,8,8,128]{4,3,2,1,0:T(8,128)(2,1)S(1)}, u32[]{:S(2)}, u32[]{:S(2)}) collective-permute-start(bf16[2,5,8,8,128]{4,3,2,1,0:T(8,128)(2,1)S(1)} %get-tuple-element.7), channel_id=1, source_target_pairs={{0,64},{1,96},{32,65},{33,97},{64,128},{65,160},{96,129},{97,161},... | collective-permute-start | bytes 491528 | tf_op jit(solution)/shard_map/ppermute | solution.py:243
  41.1 3.1 %collective-permute-start = (bf16[2,5,8,8,128]{4,3,2,1,0:T(8,128)(2,1)S(1)}, bf16[2,5,8,8,128]{4,3,2,1,0:T(8,128)(2,1)S(1)}, u32[]{:S(2)}, u32[]{:S(2)}) collective-permute-start(bf16[2,5,8,8,128]{4,3,2,1,0:T(8,128)(2,1)S(1)} %get-tuple-element.8), channel_id=1, source_target_pairs={{0,0},{1,32},{32,1},{33,33},{64,64},{65,96},{96,65},{97,97},{128,1... | collective-permute-start | bytes 491528 | tf_op jit(solution)/shard_map/ppermute | solution.py:243
  44.2 0.1 collective-permute-done.3.refs_3_
  44.3 0.1 collective-permute-start.7
  44.4 3.9 %collective-permute-done.2.refs_2_ = bf16[2,5,8,8,128]{4,3,2,1,0:T(8,128)(2,1)S(1)} collective-permute-done((bf16[2,5,8,8,128]{4,3,2,1,0:T(8,128)(2,1)S(1)}, bf16[2,5,8,8,128]{4,3,2,1,0:T(8,128)(2,1)S(1)}, u32[]{:S(2)}, u32[]{:S(2)}) %collective-permute-start.2) | collective-permute-done | bytes 163872 | tf_op jit(solution)/shard_map/ppermute | solution.py:243
  48.3 0.0 collective-permute-start.6
  48.3 3.2 %collective-permute-done.1.refs_1_ = bf16[2,5,8,8,128]{4,3,2,1,0:T(8,128)(2,1)S(1)} collective-permute-done((bf16[2,5,8,8,128]{4,3,2,1,0:T(8,128)(2,1)S(1)}, bf16[2,5,8,8,128]{4,3,2,1,0:T(8,128)(2,1)S(1)}, u32[]{:S(2)}, u32[]{:S(2)}) %collective-permute-start.1) | collective-permute-done | bytes 163872 | tf_op jit(solution)/shard_map/ppermute | solution.py:243
  51.5 0.0 collective-permute-start.5
  51.5 1.4 %collective-permute-done.refs_0_ = bf16[2,5,8,8,128]{4,3,2,1,0:T(8,128)(2,1)S(1)} collective-permute-done((bf16[2,5,8,8,128]{4,3,2,1,0:T(8,128)(2,1)S(1)}, bf16[2,5,8,8,128]{4,3,2,1,0:T(8,128)(2,1)S(1)}, u32[]{:S(2)}, u32[]{:S(2)}) %collective-permute-start) | collective-permute-done | bytes 163872 | tf_op jit(solution)/shard_map/ppermute | solution.py:243
  52.9 0.0 collective-permute-start.4
  52.9 0.0 collective-permute-done.7.refs_7_
  53.0 0.0 collective-permute-done.6.refs_6_
  53.0 0.0 collective-permute-done.5.refs_5_
  53.0 1.2 %collective-permute-done.4.refs_4_ = bf16[5,8,8,128]{3,2,1,0:T(8,128)(2,1)S(1)} collective-permute-done((bf16[5,8,8,128]{3,2,1,0:T(8,128)(2,1)S(1)}, bf16[5,8,8,128]{3,2,1,0:T(8,128)(2,1)S(1)}, u32[]{:S(2)}, u32[]{:S(2)}) %collective-permute-start.4) | collective-permute-done | bytes 81952 | tf_op jit(solution)/shard_map/ppermute | solution.py:253
  54.2 0.9 %finish.1 = f32[5,32,2,512]{3,2,1,0:T(2,128)} custom-call(bf16[2,5,8,8,128]{4,3,2,1,0:T(8,128)(2,1)S(1)} %collective-permute-done.refs_0_, bf16[2,5,8,8,128]{4,3,2,1,0:T(8,128)(2,1)S(1)} %collective-permute-done.1.refs_1_, bf16[2,5,8,8,128]{4,3,2,1,0:T(8,128)(2,1)S(1)} %collective-permute-done.2.refs_2_, ...), custom_call_target="tpu_custom_call" | custom-call | tf_op jit(solution)/shard_map/finish/pallas_call | solution.py:222
  (4 shorter events, 0.0 us)
Async XLA Ops:
  3.0 23.1 %copy-start = (bf16[2,128,128]{2,1,0:T(8,128)(2,1)S(1)}, bf16[2,128,128]{2,1,0:T(8,128)(2,1)}, u32[]{:S(2)}) copy-start(bf16[2,128,128]{2,1,0:T(8,128)(2,1)} %constant.8.clone.outer_ref) | copy-start | bytes 196612
  3.0 23.1 %copy-start.1 = (f32[2,64,128]{2,1,0:T(8,128)S(1)}, f32[2,64,128]{2,1,0:T(8,128)}, u32[]{:S(2)}) copy-start(f32[2,64,128]{2,1,0:T(8,128)} %constant.7.clone.twiddle_ref) | copy-start | bytes 196612
  3.0 23.1 %copy-start.2 = (bf16[2,128,64]{2,1,0:T(8,128)(2,1)S(1)}, bf16[2,128,64]{2,1,0:T(8,128)(2,1)}, u32[]{:S(2)}) copy-start(bf16[2,128,64]{2,1,0:T(8,128)(2,1)} %constant.6.clone.inner_ref) | copy-start | bytes 98308
  29.6 14.7 %collective-permute-start.3 = (bf16[2,5,8,8,128]{4,3,2,1,0:T(8,128)(2,1)S(1)}, bf16[2,5,8,8,128]{4,3,2,1,0:T(8,128)(2,1)S(1)}, u32[]{:S(2)}, u32[]{:S(2)}) collective-permute-start(bf16[2,5,8,8,128]{4,3,2,1,0:T(8,128)(2,1)S(1)} %get-tuple-element.5), channel_id=1, source_target_pairs={{0,192},{1,224},{32,193},{33,225},{64,0},{65,32},{96,1},{97,33},{1... | collective-permute-start | bytes 491528 | tf_op jit(solution)/shard_map/ppermute | solution.py:243
  36.2 12.1 %collective-permute-start.2 = (bf16[2,5,8,8,128]{4,3,2,1,0:T(8,128)(2,1)S(1)}, bf16[2,5,8,8,128]{4,3,2,1,0:T(8,128)(2,1)S(1)}, u32[]{:S(2)}, u32[]{:S(2)}) collective-permute-start(bf16[2,5,8,8,128]{4,3,2,1,0:T(8,128)(2,1)S(1)} %get-tuple-element.6), channel_id=1, source_target_pairs={{0,128},{1,160},{32,129},{33,161},{64,192},{65,224},{96,193},{97,2... | collective-permute-start | bytes 491528 | tf_op jit(solution)/shard_map/ppermute | solution.py:243
  36.4 15.1 %collective-permute-start.1 = (bf16[2,5,8,8,128]{4,3,2,1,0:T(8,128)(2,1)S(1)}, bf16[2,5,8,8,128]{4,3,2,1,0:T(8,128)(2,1)S(1)}, u32[]{:S(2)}, u32[]{:S(2)}) collective-permute-start(bf16[2,5,8,8,128]{4,3,2,1,0:T(8,128)(2,1)S(1)} %get-tuple-element.7), channel_id=1, source_target_pairs={{0,64},{1,96},{32,65},{33,97},{64,128},{65,160},{96,129},{97,161},... | collective-permute-start | bytes 491528 | tf_op jit(solution)/shard_map/ppermute | solution.py:243
  41.1 11.8 %collective-permute-start = (bf16[2,5,8,8,128]{4,3,2,1,0:T(8,128)(2,1)S(1)}, bf16[2,5,8,8,128]{4,3,2,1,0:T(8,128)(2,1)S(1)}, u32[]{:S(2)}, u32[]{:S(2)}) collective-permute-start(bf16[2,5,8,8,128]{4,3,2,1,0:T(8,128)(2,1)S(1)} %get-tuple-element.8), channel_id=1, source_target_pairs={{0,0},{1,32},{32,1},{33,33},{64,64},{65,96},{96,65},{97,97},{128,1... | collective-permute-start | bytes 491528 | tf_op jit(solution)/shard_map/ppermute | solution.py:243
  44.3 8.7 %collective-permute-start.7 = (bf16[5,8,8,128]{3,2,1,0:T(8,128)(2,1)S(1)}, bf16[5,8,8,128]{3,2,1,0:T(8,128)(2,1)S(1)}, u32[]{:S(2)}, u32[]{:S(2)}) collective-permute-start(bf16[5,8,8,128]{3,2,1,0:T(8,128)(2,1)S(1)} %slice_bitcast_fusion.4), channel_id=1, source_target_pairs={{0,1},{1,0},{2,3},{3,2},{4,5},{5,4},{6,7},{7,6},{8,9},{9,8},{10,11... | collective-permute-start | bytes 245768 | tf_op jit(solution)/shard_map/ppermute | solution.py:253
  48.3 4.7 %collective-permute-start.6 = (bf16[5,8,8,128]{3,2,1,0:T(8,128)(2,1)S(1)}, bf16[5,8,8,128]{3,2,1,0:T(8,128)(2,1)S(1)}, u32[]{:S(2)}, u32[]{:S(2)}) collective-permute-start(bf16[5,8,8,128]{3,2,1,0:T(8,128)(2,1)S(1)} %slice_bitcast_fusion.5), channel_id=1, source_target_pairs={{0,1},{1,0},{2,3},{3,2},{4,5},{5,4},{6,7},{7,6},{8,9},{9,8},{10,11... | collective-permute-start | bytes 245768 | tf_op jit(solution)/shard_map/ppermute | solution.py:253
  51.5 1.4 %collective-permute-start.5 = (bf16[5,8,8,128]{3,2,1,0:T(8,128)(2,1)S(1)}, bf16[5,8,8,128]{3,2,1,0:T(8,128)(2,1)S(1)}, u32[]{:S(2)}, u32[]{:S(2)}) collective-permute-start(bf16[5,8,8,128]{3,2,1,0:T(8,128)(2,1)S(1)} %slice_bitcast_fusion.6), channel_id=1, source_target_pairs={{0,1},{1,0},{2,3},{3,2},{4,5},{5,4},{6,7},{7,6},{8,9},{9,8},{10,11... | collective-permute-start | bytes 245768 | tf_op jit(solution)/shard_map/ppermute | solution.py:253
  52.9 1.3 %collective-permute-start.4 = (bf16[5,8,8,128]{3,2,1,0:T(8,128)(2,1)S(1)}, bf16[5,8,8,128]{3,2,1,0:T(8,128)(2,1)S(1)}, u32[]{:S(2)}, u32[]{:S(2)}) collective-permute-start(bf16[5,8,8,128]{3,2,1,0:T(8,128)(2,1)S(1)} %slice_bitcast_fusion.7), channel_id=1, source_target_pairs={{0,1},{1,0},{2,3},{3,2},{4,5},{5,4},{6,7},{7,6},{8,9},{9,8},{10,11... | collective-permute-start | bytes 245768 | tf_op jit(solution)/shard_map/ppermute | solution.py:253

commit v6 on v5

--- a/solution.py
+++ b/solution.py
@@ -15,6 +15,7 @@
 
 FIELDS = 4
 LEV = 80
+CMAX = 8
 ROWS = 8
 BLOCK = 128
 N_COL = 64
@@ -84,14 +85,21 @@
         most = jnp.maximum(most, costs[r])
     cost_lanes = jnp.concatenate([jnp.full((16, BLOCK), costs[r], jnp.int32) for r in range(ROWS)], axis=1).astype(f32).astype(bf16)
 
-    @pl.loop(0, most)
-    def _(s):
+    def sweep(s):
         step = jnp.full((16, ROWS * BLOCK), s, jnp.int32).astype(f32).astype(bf16)
-        active = jnp.concatenate([cost_lanes > step] * (LEV // 16), axis=0)
         for f in range(FIELDS):
-            now = state[f]
-            new = jnp.dot(inverse_ref[f], now, preferred_element_type=f32)
-            state[f] = jnp.where(active, new.astype(bf16), now)
+            for t in range(0, ROWS * BLOCK, 2 * BLOCK):
+                active = jnp.concatenate([cost_lanes[:, t:t + 2 * BLOCK] > step[:, t:t + 2 * BLOCK]] * (LEV // 16), axis=0)
+                now = state[f, :, t:t + 2 * BLOCK]
+                new = jnp.dot(inverse_ref[f], now, preferred_element_type=f32)
+                state[f, :, t:t + 2 * BLOCK] = jnp.where(active, new.astype(bf16), now)
+
+    sweep(0)
+
+    @pl.when(most > 1)
+    def _():
+        for s in range(1, CMAX):
+            sweep(s)
 
     lane = first + lax.broadcasted_iota(jnp.int32, (1, BLOCK), 1)
     keep = [lane < length_ref[r] for r in range(ROWS)]

time: 55.8 us -> 54.6 us (0.978)
  the two profiles are of different devices: /device:TPU:1 before, /device:TPU:33 now
where the time goes in v6:
time: 54.6 us; the launch traced here: 54.4 us
  blocking collectives  20.4 us (37%)
  starting transfers between devices  15.4 us (28%)
  waiting for transfers between devices  9.82 us (18%)
  Pallas kernels  8.55 us (16%)
    all_to_all x1, blocking collectives, shards(): lax.all_to_all(updated.reshape(HALF, PAIR, ROWS, BLOCK), ('y', 'x', 'core...  20.4 us
    ppermute x4, starting transfers between devices, along_z(): return lax.ppermute(piece, ('band', 'zhi', 'core'), pairs)  13.1 us
    ppermute x4, waiting for transfers between devices, along_z(): return lax.ppermute(piece, ('band', 'zhi', 'core'), pairs)  8.57 us
    pallas_call x1, Pallas kernels, relax(): pl.pallas_call(relax_kernel, out_shape=jax.ShapeDtypeStruct((PAIRS, 2, PA...  4.33 us
    pallas_call x1, Pallas kernels, fourier(): pl.pallas_call(fourier_kernel, out_shape=jax.ShapeDtypeStruct((N_BAND, 2,...  3.31 us
    ppermute x4, starting transfers between devices, shards(): lax.ppermute(piece[1], 'core', [(0, 1), (1, 0)])  2.36 us
    ppermute x4, waiting for transfers between devices, shards(): lax.ppermute(piece[1], 'core', [(0, 1), (1, 0)])  1.24 us
  transfers between devices with their start and end apart: 8, of which 4 were waited for; matrix products, arithmetic and copies ran while one was open for 0% of the time, Pallas kernels for 0%

profile of v6, /device:TPU:33, one launch (start us, length us, event | category | flops | bytes accessed | tf_op | source)
XLA Modules:
  0.0 54.4 jit_solution(3991427968705802729)
XLA Ops:
  0.0 4.3 %relax.1 = bf16[16,2,10,8,128]{4,3,2,1,0:T(8,128)(2,1)} custom-call(s32[1,8]{1,0:T(1,128)} %cost_hbm.1, s32[8]{0:T(128)} %length_hbm.1, bf16[4,80,8,128]{3,2,1,0:T(8,128)(2,1)} %fields_hbm.1, bf16[4,80,80]{2,1,0:T(8,128)(2,1)} %inverse_hbm.1), custom_call_target="tpu_custom_call" | custom-call | tf_op jit(solution)/shard_map/relax/pallas_call | solution.py:125
  4.3 0.0 copy-start
  4.3 0.0 copy-start.1
  4.4 0.0 copy-start.2
  4.4 20.4 %all_to_all.5.x_ref = bf16[32,10,8,128]{3,2,1,0:T(8,128)(2,1)S(1)} all-to-all(bf16[32,10,8,128]{3,2,1,0:T(8,128)(2,1)} %bitcast.17), channel_id=1, replica_groups=mesh['band'=4,'zhi'=2,'y'=4,'x'=4,'core'=2] {'y','x','core'}, dimensions={0} | all-to-all | bytes 1310720 | tf_op jit(solution)/shard_map/all_to_all | solution.py:256
  24.7 0.0 copy-done
  24.7 0.0 copy-done.1
  24.7 0.0 copy-done.2
  24.8 3.3 %fourier.1 = bf16[4,2,5,8,8,128]{5,4,3,2,1,0:T(8,128)(2,1)S(1)} custom-call(bf16[32,10,8,128]{3,2,1,0:T(8,128)(2,1)S(1)} %all_to_all.5.x_ref, bf16[2,128,64]{2,1,0:T(8,128)(2,1)S(1)} %copy-done.2, f32[2,64,128]{2,1,0:T(8,128)S(1)} %copy-done.1, bf16[2,128,128]{2,1,0:T(8,128)(2,1)S(1)} %copy-done), custom_call_target="tpu_custom_call" | custom-call | tf_op jit(solution)/shard_map/fourier/pallas_call | solution.py:199
  28.1 0.1 slice_bitcast_fusion
  28.1 6.0 %collective-permute-start.3 = (bf16[2,5,8,8,128]{4,3,2,1,0:T(8,128)(2,1)S(1)}, bf16[2,5,8,8,128]{4,3,2,1,0:T(8,128)(2,1)S(1)}, u32[]{:S(2)}, u32[]{:S(2)}) collective-permute-start(bf16[2,5,8,8,128]{4,3,2,1,0:T(8,128)(2,1)S(1)} %get-tuple-element.5), channel_id=1, source_target_pairs={{0,192},{1,224},{32,193},{33,225},{64,0},{65,32},{96,1},{97,33},{1... | collective-permute-start | bytes 491528 | tf_op jit(solution)/shard_map/ppermute | solution.py:251
  34.1 0.0 collective-permute-start.2
  34.1 3.4 %collective-permute-start.1 = (bf16[2,5,8,8,128]{4,3,2,1,0:T(8,128)(2,1)S(1)}, bf16[2,5,8,8,128]{4,3,2,1,0:T(8,128)(2,1)S(1)}, u32[]{:S(2)}, u32[]{:S(2)}) collective-permute-start(bf16[2,5,8,8,128]{4,3,2,1,0:T(8,128)(2,1)S(1)} %get-tuple-element.7), channel_id=1, source_target_pairs={{0,64},{1,96},{32,65},{33,97},{64,128},{65,160},{96,129},{97,161},... | collective-permute-start | bytes 491528 | tf_op jit(solution)/shard_map/ppermute | solution.py:251
  37.5 3.7 %collective-permute-start = (bf16[2,5,8,8,128]{4,3,2,1,0:T(8,128)(2,1)S(1)}, bf16[2,5,8,8,128]{4,3,2,1,0:T(8,128)(2,1)S(1)}, u32[]{:S(2)}, u32[]{:S(2)}) collective-permute-start(bf16[2,5,8,8,128]{4,3,2,1,0:T(8,128)(2,1)S(1)} %get-tuple-element.8), channel_id=1, source_target_pairs={{0,0},{1,32},{32,1},{33,33},{64,64},{65,96},{96,65},{97,97},{128,1... | collective-permute-start | bytes 491528 | tf_op jit(solution)/shard_map/ppermute | solution.py:251
  41.2 2.5 %collective-permute-done.3.refs_3_ = bf16[2,5,8,8,128]{4,3,2,1,0:T(8,128)(2,1)S(1)} collective-permute-done((bf16[2,5,8,8,128]{4,3,2,1,0:T(8,128)(2,1)S(1)}, bf16[2,5,8,8,128]{4,3,2,1,0:T(8,128)(2,1)S(1)}, u32[]{:S(2)}, u32[]{:S(2)}) %collective-permute-start.3) | collective-permute-done | bytes 163872 | tf_op jit(solution)/shard_map/ppermute | solution.py:251
  43.7 0.0 collective-permute-start.7
  43.7 0.0 collective-permute-done.2.refs_2_
  43.7 0.6 %collective-permute-start.6 = (bf16[5,8,8,128]{3,2,1,0:T(8,128)(2,1)S(1)}, bf16[5,8,8,128]{3,2,1,0:T(8,128)(2,1)S(1)}, u32[]{:S(2)}, u32[]{:S(2)}) collective-permute-start(bf16[5,8,8,128]{3,2,1,0:T(8,128)(2,1)S(1)} %slice_bitcast_fusion.5), channel_id=1, source_target_pairs={{0,1},{1,0},{2,3},{3,2},{4,5},{5,4},{6,7},{7,6},{8,9},{9,8},{10,11... | collective-permute-start | bytes 245768 | tf_op jit(solution)/shard_map/ppermute | solution.py:261
  44.3 1.4 %collective-permute-done.1.refs_1_ = bf16[2,5,8,8,128]{4,3,2,1,0:T(8,128)(2,1)S(1)} collective-permute-done((bf16[2,5,8,8,128]{4,3,2,1,0:T(8,128)(2,1)S(1)}, bf16[2,5,8,8,128]{4,3,2,1,0:T(8,128)(2,1)S(1)}, u32[]{:S(2)}, u32[]{:S(2)}) %collective-permute-start.1) | collective-permute-done | bytes 163872 | tf_op jit(solution)/shard_map/ppermute | solution.py:251
  45.7 1.8 %collective-permute-start.5 = (bf16[5,8,8,128]{3,2,1,0:T(8,128)(2,1)S(1)}, bf16[5,8,8,128]{3,2,1,0:T(8,128)(2,1)S(1)}, u32[]{:S(2)}, u32[]{:S(2)}) collective-permute-start(bf16[5,8,8,128]{3,2,1,0:T(8,128)(2,1)S(1)} %slice_bitcast_fusion.6), channel_id=1, source_target_pairs={{0,1},{1,0},{2,3},{3,2},{4,5},{5,4},{6,7},{7,6},{8,9},{9,8},{10,11... | collective-permute-start | bytes 245768 | tf_op jit(solution)/shard_map/ppermute | solution.py:261
  47.5 4.7 %collective-permute-done.refs_0_ = bf16[2,5,8,8,128]{4,3,2,1,0:T(8,128)(2,1)S(1)} collective-permute-done((bf16[2,5,8,8,128]{4,3,2,1,0:T(8,128)(2,1)S(1)}, bf16[2,5,8,8,128]{4,3,2,1,0:T(8,128)(2,1)S(1)}, u32[]{:S(2)}, u32[]{:S(2)}) %collective-permute-start) | collective-permute-done | bytes 163872 | tf_op jit(solution)/shard_map/ppermute | solution.py:251
  52.2 0.0 collective-permute-start.4
  52.2 0.0 collective-permute-done.7.refs_7_
  52.2 0.0 collective-permute-done.6.refs_6_
  52.2 0.0 collective-permute-done.5.refs_5_
  52.2 1.2 %collective-permute-done.4.refs_4_ = bf16[5,8,8,128]{3,2,1,0:T(8,128)(2,1)S(1)} collective-permute-done((bf16[5,8,8,128]{3,2,1,0:T(8,128)(2,1)S(1)}, bf16[5,8,8,128]{3,2,1,0:T(8,128)(2,1)S(1)}, u32[]{:S(2)}, u32[]{:S(2)}) %collective-permute-start.4) | collective-permute-done | bytes 81952 | tf_op jit(solution)/shard_map/ppermute | solution.py:261
  53.5 0.9 %finish.1 = f32[5,32,2,512]{3,2,1,0:T(2,128)} custom-call(bf16[2,5,8,8,128]{4,3,2,1,0:T(8,128)(2,1)S(1)} %collective-permute-done.refs_0_, bf16[2,5,8,8,128]{4,3,2,1,0:T(8,128)(2,1)S(1)} %collective-permute-done.1.refs_1_, bf16[2,5,8,8,128]{4,3,2,1,0:T(8,128)(2,1)S(1)} %collective-permute-done.2.refs_2_, ...), custom_call_target="tpu_custom_call" | custom-call | tf_op jit(solution)/shard_map/finish/pallas_call | solution.py:230
  (4 shorter events, 0.0 us)
Async XLA Ops:
  4.3 20.4 %copy-start = (bf16[2,128,128]{2,1,0:T(8,128)(2,1)S(1)}, bf16[2,128,128]{2,1,0:T(8,128)(2,1)}, u32[]{:S(2)}) copy-start(bf16[2,128,128]{2,1,0:T(8,128)(2,1)} %constant.8.clone.outer_ref) | copy-start | bytes 196612
  4.3 20.4 %copy-start.1 = (f32[2,64,128]{2,1,0:T(8,128)S(1)}, f32[2,64,128]{2,1,0:T(8,128)}, u32[]{:S(2)}) copy-start(f32[2,64,128]{2,1,0:T(8,128)} %constant.7.clone.twiddle_ref) | copy-start | bytes 196612
  4.4 20.4 %copy-start.2 = (bf16[2,128,64]{2,1,0:T(8,128)(2,1)S(1)}, bf16[2,128,64]{2,1,0:T(8,128)(2,1)}, u32[]{:S(2)}) copy-start(bf16[2,128,64]{2,1,0:T(8,128)(2,1)} %constant.6.clone.inner_ref) | copy-start | bytes 98308
  28.1 15.5 %collective-permute-start.3 = (bf16[2,5,8,8,128]{4,3,2,1,0:T(8,128)(2,1)S(1)}, bf16[2,5,8,8,128]{4,3,2,1,0:T(8,128)(2,1)S(1)}, u32[]{:S(2)}, u32[]{:S(2)}) collective-permute-start(bf16[2,5,8,8,128]{4,3,2,1,0:T(8,128)(2,1)S(1)} %get-tuple-element.5), channel_id=1, source_target_pairs={{0,192},{1,224},{32,193},{33,225},{64,0},{65,32},{96,1},{97,33},{1... | collective-permute-start | bytes 491528 | tf_op jit(solution)/shard_map/ppermute | solution.py:251
  34.1 9.6 %collective-permute-start.2 = (bf16[2,5,8,8,128]{4,3,2,1,0:T(8,128)(2,1)S(1)}, bf16[2,5,8,8,128]{4,3,2,1,0:T(8,128)(2,1)S(1)}, u32[]{:S(2)}, u32[]{:S(2)}) collective-permute-start(bf16[2,5,8,8,128]{4,3,2,1,0:T(8,128)(2,1)S(1)} %get-tuple-element.6), channel_id=1, source_target_pairs={{0,128},{1,160},{32,129},{33,161},{64,192},{65,224},{96,193},{97,2... | collective-permute-start | bytes 491528 | tf_op jit(solution)/shard_map/ppermute | solution.py:251
  34.1 11.6 %collective-permute-start.1 = (bf16[2,5,8,8,128]{4,3,2,1,0:T(8,128)(2,1)S(1)}, bf16[2,5,8,8,128]{4,3,2,1,0:T(8,128)(2,1)S(1)}, u32[]{:S(2)}, u32[]{:S(2)}) collective-permute-start(bf16[2,5,8,8,128]{4,3,2,1,0:T(8,128)(2,1)S(1)} %get-tuple-element.7), channel_id=1, source_target_pairs={{0,64},{1,96},{32,65},{33,97},{64,128},{65,160},{96,129},{97,161},... | collective-permute-start | bytes 491528 | tf_op jit(solution)/shard_map/ppermute | solution.py:251
  37.5 14.7 %collective-permute-start = (bf16[2,5,8,8,128]{4,3,2,1,0:T(8,128)(2,1)S(1)}, bf16[2,5,8,8,128]{4,3,2,1,0:T(8,128)(2,1)S(1)}, u32[]{:S(2)}, u32[]{:S(2)}) collective-permute-start(bf16[2,5,8,8,128]{4,3,2,1,0:T(8,128)(2,1)S(1)} %get-tuple-element.8), channel_id=1, source_target_pairs={{0,0},{1,32},{32,1},{33,33},{64,64},{65,96},{96,65},{97,97},{128,1... | collective-permute-start | bytes 491528 | tf_op jit(solution)/shard_map/ppermute | solution.py:251
  43.7 8.5 %collective-permute-start.7 = (bf16[5,8,8,128]{3,2,1,0:T(8,128)(2,1)S(1)}, bf16[5,8,8,128]{3,2,1,0:T(8,128)(2,1)S(1)}, u32[]{:S(2)}, u32[]{:S(2)}) collective-permute-start(bf16[5,8,8,128]{3,2,1,0:T(8,128)(2,1)S(1)} %slice_bitcast_fusion.4), channel_id=1, source_target_pairs={{0,1},{1,0},{2,3},{3,2},{4,5},{5,4},{6,7},{7,6},{8,9},{9,8},{10,11... | collective-permute-start | bytes 245768 | tf_op jit(solution)/shard_map/ppermute | solution.py:261
  43.7 8.5 %collective-permute-start.6 = (bf16[5,8,8,128]{3,2,1,0:T(8,128)(2,1)S(1)}, bf16[5,8,8,128]{3,2,1,0:T(8,128)(2,1)S(1)}, u32[]{:S(2)}, u32[]{:S(2)}) collective-permute-start(bf16[5,8,8,128]{3,2,1,0:T(8,128)(2,1)S(1)} %slice_bitcast_fusion.5), channel_id=1, source_target_pairs={{0,1},{1,0},{2,3},{3,2},{4,5},{5,4},{6,7},{7,6},{8,9},{9,8},{10,11... | collective-permute-start | bytes 245768 | tf_op jit(solution)/shard_map/ppermute | solution.py:261
  45.7 6.5 %collective-permute-start.5 = (bf16[5,8,8,128]{3,2,1,0:T(8,128)(2,1)S(1)}, bf16[5,8,8,128]{3,2,1,0:T(8,128)(2,1)S(1)}, u32[]{:S(2)}, u32[]{:S(2)}) collective-permute-start(bf16[5,8,8,128]{3,2,1,0:T(8,128)(2,1)S(1)} %slice_bitcast_fusion.6), channel_id=1, source_target_pairs={{0,1},{1,0},{2,3},{3,2},{4,5},{5,4},{6,7},{7,6},{8,9},{9,8},{10,11... | collective-permute-start | bytes 245768 | tf_op jit(solution)/shard_map/ppermute | solution.py:261
  52.2 1.3 %collective-permute-start.4 = (bf16[5,8,8,128]{3,2,1,0:T(8,128)(2,1)S(1)}, bf16[5,8,8,128]{3,2,1,0:T(8,128)(2,1)S(1)}, u32[]{:S(2)}, u32[]{:S(2)}) collective-permute-start(bf16[5,8,8,128]{3,2,1,0:T(8,128)(2,1)S(1)} %slice_bitcast_fusion.7), channel_id=1, source_target_pairs={{0,1},{1,0},{2,3},{3,2},{4,5},{5,4},{6,7},{7,6},{8,9},{9,8},{10,11... | collective-permute-start | bytes 245768 | tf_op jit(solution)/shard_map/ppermute | solution.py:261

commit v7 on v6

--- a/solution.py
+++ b/solution.py
@@ -1,3 +1,4 @@
+import functools
 import math
 
 import jax
@@ -158,8 +159,7 @@
         flat[slot] = x_ref[:, i].astype(f32).reshape(HALF * ROWS, BLOCK)
 
     def transform(i, buffer):
-        core = lax.div(i, LEVELS)
-        level = i - core * LEVELS
+        core, level = divmod(i, LEVELS)
         slot = lax.rem(core + half, 2)
         for r in range(0, ROWS, 4):
             twisted = []
@@ -184,13 +184,10 @@
                         out_ref[place[to], slot, level, r + 2 * k + d] = rows[d][to * 8:(to + 1) * 8].astype(bf16)
 
     load(0, 0)
-
-    @pl.loop(0, PAIR // 2)
-    def _(j):
-        load(2 * j + 1, 1)
-        transform(2 * j, 0)
-        load(jnp.minimum(2 * j + 2, PAIR - 1), 0)
-        transform(2 * j + 1, 1)
+    for i in range(PAIR):
+        if i + 1 < PAIR:
+            load(i + 1, (i + 1) % 2)
+        transform(i, i % 2)
 
 
 def fourier(pieces):
@@ -207,38 +204,43 @@
     )(pieces, jnp.asarray(inner), jnp.asarray(twiddle), jnp.asarray(outer))
 
 
-def finish_kernel(*refs):
-    ours, theirs = refs[:N_BAND], refs[N_BAND:2 * N_BAND]
-    out_hbm, buffer, sems = refs[2 * N_BAND:]
+def finish_kernel(shifts, *refs):
+    count = len(shifts)
+    ours, theirs = refs[:count], refs[count:2 * count]
+    out_hbm, buffer, sems = refs[-3:]
     band = lax.axis_index("band")
     copies = []
-    for shift in range(N_BAND):
+    for k, shift in enumerate(shifts):
         first = lax.rem(band + N_BAND - shift, N_BAND) * ROWS
         for i in range(LEVELS):
             for r in range(ROWS):
-                piece = ours[shift][0, i, r].astype(f32) + theirs[shift][i, r].astype(f32)
+                piece = ours[k][0, i, r].astype(f32) + theirs[k][i, r].astype(f32)
                 for t in range(4):
-                    buffer[shift, i, r, :, t * BLOCK:(t + 1) * BLOCK] = piece[2 * t:2 * t + 2]
-        copies.append(pltpu.make_async_copy(buffer.at[shift], out_hbm.at[:, pl.ds(first, ROWS)], sems.at[shift]))
+                    buffer[k, i, r, :, t * BLOCK:(t + 1) * BLOCK] = piece[2 * t:2 * t + 2]
+        copies.append(pltpu.make_async_copy(buffer.at[k], out_hbm.at[:, pl.ds(first, ROWS)], sems.at[k]))
         copies[-1].start()
     for copy in copies:
         copy.wait()
 
 
-def finish(ours, theirs):
+def finish(shifts, ours, theirs, before=None):
     vmem = pl.BlockSpec(memory_space=pltpu.VMEM)
+    hbm = pl.BlockSpec(memory_space=pltpu.HBM)
+    count = len(shifts)
+    rest = [] if before is None else [before]
     return pl.pallas_call(
-        finish_kernel,
+        functools.partial(finish_kernel, shifts),
         out_shape=jax.ShapeDtypeStruct((LEVELS, N_BAND * ROWS, 2, WAVES // N_BAND), f32),
-        in_specs=[vmem] * (2 * N_BAND),
-        out_specs=pl.BlockSpec(memory_space=pltpu.HBM),
+        in_specs=[vmem] * (2 * count) + [hbm] * len(rest),
+        out_specs=hbm,
         scratch_shapes=[
-            pltpu.VMEM((N_BAND, LEVELS, ROWS, 2, WAVES // N_BAND), f32),
-            pltpu.SemaphoreType.DMA((N_BAND,)),
+            pltpu.VMEM((count, LEVELS, ROWS, 2, WAVES // N_BAND), f32),
+            pltpu.SemaphoreType.DMA((count,)),
         ],
+        input_output_aliases={2 * count: 0} if rest else {},
         compiler_params=pltpu.CompilerParams(vmem_limit_bytes=VMEM_BYTES),
         name="finish",
-    )(*ours, *theirs)
+    )(*[ours[shift] for shift in shifts], *[theirs[shift] for shift in shifts], *rest)
 
 
 def along_z(piece, shift):
@@ -259,7 +261,7 @@
     spectra = fourier(half_rows)
     ours = [along_z(spectra[shift], shift) for shift in range(N_BAND)]
     theirs = [lax.ppermute(piece[1], "core", [(0, 1), (1, 0)]) for piece in ours]
-    return finish(ours, theirs)
+    return finish((3,), ours, theirs, finish((0, 1, 2), ours, theirs))
 
 
 def solution(mesh):

time: 54.6 us -> 53 us (0.971)
  the two profiles are of different devices: /device:TPU:33 before, /device:TPU:65 now
where the time goes in v7:
time: 53 us
  blocking collectives  21.7 us (41%)
  starting transfers between devices  13.3 us (25%)
  waiting for transfers between devices  11.4 us (22%)
  Pallas kernels  6.4 us (12%)
    all_to_all x1, blocking collectives, shards(): lax.all_to_all(updated.reshape(HALF, PAIR, ROWS, BLOCK), ('y', 'x', 'core...  21.7 us
    ppermute x4, starting transfers between devices, along_z(): return lax.ppermute(piece, ('band', 'zhi', 'core'), pairs)  12.7 us
    ppermute x4, waiting for transfers between devices, along_z(): return lax.ppermute(piece, ('band', 'zhi', 'core'), pairs)  11 us
    pallas_call x1, Pallas kernels, relax(): pl.pallas_call(relax_kernel, out_shape=jax.ShapeDtypeStruct((PAIRS, 2, PA...  3 us
    pallas_call x1, Pallas kernels, fourier(): pl.pallas_call(fourier_kernel, out_shape=jax.ShapeDtypeStruct((N_BAND, 2,...  1.83 us
    pallas_call x2, Pallas kernels, finish(): pl.pallas_call(functools.partial(finish_kernel, shifts), out_shape=jax.Sh...  1.57 us
  transfers between devices with their start and end apart: 8, of which 4 were waited for; matrix products, arithmetic and copies ran while one was open for 0% of the time, Pallas kernels for 2%

profile of v7, /device:TPU:65, one launch (start us, length us, event | category | flops | bytes accessed | tf_op | source)
XLA Modules:
  0.0 53.0 jit_solution(9673959070689441571)
XLA Ops:
  0.0 3.0 %relax.1 = bf16[16,2,10,8,128]{4,3,2,1,0:T(8,128)(2,1)} custom-call(s32[1,8]{1,0:T(1,128)} %cost_hbm.1, s32[8]{0:T(128)} %length_hbm.1, bf16[4,80,8,128]{3,2,1,0:T(8,128)(2,1)} %fields_hbm.1, bf16[4,80,80]{2,1,0:T(8,128)(2,1)} %inverse_hbm.1), custom_call_target="tpu_custom_call" | custom-call | tf_op jit(solution)/shard_map/relax/pallas_call | solution.py:126
  3.0 0.0 copy-start
  3.0 0.0 copy-start.1
  3.0 0.0 copy-start.2
  3.0 21.7 %all_to_all.5.x_ref = bf16[32,10,8,128]{3,2,1,0:T(8,128)(2,1)S(1)} all-to-all(bf16[32,10,8,128]{3,2,1,0:T(8,128)(2,1)} %bitcast.17), channel_id=1, replica_groups=mesh['band'=4,'zhi'=2,'y'=4,'x'=4,'core'=2] {'y','x','core'}, dimensions={0} | all-to-all | bytes 1310720 | tf_op jit(solution)/shard_map/all_to_all | solution.py:258
  24.8 0.0 copy-done
  24.8 0.0 copy-done.1
  24.8 0.0 copy-done.2
  24.8 1.8 %fourier.1 = bf16[4,2,5,8,8,128]{5,4,3,2,1,0:T(8,128)(2,1)S(1)} custom-call(bf16[32,10,8,128]{3,2,1,0:T(8,128)(2,1)S(1)} %all_to_all.5.x_ref, bf16[2,128,64]{2,1,0:T(8,128)(2,1)S(1)} %copy-done.2, f32[2,64,128]{2,1,0:T(8,128)S(1)} %copy-done.1, bf16[2,128,128]{2,1,0:T(8,128)(2,1)S(1)} %copy-done), custom_call_target="tpu_custom_call" | custom-call | tf_op jit(solution)/shard_map/fourier/pallas_call | solution.py:196
  26.6 0.1 slice_bitcast_fusion
  26.7 5.0 %collective-permute-start.4 = (bf16[2,5,8,8,128]{4,3,2,1,0:T(8,128)(2,1)S(1)}, bf16[2,5,8,8,128]{4,3,2,1,0:T(8,128)(2,1)S(1)}, u32[]{:S(2)}, u32[]{:S(2)}) collective-permute-start(bf16[2,5,8,8,128]{4,3,2,1,0:T(8,128)(2,1)S(1)} %get-tuple-element.5), channel_id=1, source_target_pairs={{0,128},{1,160},{32,129},{33,161},{64,192},{65,224},{96,193},{97,2... | collective-permute-start | bytes 491528 | tf_op jit(solution)/shard_map/ppermute | solution.py:253
  31.7 0.6 %collective-permute-start.3 = (bf16[2,5,8,8,128]{4,3,2,1,0:T(8,128)(2,1)S(1)}, bf16[2,5,8,8,128]{4,3,2,1,0:T(8,128)(2,1)S(1)}, u32[]{:S(2)}, u32[]{:S(2)}) collective-permute-start(bf16[2,5,8,8,128]{4,3,2,1,0:T(8,128)(2,1)S(1)} %get-tuple-element.6), channel_id=1, source_target_pairs={{0,64},{1,96},{32,65},{33,97},{64,128},{65,160},{96,129},{97,161},... | collective-permute-start | bytes 491528 | tf_op jit(solution)/shard_map/ppermute | solution.py:253
  32.2 6.5 %collective-permute-start.2 = (bf16[2,5,8,8,128]{4,3,2,1,0:T(8,128)(2,1)S(1)}, bf16[2,5,8,8,128]{4,3,2,1,0:T(8,128)(2,1)S(1)}, u32[]{:S(2)}, u32[]{:S(2)}) collective-permute-start(bf16[2,5,8,8,128]{4,3,2,1,0:T(8,128)(2,1)S(1)} %get-tuple-element.7), channel_id=1, source_target_pairs={{0,0},{1,32},{32,1},{33,33},{64,64},{65,96},{96,65},{97,97},{128,1... | collective-permute-start | bytes 491528 | tf_op jit(solution)/shard_map/ppermute | solution.py:253
  38.8 0.6 %collective-permute-start = (bf16[2,5,8,8,128]{4,3,2,1,0:T(8,128)(2,1)S(1)}, bf16[2,5,8,8,128]{4,3,2,1,0:T(8,128)(2,1)S(1)}, u32[]{:S(2)}, u32[]{:S(2)}) collective-permute-start(bf16[2,5,8,8,128]{4,3,2,1,0:T(8,128)(2,1)S(1)} %get-tuple-element.8), channel_id=1, source_target_pairs={{0,192},{1,224},{32,193},{33,225},{64,0},{65,32},{96,1},{97,33},{1... | collective-permute-start | bytes 491528 | tf_op jit(solution)/shard_map/ppermute | solution.py:253
  39.4 0.0 collective-permute-done.4.refs_2_
  39.4 0.1 collective-permute-start.7
  39.5 6.3 %collective-permute-done.3.refs_1_ = bf16[2,5,8,8,128]{4,3,2,1,0:T(8,128)(2,1)S(1)} collective-permute-done((bf16[2,5,8,8,128]{4,3,2,1,0:T(8,128)(2,1)S(1)}, bf16[2,5,8,8,128]{4,3,2,1,0:T(8,128)(2,1)S(1)}, u32[]{:S(2)}, u32[]{:S(2)}) %collective-permute-start.3) | collective-permute-done | bytes 163872 | tf_op jit(solution)/shard_map/ppermute | solution.py:253
  45.8 0.0 collective-permute-start.6
  45.8 0.1 collective-permute-done.2.refs_0_
  45.9 0.5 collective-permute-start.5
  46.4 4.6 %collective-permute-done.refs_0_ = bf16[2,5,8,8,128]{4,3,2,1,0:T(8,128)(2,1)S(1)} collective-permute-done((bf16[2,5,8,8,128]{4,3,2,1,0:T(8,128)(2,1)S(1)}, bf16[2,5,8,8,128]{4,3,2,1,0:T(8,128)(2,1)S(1)}, u32[]{:S(2)}, u32[]{:S(2)}) %collective-permute-start) | collective-permute-done | bytes 163872 | tf_op jit(solution)/shard_map/ppermute | solution.py:253
  51.0 0.0 collective-permute-start.1
  51.0 0.0 collective-permute-done.7.refs_5_
  51.0 0.0 collective-permute-done.6.refs_4_
  51.0 0.0 collective-permute-done.5.refs_3_
  51.0 0.8 %finish.2.refs_2_ = f32[5,32,2,512]{3,2,1,0:T(2,128)} custom-call(bf16[2,5,8,8,128]{4,3,2,1,0:T(8,128)(2,1)S(1)} %collective-permute-done.2.refs_0_, bf16[2,5,8,8,128]{4,3,2,1,0:T(8,128)(2,1)S(1)} %collective-permute-done.3.refs_1_, bf16[2,5,8,8,128]{4,3,2,1,0:T(8,128)(2,1)S(1)} %collective-permute-done.4.refs_2_, ...), custom_call_target="tpu_custom_call" | custom-call | tf_op jit(solution)/shard_map/finish/pallas_call | solution.py:231
  51.9 0.4 collective-permute-done.1.refs_1_
  52.3 0.7 %finish.3 = f32[5,32,2,512]{3,2,1,0:T(2,128)} custom-call(bf16[2,5,8,8,128]{4,3,2,1,0:T(8,128)(2,1)S(1)} %collective-permute-done.refs_0_, bf16[5,8,8,128]{3,2,1,0:T(8,128)(2,1)S(1)} %collective-permute-done.1.refs_1_, f32[5,32,2,512]{3,2,1,0:T(2,128)} %finish.2.refs_2_), custom_call_target="tpu_custom_call", output_to_operand_aliasing={{}: (2, {})} | custom-call | tf_op jit(solution)/shard_map/finish/pallas_call | solution.py:231
  (4 shorter events, 0.0 us)
Async XLA Ops:
  3.0 21.7 %copy-start = (bf16[2,128,128]{2,1,0:T(8,128)(2,1)S(1)}, bf16[2,128,128]{2,1,0:T(8,128)(2,1)}, u32[]{:S(2)}) copy-start(bf16[2,128,128]{2,1,0:T(8,128)(2,1)} %constant.8.clone.outer_ref) | copy-start | bytes 196612
  3.0 21.7 %copy-start.1 = (f32[2,64,128]{2,1,0:T(8,128)S(1)}, f32[2,64,128]{2,1,0:T(8,128)}, u32[]{:S(2)}) copy-start(f32[2,64,128]{2,1,0:T(8,128)} %constant.7.clone.twiddle_ref) | copy-start | bytes 196612
  3.0 21.7 %copy-start.2 = (bf16[2,128,64]{2,1,0:T(8,128)(2,1)S(1)}, bf16[2,128,64]{2,1,0:T(8,128)(2,1)}, u32[]{:S(2)}) copy-start(bf16[2,128,64]{2,1,0:T(8,128)(2,1)} %constant.6.clone.inner_ref) | copy-start | bytes 98308
  26.7 12.7 %collective-permute-start.4 = (bf16[2,5,8,8,128]{4,3,2,1,0:T(8,128)(2,1)S(1)}, bf16[2,5,8,8,128]{4,3,2,1,0:T(8,128)(2,1)S(1)}, u32[]{:S(2)}, u32[]{:S(2)}) collective-permute-start(bf16[2,5,8,8,128]{4,3,2,1,0:T(8,128)(2,1)S(1)} %get-tuple-element.5), channel_id=1, source_target_pairs={{0,128},{1,160},{32,129},{33,161},{64,192},{65,224},{96,193},{97,2... | collective-permute-start | bytes 491528 | tf_op jit(solution)/shard_map/ppermute | solution.py:253
  31.7 14.1 %collective-permute-start.3 = (bf16[2,5,8,8,128]{4,3,2,1,0:T(8,128)(2,1)S(1)}, bf16[2,5,8,8,128]{4,3,2,1,0:T(8,128)(2,1)S(1)}, u32[]{:S(2)}, u32[]{:S(2)}) collective-permute-start(bf16[2,5,8,8,128]{4,3,2,1,0:T(8,128)(2,1)S(1)} %get-tuple-element.6), channel_id=1, source_target_pairs={{0,64},{1,96},{32,65},{33,97},{64,128},{65,160},{96,129},{97,161},... | collective-permute-start | bytes 491528 | tf_op jit(solution)/shard_map/ppermute | solution.py:253
  32.2 13.7 %collective-permute-start.2 = (bf16[2,5,8,8,128]{4,3,2,1,0:T(8,128)(2,1)S(1)}, bf16[2,5,8,8,128]{4,3,2,1,0:T(8,128)(2,1)S(1)}, u32[]{:S(2)}, u32[]{:S(2)}) collective-permute-start(bf16[2,5,8,8,128]{4,3,2,1,0:T(8,128)(2,1)S(1)} %get-tuple-element.7), channel_id=1, source_target_pairs={{0,0},{1,32},{32,1},{33,33},{64,64},{65,96},{96,65},{97,97},{128,1... | collective-permute-start | bytes 491528 | tf_op jit(solution)/shard_map/ppermute | solution.py:253
  38.8 12.2 %collective-permute-start = (bf16[2,5,8,8,128]{4,3,2,1,0:T(8,128)(2,1)S(1)}, bf16[2,5,8,8,128]{4,3,2,1,0:T(8,128)(2,1)S(1)}, u32[]{:S(2)}, u32[]{:S(2)}) collective-permute-start(bf16[2,5,8,8,128]{4,3,2,1,0:T(8,128)(2,1)S(1)} %get-tuple-element.8), channel_id=1, source_target_pairs={{0,192},{1,224},{32,193},{33,225},{64,0},{65,32},{96,1},{97,33},{1... | collective-permute-start | bytes 491528 | tf_op jit(solution)/shard_map/ppermute | solution.py:253
  39.4 11.6 %collective-permute-start.7 = (bf16[5,8,8,128]{3,2,1,0:T(8,128)(2,1)S(1)}, bf16[5,8,8,128]{3,2,1,0:T(8,128)(2,1)S(1)}, u32[]{:S(2)}, u32[]{:S(2)}) collective-permute-start(bf16[5,8,8,128]{3,2,1,0:T(8,128)(2,1)S(1)} %slice_bitcast_fusion.4), channel_id=1, source_target_pairs={{0,1},{1,0},{2,3},{3,2},{4,5},{5,4},{6,7},{7,6},{8,9},{9,8},{10,11... | collective-permute-start | bytes 245768 | tf_op jit(solution)/shard_map/ppermute | solution.py:263
  45.8 5.2 %collective-permute-start.6 = (bf16[5,8,8,128]{3,2,1,0:T(8,128)(2,1)S(1)}, bf16[5,8,8,128]{3,2,1,0:T(8,128)(2,1)S(1)}, u32[]{:S(2)}, u32[]{:S(2)}) collective-permute-start(bf16[5,8,8,128]{3,2,1,0:T(8,128)(2,1)S(1)} %slice_bitcast_fusion.5), channel_id=1, source_target_pairs={{0,1},{1,0},{2,3},{3,2},{4,5},{5,4},{6,7},{7,6},{8,9},{9,8},{10,11... | collective-permute-start | bytes 245768 | tf_op jit(solution)/shard_map/ppermute | solution.py:263
  45.9 5.1 %collective-permute-start.5 = (bf16[5,8,8,128]{3,2,1,0:T(8,128)(2,1)S(1)}, bf16[5,8,8,128]{3,2,1,0:T(8,128)(2,1)S(1)}, u32[]{:S(2)}, u32[]{:S(2)}) collective-permute-start(bf16[5,8,8,128]{3,2,1,0:T(8,128)(2,1)S(1)} %slice_bitcast_fusion.6), channel_id=1, source_target_pairs={{0,1},{1,0},{2,3},{3,2},{4,5},{5,4},{6,7},{7,6},{8,9},{9,8},{10,11... | collective-permute-start | bytes 245768 | tf_op jit(solution)/shard_map/ppermute | solution.py:263
  51.0 1.3 %collective-permute-start.1 = (bf16[5,8,8,128]{3,2,1,0:T(8,128)(2,1)S(1)}, bf16[5,8,8,128]{3,2,1,0:T(8,128)(2,1)S(1)}, u32[]{:S(2)}, u32[]{:S(2)}) collective-permute-start(bf16[5,8,8,128]{3,2,1,0:T(8,128)(2,1)S(1)} %slice_bitcast_fusion.7), channel_id=1, source_target_pairs={{0,1},{1,0},{2,3},{3,2},{4,5},{5,4},{6,7},{7,6},{8,9},{9,8},{10,11... | collective-permute-start | bytes 245768 | tf_op jit(solution)/shard_map/ppermute | solution.py:263

commit v8 on v7

--- a/solution.py
+++ b/solution.py
@@ -38,7 +38,7 @@
 
 def tables():
     q = np.arange(N_COL)
-    s = np.arange(HALF)
+    s = np.arange(HALF).reshape(PAIRS, 2).T.reshape(-1)
     angle = 2.0 * np.pi / N_COL * ((q[:, None] * s[None, :]) % N_COL)
     inner = np.concatenate([np.cos(angle), -np.sin(angle)], axis=0)
     sign = np.where(np.arange(2 * N_COL) % 2 == 0, 1.0, -1.0)
@@ -116,7 +116,7 @@
         piece = flat[f * LEV * ROWS:(f + 1) * LEV * ROWS, :].reshape(LEV // PAIR, PAIR, ROWS, BLOCK)
         out_ref[f] = piece.astype(bf16)
         first = f % 2 * (LEV // PAIR)
-        sends.append(pltpu.make_async_copy(out_ref.at[f], out_hbm.at[pl.ds(first, LEV // PAIR), f // 2], out_sems.at[f]))
+        sends.append(pltpu.make_async_copy(out_ref.at[f], out_hbm.at[f // 2, pl.ds(first, LEV // PAIR)], out_sems.at[f]))
         sends[-1].start()
     for send in sends:
         send.wait()
@@ -125,7 +125,7 @@
 def relax(fields, inverse, costs, lengths):
     return pl.pallas_call(
         relax_kernel,
-        out_shape=jax.ShapeDtypeStruct((PAIRS, 2, PAIR, ROWS, BLOCK), bf16),
+        out_shape=jax.ShapeDtypeStruct((2, PAIRS, PAIR, ROWS, BLOCK), bf16),
         in_specs=[pl.BlockSpec(memory_space=pltpu.HBM)] * 4,
         out_specs=pl.BlockSpec(memory_space=pltpu.HBM),
         scratch_shapes=[
@@ -256,7 +256,7 @@
 def shards(fields, inverse, block_costs, row_length):
     updated = relax(fields, inverse, block_costs, row_length)
     half_rows = lax.all_to_all(
-        updated.reshape(HALF, PAIR, ROWS, BLOCK), ("y", "x", "core"), split_axis=0, concat_axis=0, tiled=True
+        updated.reshape(HALF, PAIR, ROWS, BLOCK), ("core", "y", "x"), split_axis=0, concat_axis=0, tiled=True
     )
     spectra = fourier(half_rows)
     ours = [along_z(spectra[shift], shift) for shift in range(N_BAND)]

time: 53 us -> 52 us (0.981)
  the two profiles are of different devices: /device:TPU:65 before, /device:TPU:1 now
where the time goes in v8:
time: 52 us; the launch traced here: 51.7 us
  blocking collectives  21.6 us (42%)
  starting transfers between devices  15.6 us (30%)
  waiting for transfers between devices  7.8 us (15%)
  Pallas kernels  6.4 us (12%)
    all_to_all x1, blocking collectives, shards(): lax.all_to_all(updated.reshape(HALF, PAIR, ROWS, BLOCK), ('core', 'y', 'x...  21.6 us
    ppermute x4, starting transfers between devices, along_z(): return lax.ppermute(piece, ('band', 'zhi', 'core'), pairs)  14.9 us
    ppermute x4, waiting for transfers between devices, along_z(): return lax.ppermute(piece, ('band', 'zhi', 'core'), pairs)  7.41 us
    pallas_call x1, Pallas kernels, relax(): pl.pallas_call(relax_kernel, out_shape=jax.ShapeDtypeStruct((2, PAIRS, PA...  3 us
    pallas_call x1, Pallas kernels, fourier(): pl.pallas_call(fourier_kernel, out_shape=jax.ShapeDtypeStruct((N_BAND, 2,...  1.83 us
    pallas_call x2, Pallas kernels, finish(): pl.pallas_call(functools.partial(finish_kernel, shifts), out_shape=jax.Sh...  1.57 us
  transfers between devices with their start and end apart: 8, of which 3 were waited for; matrix products, arithmetic and copies ran while one was open for 0% of the time, Pallas kernels for 2%

profile of v8, /device:TPU:1, one launch (start us, length us, event | category | flops | bytes accessed | tf_op | source)
XLA Modules:
  0.0 51.7 jit_solution(12015815798402938518)
XLA Ops:
  0.0 3.0 %relax.1 = bf16[2,16,10,8,128]{4,3,2,1,0:T(8,128)(2,1)} custom-call(s32[1,8]{1,0:T(1,128)} %cost_hbm.1, s32[8]{0:T(128)} %length_hbm.1, bf16[4,80,8,128]{3,2,1,0:T(8,128)(2,1)} %fields_hbm.1, bf16[4,80,80]{2,1,0:T(8,128)(2,1)} %inverse_hbm.1), custom_call_target="tpu_custom_call" | custom-call | tf_op jit(solution)/shard_map/relax/pallas_call | solution.py:126
  3.0 0.0 copy-start
  3.0 0.0 copy-start.1
  3.0 0.0 copy-start.2
  3.0 21.6 %all_to_all.5.x_ref = bf16[32,10,8,128]{3,2,1,0:T(8,128)(2,1)S(1)} all-to-all(bf16[32,10,8,128]{3,2,1,0:T(8,128)(2,1)} %bitcast.17), channel_id=1, replica_groups=mesh['band'=4,'zhi'=2,'y'=4,'x'=4,'core'=2] {'core','y','x'}, dimensions={0} | all-to-all | bytes 1310720 | tf_op jit(solution)/shard_map/all_to_all | solution.py:258
  24.7 0.0 copy-done
  24.7 0.0 copy-done.1
  24.7 0.0 copy-done.2
  24.7 1.8 %fourier.1 = bf16[4,2,5,8,8,128]{5,4,3,2,1,0:T(8,128)(2,1)S(1)} custom-call(bf16[32,10,8,128]{3,2,1,0:T(8,128)(2,1)S(1)} %all_to_all.5.x_ref, bf16[2,128,64]{2,1,0:T(8,128)(2,1)S(1)} %copy-done.2, f32[2,64,128]{2,1,0:T(8,128)S(1)} %copy-done.1, bf16[2,128,128]{2,1,0:T(8,128)(2,1)S(1)} %copy-done), custom_call_target="tpu_custom_call" | custom-call | tf_op jit(solution)/shard_map/fourier/pallas_call | solution.py:196
  26.5 0.1 slice_bitcast_fusion
  26.6 7.7 %collective-permute-start.4 = (bf16[2,5,8,8,128]{4,3,2,1,0:T(8,128)(2,1)S(1)}, bf16[2,5,8,8,128]{4,3,2,1,0:T(8,128)(2,1)S(1)}, u32[]{:S(2)}, u32[]{:S(2)}) collective-permute-start(bf16[2,5,8,8,128]{4,3,2,1,0:T(8,128)(2,1)S(1)} %get-tuple-element.5), channel_id=1, source_target_pairs={{0,128},{1,160},{32,129},{33,161},{64,192},{65,224},{96,193},{97,2... | collective-permute-start | bytes 491528 | tf_op jit(solution)/shard_map/ppermute | solution.py:253
  34.3 0.6 %collective-permute-start.3 = (bf16[2,5,8,8,128]{4,3,2,1,0:T(8,128)(2,1)S(1)}, bf16[2,5,8,8,128]{4,3,2,1,0:T(8,128)(2,1)S(1)}, u32[]{:S(2)}, u32[]{:S(2)}) collective-permute-start(bf16[2,5,8,8,128]{4,3,2,1,0:T(8,128)(2,1)S(1)} %get-tuple-element.6), channel_id=1, source_target_pairs={{0,64},{1,96},{32,65},{33,97},{64,128},{65,160},{96,129},{97,161},... | collective-permute-start | bytes 491528 | tf_op jit(solution)/shard_map/ppermute | solution.py:253
  34.9 6.5 %collective-permute-start.2 = (bf16[2,5,8,8,128]{4,3,2,1,0:T(8,128)(2,1)S(1)}, bf16[2,5,8,8,128]{4,3,2,1,0:T(8,128)(2,1)S(1)}, u32[]{:S(2)}, u32[]{:S(2)}) collective-permute-start(bf16[2,5,8,8,128]{4,3,2,1,0:T(8,128)(2,1)S(1)} %get-tuple-element.7), channel_id=1, source_target_pairs={{0,0},{1,32},{32,1},{33,33},{64,64},{65,96},{96,65},{97,97},{128,1... | collective-permute-start | bytes 491528 | tf_op jit(solution)/shard_map/ppermute | solution.py:253
  41.4 0.1 collective-permute-start
  41.5 0.0 collective-permute-done.4.refs_2_
  41.6 0.1 collective-permute-start.7
  41.7 0.0 collective-permute-done.3.refs_1_
  41.7 0.6 %collective-permute-start.6 = (bf16[5,8,8,128]{3,2,1,0:T(8,128)(2,1)S(1)}, bf16[5,8,8,128]{3,2,1,0:T(8,128)(2,1)S(1)}, u32[]{:S(2)}, u32[]{:S(2)}) collective-permute-start(bf16[5,8,8,128]{3,2,1,0:T(8,128)(2,1)S(1)} %slice_bitcast_fusion.5), channel_id=1, source_target_pairs={{0,1},{1,0},{2,3},{3,2},{4,5},{5,4},{6,7},{7,6},{8,9},{9,8},{10,11... | collective-permute-start | bytes 245768 | tf_op jit(solution)/shard_map/ppermute | solution.py:263
  42.2 3.2 %collective-permute-done.2.refs_0_ = bf16[2,5,8,8,128]{4,3,2,1,0:T(8,128)(2,1)S(1)} collective-permute-done((bf16[2,5,8,8,128]{4,3,2,1,0:T(8,128)(2,1)S(1)}, bf16[2,5,8,8,128]{4,3,2,1,0:T(8,128)(2,1)S(1)}, u32[]{:S(2)}, u32[]{:S(2)}) %collective-permute-start.2) | collective-permute-done | bytes 163872 | tf_op jit(solution)/shard_map/ppermute | solution.py:253
  45.4 0.0 collective-permute-start.5
  45.4 4.2 %collective-permute-done.refs_0_ = bf16[2,5,8,8,128]{4,3,2,1,0:T(8,128)(2,1)S(1)} collective-permute-done((bf16[2,5,8,8,128]{4,3,2,1,0:T(8,128)(2,1)S(1)}, bf16[2,5,8,8,128]{4,3,2,1,0:T(8,128)(2,1)S(1)}, u32[]{:S(2)}, u32[]{:S(2)}) %collective-permute-start) | collective-permute-done | bytes 163872 | tf_op jit(solution)/shard_map/ppermute | solution.py:253
  49.7 0.0 collective-permute-start.1
  49.7 0.0 collective-permute-done.7.refs_5_
  49.7 0.0 collective-permute-done.6.refs_4_
  49.7 0.0 collective-permute-done.5.refs_3_
  49.7 0.8 %finish.2.refs_2_ = f32[5,32,2,512]{3,2,1,0:T(2,128)} custom-call(bf16[2,5,8,8,128]{4,3,2,1,0:T(8,128)(2,1)S(1)} %collective-permute-done.2.refs_0_, bf16[2,5,8,8,128]{4,3,2,1,0:T(8,128)(2,1)S(1)} %collective-permute-done.3.refs_1_, bf16[2,5,8,8,128]{4,3,2,1,0:T(8,128)(2,1)S(1)} %collective-permute-done.4.refs_2_, ...), custom_call_target="tpu_custom_call" | custom-call | tf_op jit(solution)/shard_map/finish/pallas_call | solution.py:231
  50.6 0.4 collective-permute-done.1.refs_1_
  51.0 0.7 %finish.3 = f32[5,32,2,512]{3,2,1,0:T(2,128)} custom-call(bf16[2,5,8,8,128]{4,3,2,1,0:T(8,128)(2,1)S(1)} %collective-permute-done.refs_0_, bf16[5,8,8,128]{3,2,1,0:T(8,128)(2,1)S(1)} %collective-permute-done.1.refs_1_, f32[5,32,2,512]{3,2,1,0:T(2,128)} %finish.2.refs_2_), custom_call_target="tpu_custom_call", output_to_operand_aliasing={{}: (2, {})} | custom-call | tf_op jit(solution)/shard_map/finish/pallas_call | solution.py:231
  (4 shorter events, 0.0 us)
Async XLA Ops:
  3.0 21.7 %copy-start = (bf16[2,128,128]{2,1,0:T(8,128)(2,1)S(1)}, bf16[2,128,128]{2,1,0:T(8,128)(2,1)}, u32[]{:S(2)}) copy-start(bf16[2,128,128]{2,1,0:T(8,128)(2,1)} %constant.8.clone.outer_ref) | copy-start | bytes 196612
  3.0 21.6 %copy-start.1 = (f32[2,64,128]{2,1,0:T(8,128)S(1)}, f32[2,64,128]{2,1,0:T(8,128)}, u32[]{:S(2)}) copy-start(f32[2,64,128]{2,1,0:T(8,128)} %constant.7.clone.twiddle_ref) | copy-start | bytes 196612
  3.0 21.6 %copy-start.2 = (bf16[2,128,64]{2,1,0:T(8,128)(2,1)S(1)}, bf16[2,128,64]{2,1,0:T(8,128)(2,1)}, u32[]{:S(2)}) copy-start(bf16[2,128,64]{2,1,0:T(8,128)(2,1)} %constant.6.clone.inner_ref) | copy-start | bytes 98308
  26.6 14.9 %collective-permute-start.4 = (bf16[2,5,8,8,128]{4,3,2,1,0:T(8,128)(2,1)S(1)}, bf16[2,5,8,8,128]{4,3,2,1,0:T(8,128)(2,1)S(1)}, u32[]{:S(2)}, u32[]{:S(2)}) collective-permute-start(bf16[2,5,8,8,128]{4,3,2,1,0:T(8,128)(2,1)S(1)} %get-tuple-element.5), channel_id=1, source_target_pairs={{0,128},{1,160},{32,129},{33,161},{64,192},{65,224},{96,193},{97,2... | collective-permute-start | bytes 491528 | tf_op jit(solution)/shard_map/ppermute | solution.py:253
  34.3 7.3 %collective-permute-start.3 = (bf16[2,5,8,8,128]{4,3,2,1,0:T(8,128)(2,1)S(1)}, bf16[2,5,8,8,128]{4,3,2,1,0:T(8,128)(2,1)S(1)}, u32[]{:S(2)}, u32[]{:S(2)}) collective-permute-start(bf16[2,5,8,8,128]{4,3,2,1,0:T(8,128)(2,1)S(1)} %get-tuple-element.6), channel_id=1, source_target_pairs={{0,64},{1,96},{32,65},{33,97},{64,128},{65,160},{96,129},{97,161},... | collective-permute-start | bytes 491528 | tf_op jit(solution)/shard_map/ppermute | solution.py:253
  34.9 10.5 %collective-permute-start.2 = (bf16[2,5,8,8,128]{4,3,2,1,0:T(8,128)(2,1)S(1)}, bf16[2,5,8,8,128]{4,3,2,1,0:T(8,128)(2,1)S(1)}, u32[]{:S(2)}, u32[]{:S(2)}) collective-permute-start(bf16[2,5,8,8,128]{4,3,2,1,0:T(8,128)(2,1)S(1)} %get-tuple-element.7), channel_id=1, source_target_pairs={{0,0},{1,32},{32,1},{33,33},{64,64},{65,96},{96,65},{97,97},{128,1... | collective-permute-start | bytes 491528 | tf_op jit(solution)/shard_map/ppermute | solution.py:253
  41.4 8.2 %collective-permute-start = (bf16[2,5,8,8,128]{4,3,2,1,0:T(8,128)(2,1)S(1)}, bf16[2,5,8,8,128]{4,3,2,1,0:T(8,128)(2,1)S(1)}, u32[]{:S(2)}, u32[]{:S(2)}) collective-permute-start(bf16[2,5,8,8,128]{4,3,2,1,0:T(8,128)(2,1)S(1)} %get-tuple-element.8), channel_id=1, source_target_pairs={{0,192},{1,224},{32,193},{33,225},{64,0},{65,32},{96,1},{97,33},{1... | collective-permute-start | bytes 491528 | tf_op jit(solution)/shard_map/ppermute | solution.py:253
  41.6 8.1 %collective-permute-start.7 = (bf16[5,8,8,128]{3,2,1,0:T(8,128)(2,1)S(1)}, bf16[5,8,8,128]{3,2,1,0:T(8,128)(2,1)S(1)}, u32[]{:S(2)}, u32[]{:S(2)}) collective-permute-start(bf16[5,8,8,128]{3,2,1,0:T(8,128)(2,1)S(1)} %slice_bitcast_fusion.4), channel_id=1, source_target_pairs={{0,1},{1,0},{2,3},{3,2},{4,5},{5,4},{6,7},{7,6},{8,9},{9,8},{10,11... | collective-permute-start | bytes 245768 | tf_op jit(solution)/shard_map/ppermute | solution.py:263
  41.7 8.0 %collective-permute-start.6 = (bf16[5,8,8,128]{3,2,1,0:T(8,128)(2,1)S(1)}, bf16[5,8,8,128]{3,2,1,0:T(8,128)(2,1)S(1)}, u32[]{:S(2)}, u32[]{:S(2)}) collective-permute-start(bf16[5,8,8,128]{3,2,1,0:T(8,128)(2,1)S(1)} %slice_bitcast_fusion.5), channel_id=1, source_target_pairs={{0,1},{1,0},{2,3},{3,2},{4,5},{5,4},{6,7},{7,6},{8,9},{9,8},{10,11... | collective-permute-start | bytes 245768 | tf_op jit(solution)/shard_map/ppermute | solution.py:263
  45.4 4.3 %collective-permute-start.5 = (bf16[5,8,8,128]{3,2,1,0:T(8,128)(2,1)S(1)}, bf16[5,8,8,128]{3,2,1,0:T(8,128)(2,1)S(1)}, u32[]{:S(2)}, u32[]{:S(2)}) collective-permute-start(bf16[5,8,8,128]{3,2,1,0:T(8,128)(2,1)S(1)} %slice_bitcast_fusion.6), channel_id=1, source_target_pairs={{0,1},{1,0},{2,3},{3,2},{4,5},{5,4},{6,7},{7,6},{8,9},{9,8},{10,11... | collective-permute-start | bytes 245768 | tf_op jit(solution)/shard_map/ppermute | solution.py:263
  49.7 1.3 %collective-permute-start.1 = (bf16[5,8,8,128]{3,2,1,0:T(8,128)(2,1)S(1)}, bf16[5,8,8,128]{3,2,1,0:T(8,128)(2,1)S(1)}, u32[]{:S(2)}, u32[]{:S(2)}) collective-permute-start(bf16[5,8,8,128]{3,2,1,0:T(8,128)(2,1)S(1)} %slice_bitcast_fusion.7), channel_id=1, source_target_pairs={{0,1},{1,0},{2,3},{3,2},{4,5},{5,4},{6,7},{7,6},{8,9},{9,8},{10,11... | collective-permute-start | bytes 245768 | tf_op jit(solution)/shard_map/ppermute | solution.py:263

commit v9 on v7

--- a/solution.py
+++ b/solution.py
@@ -68,7 +68,7 @@
         pltpu.make_async_copy(cost_hbm, cost_ref, sems.at[FIELDS + 1]),
         pltpu.make_async_copy(length_hbm, length_ref, sems.at[FIELDS + 2]),
     ]
-    for copy in copies + small:
+    for copy in small + copies:
         copy.start()
     first = lax.axis_index(COL_AXES) * BLOCK
     for f in range(FIELDS):

time: 53 us -> 52.4 us (0.989)
  starting transfers between devices: 13.3 us -> 12 us
    ppermute x4, starting transfers between devices: 12.7 us -> 11.3 us  [along_z(): return lax.ppermute(piece, ('band', 'zhi', 'core'), pairs)]
  transfers between devices with their start and end apart: 8 -> 8, of which waited for: 4 -> 3; matrix products, arithmetic and copies ran while one was open for 0% -> 0% of each run, Pallas kernels for 2% -> 2%
where the time goes in v9:
time: 52.4 us; the launch traced here: 51.9 us
  blocking collectives  22 us (42%)
  starting transfers between devices  12 us (23%)
  waiting for transfers between devices  11.3 us (22%)
  Pallas kernels  6.43 us (12%)
    all_to_all x1, blocking collectives, shards(): lax.all_to_all(updated.reshape(HALF, PAIR, ROWS, BLOCK), ('y', 'x', 'core...  22 us
    ppermute x4, starting transfers between devices, along_z(): return lax.ppermute(piece, ('band', 'zhi', 'core'), pairs)  11.3 us
    ppermute x4, waiting for transfers between devices, along_z(): return lax.ppermute(piece, ('band', 'zhi', 'core'), pairs)  10.9 us
    pallas_call x1, Pallas kernels, relax(): pl.pallas_call(relax_kernel, out_shape=jax.ShapeDtypeStruct((PAIRS, 2, PA...  3.03 us
    pallas_call x1, Pallas kernels, fourier(): pl.pallas_call(fourier_kernel, out_shape=jax.ShapeDtypeStruct((N_BAND, 2,...  1.83 us
    pallas_call x2, Pallas kernels, finish(): pl.pallas_call(functools.partial(finish_kernel, shifts), out_shape=jax.Sh...  1.57 us
  transfers between devices with their start and end apart: 8, of which 3 were waited for; matrix products, arithmetic and copies ran while one was open for 0% of the time, Pallas kernels for 2%

profile of v9, /device:TPU:65, one launch (start us, length us, event | category | flops | bytes accessed | tf_op | source)
XLA Modules:
  0.0 51.9 jit_solution(13305032842086163944)
XLA Ops:
  0.0 3.0 %relax.1 = bf16[16,2,10,8,128]{4,3,2,1,0:T(8,128)(2,1)} custom-call(s32[1,8]{1,0:T(1,128)} %cost_hbm.1, s32[8]{0:T(128)} %length_hbm.1, bf16[4,80,8,128]{3,2,1,0:T(8,128)(2,1)} %fields_hbm.1, bf16[4,80,80]{2,1,0:T(8,128)(2,1)} %inverse_hbm.1), custom_call_target="tpu_custom_call" | custom-call | tf_op jit(solution)/shard_map/relax/pallas_call | solution.py:126
  3.0 0.0 copy-start
  3.0 0.0 copy-start.1
  3.1 0.0 copy-start.2
  3.1 22.0 %all_to_all.5.x_ref = bf16[32,10,8,128]{3,2,1,0:T(8,128)(2,1)S(1)} all-to-all(bf16[32,10,8,128]{3,2,1,0:T(8,128)(2,1)} %bitcast.17), channel_id=1, replica_groups=mesh['band'=4,'zhi'=2,'y'=4,'x'=4,'core'=2] {'y','x','core'}, dimensions={0} | all-to-all | bytes 1310720 | tf_op jit(solution)/shard_map/all_to_all | solution.py:258
  25.1 0.0 copy-done
  25.1 0.0 copy-done.1
  25.1 0.0 copy-done.2
  25.1 1.8 %fourier.1 = bf16[4,2,5,8,8,128]{5,4,3,2,1,0:T(8,128)(2,1)S(1)} custom-call(bf16[32,10,8,128]{3,2,1,0:T(8,128)(2,1)S(1)} %all_to_all.5.x_ref, bf16[2,128,64]{2,1,0:T(8,128)(2,1)S(1)} %copy-done.2, f32[2,64,128]{2,1,0:T(8,128)S(1)} %copy-done.1, bf16[2,128,128]{2,1,0:T(8,128)(2,1)S(1)} %copy-done), custom_call_target="tpu_custom_call" | custom-call | tf_op jit(solution)/shard_map/fourier/pallas_call | solution.py:196
  26.9 0.1 slice_bitcast_fusion
  27.0 3.5 %collective-permute-start.4 = (bf16[2,5,8,8,128]{4,3,2,1,0:T(8,128)(2,1)S(1)}, bf16[2,5,8,8,128]{4,3,2,1,0:T(8,128)(2,1)S(1)}, u32[]{:S(2)}, u32[]{:S(2)}) collective-permute-start(bf16[2,5,8,8,128]{4,3,2,1,0:T(8,128)(2,1)S(1)} %get-tuple-element.5), channel_id=1, source_target_pairs={{0,128},{1,160},{32,129},{33,161},{64,192},{65,224},{96,193},{97,2... | collective-permute-start | bytes 491528 | tf_op jit(solution)/shard_map/ppermute | solution.py:253
  30.5 0.6 %collective-permute-start.3 = (bf16[2,5,8,8,128]{4,3,2,1,0:T(8,128)(2,1)S(1)}, bf16[2,5,8,8,128]{4,3,2,1,0:T(8,128)(2,1)S(1)}, u32[]{:S(2)}, u32[]{:S(2)}) collective-permute-start(bf16[2,5,8,8,128]{4,3,2,1,0:T(8,128)(2,1)S(1)} %get-tuple-element.6), channel_id=1, source_target_pairs={{0,64},{1,96},{32,65},{33,97},{64,128},{65,160},{96,129},{97,161},... | collective-permute-start | bytes 491528 | tf_op jit(solution)/shard_map/ppermute | solution.py:253
  31.1 6.6 %collective-permute-start.2 = (bf16[2,5,8,8,128]{4,3,2,1,0:T(8,128)(2,1)S(1)}, bf16[2,5,8,8,128]{4,3,2,1,0:T(8,128)(2,1)S(1)}, u32[]{:S(2)}, u32[]{:S(2)}) collective-permute-start(bf16[2,5,8,8,128]{4,3,2,1,0:T(8,128)(2,1)S(1)} %get-tuple-element.7), channel_id=1, source_target_pairs={{0,0},{1,32},{32,1},{33,33},{64,64},{65,96},{96,65},{97,97},{128,1... | collective-permute-start | bytes 491528 | tf_op jit(solution)/shard_map/ppermute | solution.py:253
  37.6 0.7 %collective-permute-start = (bf16[2,5,8,8,128]{4,3,2,1,0:T(8,128)(2,1)S(1)}, bf16[2,5,8,8,128]{4,3,2,1,0:T(8,128)(2,1)S(1)}, u32[]{:S(2)}, u32[]{:S(2)}) collective-permute-start(bf16[2,5,8,8,128]{4,3,2,1,0:T(8,128)(2,1)S(1)} %get-tuple-element.8), channel_id=1, source_target_pairs={{0,192},{1,224},{32,193},{33,225},{64,0},{65,32},{96,1},{97,33},{1... | collective-permute-start | bytes 491528 | tf_op jit(solution)/shard_map/ppermute | solution.py:253
  38.3 0.0 collective-permute-done.4.refs_2_
  38.3 0.1 collective-permute-start.7
  38.4 7.1 %collective-permute-done.3.refs_1_ = bf16[2,5,8,8,128]{4,3,2,1,0:T(8,128)(2,1)S(1)} collective-permute-done((bf16[2,5,8,8,128]{4,3,2,1,0:T(8,128)(2,1)S(1)}, bf16[2,5,8,8,128]{4,3,2,1,0:T(8,128)(2,1)S(1)}, u32[]{:S(2)}, u32[]{:S(2)}) %collective-permute-start.3) | collective-permute-done | bytes 163872 | tf_op jit(solution)/shard_map/ppermute | solution.py:253
  45.5 0.0 collective-permute-start.6
  45.5 0.0 collective-permute-done.2.refs_0_
  45.6 0.6 %collective-permute-start.5 = (bf16[5,8,8,128]{3,2,1,0:T(8,128)(2,1)S(1)}, bf16[5,8,8,128]{3,2,1,0:T(8,128)(2,1)S(1)}, u32[]{:S(2)}, u32[]{:S(2)}) collective-permute-start(bf16[5,8,8,128]{3,2,1,0:T(8,128)(2,1)S(1)} %slice_bitcast_fusion.6), channel_id=1, source_target_pairs={{0,1},{1,0},{2,3},{3,2},{4,5},{5,4},{6,7},{7,6},{8,9},{9,8},{10,11... | collective-permute-start | bytes 245768 | tf_op jit(solution)/shard_map/ppermute | solution.py:263
  46.1 3.8 %collective-permute-done.refs_0_ = bf16[2,5,8,8,128]{4,3,2,1,0:T(8,128)(2,1)S(1)} collective-permute-done((bf16[2,5,8,8,128]{4,3,2,1,0:T(8,128)(2,1)S(1)}, bf16[2,5,8,8,128]{4,3,2,1,0:T(8,128)(2,1)S(1)}, u32[]{:S(2)}, u32[]{:S(2)}) %collective-permute-start) | collective-permute-done | bytes 163872 | tf_op jit(solution)/shard_map/ppermute | solution.py:253
  49.9 0.0 collective-permute-start.1
  49.9 0.0 collective-permute-done.7.refs_5_
  49.9 0.0 collective-permute-done.6.refs_4_
  49.9 0.0 collective-permute-done.5.refs_3_
  50.0 0.8 %finish.2.refs_2_ = f32[5,32,2,512]{3,2,1,0:T(2,128)} custom-call(bf16[2,5,8,8,128]{4,3,2,1,0:T(8,128)(2,1)S(1)} %collective-permute-done.2.refs_0_, bf16[2,5,8,8,128]{4,3,2,1,0:T(8,128)(2,1)S(1)} %collective-permute-done.3.refs_1_, bf16[2,5,8,8,128]{4,3,2,1,0:T(8,128)(2,1)S(1)} %collective-permute-done.4.refs_2_, ...), custom_call_target="tpu_custom_call" | custom-call | tf_op jit(solution)/shard_map/finish/pallas_call | solution.py:231
  50.8 0.4 collective-permute-done.1.refs_1_
  51.2 0.7 %finish.3 = f32[5,32,2,512]{3,2,1,0:T(2,128)} custom-call(bf16[2,5,8,8,128]{4,3,2,1,0:T(8,128)(2,1)S(1)} %collective-permute-done.refs_0_, bf16[5,8,8,128]{3,2,1,0:T(8,128)(2,1)S(1)} %collective-permute-done.1.refs_1_, f32[5,32,2,512]{3,2,1,0:T(2,128)} %finish.2.refs_2_), custom_call_target="tpu_custom_call", output_to_operand_aliasing={{}: (2, {})} | custom-call | tf_op jit(solution)/shard_map/finish/pallas_call | solution.py:231
  (4 shorter events, 0.0 us)
Async XLA Ops:
  3.0 22.0 %copy-start = (bf16[2,128,128]{2,1,0:T(8,128)(2,1)S(1)}, bf16[2,128,128]{2,1,0:T(8,128)(2,1)}, u32[]{:S(2)}) copy-start(bf16[2,128,128]{2,1,0:T(8,128)(2,1)} %constant.8.clone.outer_ref) | copy-start | bytes 196612
  3.0 22.0 %copy-start.1 = (f32[2,64,128]{2,1,0:T(8,128)S(1)}, f32[2,64,128]{2,1,0:T(8,128)}, u32[]{:S(2)}) copy-start(f32[2,64,128]{2,1,0:T(8,128)} %constant.7.clone.twiddle_ref) | copy-start | bytes 196612
  3.1 22.0 %copy-start.2 = (bf16[2,128,64]{2,1,0:T(8,128)(2,1)S(1)}, bf16[2,128,64]{2,1,0:T(8,128)(2,1)}, u32[]{:S(2)}) copy-start(bf16[2,128,64]{2,1,0:T(8,128)(2,1)} %constant.6.clone.inner_ref) | copy-start | bytes 98308
  27.0 11.3 %collective-permute-start.4 = (bf16[2,5,8,8,128]{4,3,2,1,0:T(8,128)(2,1)S(1)}, bf16[2,5,8,8,128]{4,3,2,1,0:T(8,128)(2,1)S(1)}, u32[]{:S(2)}, u32[]{:S(2)}) collective-permute-start(bf16[2,5,8,8,128]{4,3,2,1,0:T(8,128)(2,1)S(1)} %get-tuple-element.5), channel_id=1, source_target_pairs={{0,128},{1,160},{32,129},{33,161},{64,192},{65,224},{96,193},{97,2... | collective-permute-start | bytes 491528 | tf_op jit(solution)/shard_map/ppermute | solution.py:253
  30.5 15.0 %collective-permute-start.3 = (bf16[2,5,8,8,128]{4,3,2,1,0:T(8,128)(2,1)S(1)}, bf16[2,5,8,8,128]{4,3,2,1,0:T(8,128)(2,1)S(1)}, u32[]{:S(2)}, u32[]{:S(2)}) collective-permute-start(bf16[2,5,8,8,128]{4,3,2,1,0:T(8,128)(2,1)S(1)} %get-tuple-element.6), channel_id=1, source_target_pairs={{0,64},{1,96},{32,65},{33,97},{64,128},{65,160},{96,129},{97,161},... | collective-permute-start | bytes 491528 | tf_op jit(solution)/shard_map/ppermute | solution.py:253
  31.1 14.5 %collective-permute-start.2 = (bf16[2,5,8,8,128]{4,3,2,1,0:T(8,128)(2,1)S(1)}, bf16[2,5,8,8,128]{4,3,2,1,0:T(8,128)(2,1)S(1)}, u32[]{:S(2)}, u32[]{:S(2)}) collective-permute-start(bf16[2,5,8,8,128]{4,3,2,1,0:T(8,128)(2,1)S(1)} %get-tuple-element.7), channel_id=1, source_target_pairs={{0,0},{1,32},{32,1},{33,33},{64,64},{65,96},{96,65},{97,97},{128,1... | collective-permute-start | bytes 491528 | tf_op jit(solution)/shard_map/ppermute | solution.py:253
  37.6 12.3 %collective-permute-start = (bf16[2,5,8,8,128]{4,3,2,1,0:T(8,128)(2,1)S(1)}, bf16[2,5,8,8,128]{4,3,2,1,0:T(8,128)(2,1)S(1)}, u32[]{:S(2)}, u32[]{:S(2)}) collective-permute-start(bf16[2,5,8,8,128]{4,3,2,1,0:T(8,128)(2,1)S(1)} %get-tuple-element.8), channel_id=1, source_target_pairs={{0,192},{1,224},{32,193},{33,225},{64,0},{65,32},{96,1},{97,33},{1... | collective-permute-start | bytes 491528 | tf_op jit(solution)/shard_map/ppermute | solution.py:253
  38.3 11.6 %collective-permute-start.7 = (bf16[5,8,8,128]{3,2,1,0:T(8,128)(2,1)S(1)}, bf16[5,8,8,128]{3,2,1,0:T(8,128)(2,1)S(1)}, u32[]{:S(2)}, u32[]{:S(2)}) collective-permute-start(bf16[5,8,8,128]{3,2,1,0:T(8,128)(2,1)S(1)} %slice_bitcast_fusion.4), channel_id=1, source_target_pairs={{0,1},{1,0},{2,3},{3,2},{4,5},{5,4},{6,7},{7,6},{8,9},{9,8},{10,11... | collective-permute-start | bytes 245768 | tf_op jit(solution)/shard_map/ppermute | solution.py:263
  45.5 4.4 %collective-permute-start.6 = (bf16[5,8,8,128]{3,2,1,0:T(8,128)(2,1)S(1)}, bf16[5,8,8,128]{3,2,1,0:T(8,128)(2,1)S(1)}, u32[]{:S(2)}, u32[]{:S(2)}) collective-permute-start(bf16[5,8,8,128]{3,2,1,0:T(8,128)(2,1)S(1)} %slice_bitcast_fusion.5), channel_id=1, source_target_pairs={{0,1},{1,0},{2,3},{3,2},{4,5},{5,4},{6,7},{7,6},{8,9},{9,8},{10,11... | collective-permute-start | bytes 245768 | tf_op jit(solution)/shard_map/ppermute | solution.py:263
  45.6 4.4 %collective-permute-start.5 = (bf16[5,8,8,128]{3,2,1,0:T(8,128)(2,1)S(1)}, bf16[5,8,8,128]{3,2,1,0:T(8,128)(2,1)S(1)}, u32[]{:S(2)}, u32[]{:S(2)}) collective-permute-start(bf16[5,8,8,128]{3,2,1,0:T(8,128)(2,1)S(1)} %slice_bitcast_fusion.6), channel_id=1, source_target_pairs={{0,1},{1,0},{2,3},{3,2},{4,5},{5,4},{6,7},{7,6},{8,9},{9,8},{10,11... | collective-permute-start | bytes 245768 | tf_op jit(solution)/shard_map/ppermute | solution.py:263
  49.9 1.3 %collective-permute-start.1 = (bf16[5,8,8,128]{3,2,1,0:T(8,128)(2,1)S(1)}, bf16[5,8,8,128]{3,2,1,0:T(8,128)(2,1)S(1)}, u32[]{:S(2)}, u32[]{:S(2)}) collective-permute-start(bf16[5,8,8,128]{3,2,1,0:T(8,128)(2,1)S(1)} %slice_bitcast_fusion.7), channel_id=1, source_target_pairs={{0,1},{1,0},{2,3},{3,2},{4,5},{5,4},{6,7},{7,6},{8,9},{9,8},{10,11... | collective-permute-start | bytes 245768 | tf_op jit(solution)/shard_map/ppermute | solution.py:263

commit v10 on v7

--- a/solution.py
+++ b/solution.py
@@ -161,9 +161,9 @@
     def transform(i, buffer):
         core, level = divmod(i, LEVELS)
         slot = lax.rem(core + half, 2)
-        for r in range(0, ROWS, 4):
+        for r in range(0, ROWS, 2):
             twisted = []
-            for e in range(r, r + 4, 2):
+            for e in range(r, r + 2, 2):
                 pair = [flat[buffer, pl.ds(e + d, HALF, stride=ROWS), :] for d in range(2)]
                 x = jnp.concatenate(pair, axis=1).astype(bf16)
                 y = jnp.dot(inner, jnp.concatenate([x, x], axis=0), preferred_element_type=f32)
@@ -175,7 +175,7 @@
             z = jnp.concatenate(twisted, axis=0)
             w = lax.dot_general(outer, z, (((1,), (1,)), ((), ())), preferred_element_type=f32)
             w = w[:2 * waves] + w[2 * waves:]
-            for k in range(4 // 2):
+            for k in range(1):
                 even = w[:waves, k * BLOCK:(k + 1) * BLOCK]
                 odd = w[waves:, k * BLOCK:(k + 1) * BLOCK]
                 rows = (jnp.where(left, even, pltpu.roll(odd, N_COL, 1)), jnp.where(left, pltpu.roll(even, N_COL, 1), odd))

time: 53 us -> 52.6 us (level); the launches traced: 53 us -> 51.8 us
  starting transfers between devices: 13.3 us -> 11.8 us
    ppermute x4, starting transfers between devices: 12.7 us -> 11.1 us  [along_z(): return lax.ppermute(piece, ('band', 'zhi', 'core'), pairs)]
  transfers between devices with their start and end apart: 8 -> 8, of which waited for: 4 -> 3; matrix products, arithmetic and copies ran while one was open for 0% -> 0% of each run, Pallas kernels for 2% -> 2%
where the time goes in v10:
time: 52.6 us; the launch traced here: 51.8 us
  blocking collectives  22.1 us (42%)
  starting transfers between devices  11.8 us (22%)
  waiting for transfers between devices  11.3 us (21%)
  Pallas kernels  6.33 us (12%)
    all_to_all x1, blocking collectives, shards(): lax.all_to_all(updated.reshape(HALF, PAIR, ROWS, BLOCK), ('y', 'x', 'core...  22.1 us
    ppermute x4, starting transfers between devices, along_z(): return lax.ppermute(piece, ('band', 'zhi', 'core'), pairs)  11.1 us
    ppermute x4, waiting for transfers between devices, along_z(): return lax.ppermute(piece, ('band', 'zhi', 'core'), pairs)  10.9 us
    pallas_call x1, Pallas kernels, relax(): pl.pallas_call(relax_kernel, out_shape=jax.ShapeDtypeStruct((PAIRS, 2, PA...  3 us
    pallas_call x1, Pallas kernels, fourier(): pl.pallas_call(fourier_kernel, out_shape=jax.ShapeDtypeStruct((N_BAND, 2,...  1.76 us
    pallas_call x2, Pallas kernels, finish(): pl.pallas_call(functools.partial(finish_kernel, shifts), out_shape=jax.Sh...  1.57 us
  transfers between devices with their start and end apart: 8, of which 3 were waited for; matrix products, arithmetic and copies ran while one was open for 0% of the time, Pallas kernels for 2%

profile of v10, /device:TPU:65, one launch (start us, length us, event | category | flops | bytes accessed | tf_op | source)
XLA Modules:
  0.0 51.8 jit_solution(2101715650045869825)
XLA Ops:
  0.0 3.0 %relax.1 = bf16[16,2,10,8,128]{4,3,2,1,0:T(8,128)(2,1)} custom-call(s32[1,8]{1,0:T(1,128)} %cost_hbm.1, s32[8]{0:T(128)} %length_hbm.1, bf16[4,80,8,128]{3,2,1,0:T(8,128)(2,1)} %fields_hbm.1, bf16[4,80,80]{2,1,0:T(8,128)(2,1)} %inverse_hbm.1), custom_call_target="tpu_custom_call" | custom-call | tf_op jit(solution)/shard_map/relax/pallas_call | solution.py:126
  3.0 0.0 copy-start
  3.0 0.0 copy-start.1
  3.0 0.0 copy-start.2
  3.0 22.1 %all_to_all.5.x_ref = bf16[32,10,8,128]{3,2,1,0:T(8,128)(2,1)S(1)} all-to-all(bf16[32,10,8,128]{3,2,1,0:T(8,128)(2,1)} %bitcast.17), channel_id=1, replica_groups=mesh['band'=4,'zhi'=2,'y'=4,'x'=4,'core'=2] {'y','x','core'}, dimensions={0} | all-to-all | bytes 1310720 | tf_op jit(solution)/shard_map/all_to_all | solution.py:258
  25.2 0.0 copy-done
  25.2 0.0 copy-done.1
  25.2 0.0 copy-done.2
  25.2 1.8 %fourier.1 = bf16[4,2,5,8,8,128]{5,4,3,2,1,0:T(8,128)(2,1)S(1)} custom-call(bf16[32,10,8,128]{3,2,1,0:T(8,128)(2,1)S(1)} %all_to_all.5.x_ref, bf16[2,128,64]{2,1,0:T(8,128)(2,1)S(1)} %copy-done.2, f32[2,64,128]{2,1,0:T(8,128)S(1)} %copy-done.1, bf16[2,128,128]{2,1,0:T(8,128)(2,1)S(1)} %copy-done), custom_call_target="tpu_custom_call" | custom-call | tf_op jit(solution)/shard_map/fourier/pallas_call | solution.py:196
  27.0 0.1 slice_bitcast_fusion
  27.0 3.4 %collective-permute-start.4 = (bf16[2,5,8,8,128]{4,3,2,1,0:T(8,128)(2,1)S(1)}, bf16[2,5,8,8,128]{4,3,2,1,0:T(8,128)(2,1)S(1)}, u32[]{:S(2)}, u32[]{:S(2)}) collective-permute-start(bf16[2,5,8,8,128]{4,3,2,1,0:T(8,128)(2,1)S(1)} %get-tuple-element.5), channel_id=1, source_target_pairs={{0,128},{1,160},{32,129},{33,161},{64,192},{65,224},{96,193},{97,2... | collective-permute-start | bytes 491528 | tf_op jit(solution)/shard_map/ppermute | solution.py:253
  30.4 0.6 %collective-permute-start.3 = (bf16[2,5,8,8,128]{4,3,2,1,0:T(8,128)(2,1)S(1)}, bf16[2,5,8,8,128]{4,3,2,1,0:T(8,128)(2,1)S(1)}, u32[]{:S(2)}, u32[]{:S(2)}) collective-permute-start(bf16[2,5,8,8,128]{4,3,2,1,0:T(8,128)(2,1)S(1)} %get-tuple-element.6), channel_id=1, source_target_pairs={{0,64},{1,96},{32,65},{33,97},{64,128},{65,160},{96,129},{97,161},... | collective-permute-start | bytes 491528 | tf_op jit(solution)/shard_map/ppermute | solution.py:253
  31.0 6.5 %collective-permute-start.2 = (bf16[2,5,8,8,128]{4,3,2,1,0:T(8,128)(2,1)S(1)}, bf16[2,5,8,8,128]{4,3,2,1,0:T(8,128)(2,1)S(1)}, u32[]{:S(2)}, u32[]{:S(2)}) collective-permute-start(bf16[2,5,8,8,128]{4,3,2,1,0:T(8,128)(2,1)S(1)} %get-tuple-element.7), channel_id=1, source_target_pairs={{0,0},{1,32},{32,1},{33,33},{64,64},{65,96},{96,65},{97,97},{128,1... | collective-permute-start | bytes 491528 | tf_op jit(solution)/shard_map/ppermute | solution.py:253
  37.5 0.6 %collective-permute-start = (bf16[2,5,8,8,128]{4,3,2,1,0:T(8,128)(2,1)S(1)}, bf16[2,5,8,8,128]{4,3,2,1,0:T(8,128)(2,1)S(1)}, u32[]{:S(2)}, u32[]{:S(2)}) collective-permute-start(bf16[2,5,8,8,128]{4,3,2,1,0:T(8,128)(2,1)S(1)} %get-tuple-element.8), channel_id=1, source_target_pairs={{0,192},{1,224},{32,193},{33,225},{64,0},{65,32},{96,1},{97,33},{1... | collective-permute-start | bytes 491528 | tf_op jit(solution)/shard_map/ppermute | solution.py:253
  38.1 0.0 collective-permute-done.4.refs_2_
  38.1 0.1 collective-permute-start.7
  38.2 7.2 %collective-permute-done.3.refs_1_ = bf16[2,5,8,8,128]{4,3,2,1,0:T(8,128)(2,1)S(1)} collective-permute-done((bf16[2,5,8,8,128]{4,3,2,1,0:T(8,128)(2,1)S(1)}, bf16[2,5,8,8,128]{4,3,2,1,0:T(8,128)(2,1)S(1)}, u32[]{:S(2)}, u32[]{:S(2)}) %collective-permute-start.3) | collective-permute-done | bytes 163872 | tf_op jit(solution)/shard_map/ppermute | solution.py:253
  45.4 0.0 collective-permute-start.6
  45.4 0.0 collective-permute-done.2.refs_0_
  45.5 0.6 %collective-permute-start.5 = (bf16[5,8,8,128]{3,2,1,0:T(8,128)(2,1)S(1)}, bf16[5,8,8,128]{3,2,1,0:T(8,128)(2,1)S(1)}, u32[]{:S(2)}, u32[]{:S(2)}) collective-permute-start(bf16[5,8,8,128]{3,2,1,0:T(8,128)(2,1)S(1)} %slice_bitcast_fusion.6), channel_id=1, source_target_pairs={{0,1},{1,0},{2,3},{3,2},{4,5},{5,4},{6,7},{7,6},{8,9},{9,8},{10,11... | collective-permute-start | bytes 245768 | tf_op jit(solution)/shard_map/ppermute | solution.py:263
  46.0 3.7 %collective-permute-done.refs_0_ = bf16[2,5,8,8,128]{4,3,2,1,0:T(8,128)(2,1)S(1)} collective-permute-done((bf16[2,5,8,8,128]{4,3,2,1,0:T(8,128)(2,1)S(1)}, bf16[2,5,8,8,128]{4,3,2,1,0:T(8,128)(2,1)S(1)}, u32[]{:S(2)}, u32[]{:S(2)}) %collective-permute-start) | collective-permute-done | bytes 163872 | tf_op jit(solution)/shard_map/ppermute | solution.py:253
  49.8 0.0 collective-permute-start.1
  49.8 0.0 collective-permute-done.7.refs_5_
  49.8 0.0 collective-permute-done.6.refs_4_
  49.8 0.0 collective-permute-done.5.refs_3_
  49.8 0.8 %finish.2.refs_2_ = f32[5,32,2,512]{3,2,1,0:T(2,128)} custom-call(bf16[2,5,8,8,128]{4,3,2,1,0:T(8,128)(2,1)S(1)} %collective-permute-done.2.refs_0_, bf16[2,5,8,8,128]{4,3,2,1,0:T(8,128)(2,1)S(1)} %collective-permute-done.3.refs_1_, bf16[2,5,8,8,128]{4,3,2,1,0:T(8,128)(2,1)S(1)} %collective-permute-done.4.refs_2_, ...), custom_call_target="tpu_custom_call" | custom-call | tf_op jit(solution)/shard_map/finish/pallas_call | solution.py:231
  50.7 0.4 collective-permute-done.1.refs_1_
  51.0 0.7 %finish.3 = f32[5,32,2,512]{3,2,1,0:T(2,128)} custom-call(bf16[2,5,8,8,128]{4,3,2,1,0:T(8,128)(2,1)S(1)} %collective-permute-done.refs_0_, bf16[5,8,8,128]{3,2,1,0:T(8,128)(2,1)S(1)} %collective-permute-done.1.refs_1_, f32[5,32,2,512]{3,2,1,0:T(2,128)} %finish.2.refs_2_), custom_call_target="tpu_custom_call", output_to_operand_aliasing={{}: (2, {})} | custom-call | tf_op jit(solution)/shard_map/finish/pallas_call | solution.py:231
  (4 shorter events, 0.0 us)
Async XLA Ops:
  3.0 22.2 %copy-start = (bf16[2,128,128]{2,1,0:T(8,128)(2,1)S(1)}, bf16[2,128,128]{2,1,0:T(8,128)(2,1)}, u32[]{:S(2)}) copy-start(bf16[2,128,128]{2,1,0:T(8,128)(2,1)} %constant.8.clone.outer_ref) | copy-start | bytes 196612
  3.0 22.2 %copy-start.1 = (f32[2,64,128]{2,1,0:T(8,128)S(1)}, f32[2,64,128]{2,1,0:T(8,128)}, u32[]{:S(2)}) copy-start(f32[2,64,128]{2,1,0:T(8,128)} %constant.7.clone.twiddle_ref) | copy-start | bytes 196612
  3.0 22.2 %copy-start.2 = (bf16[2,128,64]{2,1,0:T(8,128)(2,1)S(1)}, bf16[2,128,64]{2,1,0:T(8,128)(2,1)}, u32[]{:S(2)}) copy-start(bf16[2,128,64]{2,1,0:T(8,128)(2,1)} %constant.6.clone.inner_ref) | copy-start | bytes 98308
  27.0 11.1 %collective-permute-start.4 = (bf16[2,5,8,8,128]{4,3,2,1,0:T(8,128)(2,1)S(1)}, bf16[2,5,8,8,128]{4,3,2,1,0:T(8,128)(2,1)S(1)}, u32[]{:S(2)}, u32[]{:S(2)}) collective-permute-start(bf16[2,5,8,8,128]{4,3,2,1,0:T(8,128)(2,1)S(1)} %get-tuple-element.5), channel_id=1, source_target_pairs={{0,128},{1,160},{32,129},{33,161},{64,192},{65,224},{96,193},{97,2... | collective-permute-start | bytes 491528 | tf_op jit(solution)/shard_map/ppermute | solution.py:253
  30.4 15.0 %collective-permute-start.3 = (bf16[2,5,8,8,128]{4,3,2,1,0:T(8,128)(2,1)S(1)}, bf16[2,5,8,8,128]{4,3,2,1,0:T(8,128)(2,1)S(1)}, u32[]{:S(2)}, u32[]{:S(2)}) collective-permute-start(bf16[2,5,8,8,128]{4,3,2,1,0:T(8,128)(2,1)S(1)} %get-tuple-element.6), channel_id=1, source_target_pairs={{0,64},{1,96},{32,65},{33,97},{64,128},{65,160},{96,129},{97,161},... | collective-permute-start | bytes 491528 | tf_op jit(solution)/shard_map/ppermute | solution.py:253
  31.0 14.4 %collective-permute-start.2 = (bf16[2,5,8,8,128]{4,3,2,1,0:T(8,128)(2,1)S(1)}, bf16[2,5,8,8,128]{4,3,2,1,0:T(8,128)(2,1)S(1)}, u32[]{:S(2)}, u32[]{:S(2)}) collective-permute-start(bf16[2,5,8,8,128]{4,3,2,1,0:T(8,128)(2,1)S(1)} %get-tuple-element.7), channel_id=1, source_target_pairs={{0,0},{1,32},{32,1},{33,33},{64,64},{65,96},{96,65},{97,97},{128,1... | collective-permute-start | bytes 491528 | tf_op jit(solution)/shard_map/ppermute | solution.py:253
  37.5 12.2 %collective-permute-start = (bf16[2,5,8,8,128]{4,3,2,1,0:T(8,128)(2,1)S(1)}, bf16[2,5,8,8,128]{4,3,2,1,0:T(8,128)(2,1)S(1)}, u32[]{:S(2)}, u32[]{:S(2)}) collective-permute-start(bf16[2,5,8,8,128]{4,3,2,1,0:T(8,128)(2,1)S(1)} %get-tuple-element.8), channel_id=1, source_target_pairs={{0,192},{1,224},{32,193},{33,225},{64,0},{65,32},{96,1},{97,33},{1... | collective-permute-start | bytes 491528 | tf_op jit(solution)/shard_map/ppermute | solution.py:253
  38.1 11.6 %collective-permute-start.7 = (bf16[5,8,8,128]{3,2,1,0:T(8,128)(2,1)S(1)}, bf16[5,8,8,128]{3,2,1,0:T(8,128)(2,1)S(1)}, u32[]{:S(2)}, u32[]{:S(2)}) collective-permute-start(bf16[5,8,8,128]{3,2,1,0:T(8,128)(2,1)S(1)} %slice_bitcast_fusion.4), channel_id=1, source_target_pairs={{0,1},{1,0},{2,3},{3,2},{4,5},{5,4},{6,7},{7,6},{8,9},{9,8},{10,11... | collective-permute-start | bytes 245768 | tf_op jit(solution)/shard_map/ppermute | solution.py:263
  45.4 4.4 %collective-permute-start.6 = (bf16[5,8,8,128]{3,2,1,0:T(8,128)(2,1)S(1)}, bf16[5,8,8,128]{3,2,1,0:T(8,128)(2,1)S(1)}, u32[]{:S(2)}, u32[]{:S(2)}) collective-permute-start(bf16[5,8,8,128]{3,2,1,0:T(8,128)(2,1)S(1)} %slice_bitcast_fusion.5), channel_id=1, source_target_pairs={{0,1},{1,0},{2,3},{3,2},{4,5},{5,4},{6,7},{7,6},{8,9},{9,8},{10,11... | collective-permute-start | bytes 245768 | tf_op jit(solution)/shard_map/ppermute | solution.py:263
  45.5 4.3 %collective-permute-start.5 = (bf16[5,8,8,128]{3,2,1,0:T(8,128)(2,1)S(1)}, bf16[5,8,8,128]{3,2,1,0:T(8,128)(2,1)S(1)}, u32[]{:S(2)}, u32[]{:S(2)}) collective-permute-start(bf16[5,8,8,128]{3,2,1,0:T(8,128)(2,1)S(1)} %slice_bitcast_fusion.6), channel_id=1, source_target_pairs={{0,1},{1,0},{2,3},{3,2},{4,5},{5,4},{6,7},{7,6},{8,9},{9,8},{10,11... | collective-permute-start | bytes 245768 | tf_op jit(solution)/shard_map/ppermute | solution.py:263
  49.8 1.3 %collective-permute-start.1 = (bf16[5,8,8,128]{3,2,1,0:T(8,128)(2,1)S(1)}, bf16[5,8,8,128]{3,2,1,0:T(8,128)(2,1)S(1)}, u32[]{:S(2)}, u32[]{:S(2)}) collective-permute-start(bf16[5,8,8,128]{3,2,1,0:T(8,128)(2,1)S(1)} %slice_bitcast_fusion.7), channel_id=1, source_target_pairs={{0,1},{1,0},{2,3},{3,2},{4,5},{5,4},{6,7},{7,6},{8,9},{9,8},{10,11... | collective-permute-start | bytes 245768 | tf_op jit(solution)/shard_map/ppermute | solution.py:263
